TPU v7x, 128 devices: a whole 4x4x4 slice. The times are simulated.
128 devices in a mesh: ctx: 16 (over x_hi, z, core), mp: 8 (over x_lo, y).
Axes of the slice: x: 4 (x_hi: 2, x_lo: 2; x = x_hi * 2 + x_lo), y: 4, z: 4, core: 2. Of those that a mesh axis runs over, the one named last changes fastest.
Arguments:
- tokens: bfloat16 [2048, 4096], P('ctx'), may hold values from -8 to 8
- out_grad: bfloat16 [2048, 4096], P('ctx'), may hold values from -8 to 8
- in_weight: bfloat16 [4096, 3, 4096], P(None, None, 'mp'), may hold values from -0.09375 to 0.09375
- out_weight: bfloat16 [4096, 4096], P('mp'), may hold values from -0.09375 to 0.09375
- filters: float32 [2048, 4096], P('ctx', 'mp'), may hold values from -0.125 to 0.125
Outputs:
- input_grad: bfloat16 [2048, 4096], P('ctx', 'mp')
- in_weight_grad: float32 [4096, 3, 4096], P('ctx', None, 'mp')
- out_weight_grad: float32 [4096, 4096], P('mp', 'ctx')
- filter_grad: float32 [2048, 4096], P('ctx', 'mp')
All inputs are finite; a program needn't handle non-finite values.
Results may differ from a plain program's by a relative error of at most 0.025.
Values may be sent and summed in bfloat16 or wider, within the bound.
No kernel may reach another device: no remote copies, remote signals or barrier semaphores. Data moves between devices by JAX's collectives and lax.ppermute only.
A program may use at most 192 MiB of HBM per device.

v0:
```python
import math

import jax
import jax.numpy as jnp
import ml_dtypes
import numpy as np
from jax import lax
from jax.experimental import pallas as pl
from jax.experimental.pallas import tpu as pltpu
from jax.sharding import PartitionSpec as P

F32 = jnp.float32
BF16 = jnp.bfloat16
NT = (((1,), (1,)), ((), ()))
NN = (((1,), (0,)), ((), ()))
MIB = 1 << 20
BLOCK = 32
SEQ_DEV = 128
SEQ = 2048


def dot(a, b, dims=NN):
    return lax.dot_general(a, b, dims, preferred_element_type=F32)


def call(kernel, *, flops=0, bytes_accessed=0, vmem=32, **kw):
    return pl.pallas_call(
        kernel,
        compiler_params=pltpu.CompilerParams(vmem_limit_bytes=vmem * MIB),
        cost_estimate=pl.CostEstimate(flops=flops, bytes_accessed=bytes_accessed, transcendentals=0),
        **kw,
    )


def split_columns(tokens, out_grad):
    def kernel(t_ref, g_ref, o_ref):
        for p in range(4):
            for h in range(2):
                lanes = pl.ds(p * 256 + h * 128, 128)
                o_ref[p, pl.ds(h * 128, 128), :] = t_ref[:, lanes]
                o_ref[p, pl.ds(256 + h * 128, 128), :] = g_ref[:, lanes]

    spec = pl.BlockSpec((SEQ_DEV, 1024), lambda s: (0, s))
    return call(
        kernel,
        grid=(4,),
        in_specs=[spec, spec],
        out_specs=pl.BlockSpec((4, 512, 128), lambda s: (s, 0, 0)),
        out_shape=jax.ShapeDtypeStruct((16, 512, 128), BF16),
        bytes_accessed=4 * MIB,
        name="split_columns",
    )(tokens, out_grad)


def project(tokens, out_grad, weight, out_weight, filters):
    def kernel(t_ref, g_ref, w_ref, ow_ref, f_ref, o_ref):
        s = pl.program_id(0)

        def put(rows):
            o_ref[...] = rows.astype(BF16).reshape(8, 1, BLOCK, SEQ_DEV)

        @pl.when(s < 6)
        def _():
            put(dot(t_ref[...], w_ref[0]).T)

        @pl.when((s >= 6) & (s < 8))
        def _():
            put(dot(ow_ref[...], g_ref[...], NT))

        @pl.when(s >= 8)
        def _():
            put(f_ref[...].T)

    def w_map(s):
        s = jnp.minimum(s, 5)
        return (s // 2, 0, s % 2)

    return call(
        kernel,
        grid=(10,),
        in_specs=[
            pl.BlockSpec((SEQ_DEV, 4096), lambda s: (0, 0)),
            pl.BlockSpec((SEQ_DEV, 4096), lambda s: (0, 0)),
            pl.BlockSpec((1, 4096, 256), w_map),
            pl.BlockSpec((256, 4096), lambda s: (jnp.clip(s - 6, 0, 1), 0)),
            pl.BlockSpec((SEQ_DEV, 256), lambda s: (0, jnp.clip(s - 8, 0, 1))),
        ],
        out_specs=pl.BlockSpec((8, 1, BLOCK, SEQ_DEV), lambda s: (0, s % 2, s // 2, 0)),
        out_shape=jax.ShapeDtypeStruct((8, 2, 5 * BLOCK, SEQ_DEV), BF16),
        flops=2 * 128 * 4096 * 2048,
        bytes_accessed=19 * MIB,
        name="project",
    )(tokens, out_grad, weight, out_weight, filters)


def cosine_matrix():
    odd = 2 * np.arange(SEQ, dtype=np.int64) + 1
    turns = np.outer(odd, odd) % (8 * SEQ)
    return np.cos(turns * (2.0 * np.pi / (8 * SEQ))).astype(ml_dtypes.bfloat16)


def frequency_rows():
    half = (2 * np.arange(SEQ) + 1) * (np.pi / (4 * SEQ))
    sign = 1.0 - 2.0 * (np.arange(SEQ) % 2)
    rows = np.zeros((8, SEQ), np.float32)
    rows[0], rows[1], rows[2] = np.cos(half), np.sin(half), sign
    return rows


def convolve(received, matrix, rows, flip):
    chunk = 512
    n_chunks = SEQ // chunk

    def kernel(r_ref, m_hbm, w_ref, j_ref, b_ref, o_ref, m_ref, x_ref, y_ref, sem):
        copies = []
        for n in range(n_chunks):
            lanes = pl.ds(n * chunk, chunk)
            copies.append(pltpu.make_async_copy(m_hbm.at[:, lanes], m_ref.at[:, lanes], sem.at[n]))
            copies[-1].start()
        rev = j_ref[...]
        for b in range(16):
            part = r_ref[b]
            key, value = part[32:64].astype(F32), part[64:96].astype(F32)
            query, gate = part[0:32].astype(F32), part[96:128].astype(F32)
            lanes = pl.ds(b * 128, 128)
            x_ref[0:32, lanes] = part[128:160]
            x_ref[32:64, lanes] = (key * value).astype(BF16)
            x_ref[64:96, lanes] = (gate * query).astype(BF16)
        for b in range(8):
            x_ref[96:192, pl.ds((7 - b) * 256, 256)] = dot(x_ref[0:96, pl.ds(b * 256, 256)], rev).astype(BF16)
        for n in range(n_chunks):
            lanes = pl.ds(n * chunk, chunk)
            copies[n].wait()
            spec = dot(x_ref[...], m_ref[:, lanes])
            wr, wi, sign = w_ref[0:1, lanes], w_ref[1:2, lanes], w_ref[2:3, lanes]
            hr, mr, gr = spec[0:32], spec[32:64], spec[64:96]
            neg = -sign
            hi, mi, gi = spec[96:128] * neg, spec[128:160] * neg, spec[160:192] * neg
            hwr, hwi = hr * wr - hi * wi, hr * wi + hi * wr
            mwr, mwi = mr * wr - mi * wi, mr * wi + mi * wr
            y_ref[0:32, lanes] = (hwr * mr - hwi * mi).astype(BF16)
            y_ref[32:64, lanes] = (gr * hwr + gi * hwi).astype(BF16)
            y_ref[64:96, lanes] = (gr * mwr + gi * mwi).astype(BF16)
            imag = jnp.concatenate(
                [hwr * mi + hwi * mr, gi * hwr - gr * hwi, gi * mwr - gr * mwi], axis=0
            ).astype(BF16)
            for b in range(chunk // 256):
                at = SEQ - (n * chunk + (b + 1) * 256)
                y_ref[96:192, pl.ds(at, 256)] = dot(imag[:, b * 256 : (b + 1) * 256], rev).astype(BF16)
        scale = 1.0 / SEQ
        for n in range(n_chunks):
            lanes = pl.ds(n * chunk, chunk)
            back = dot(y_ref[...], m_ref[:, lanes])
            back = (back[0:96] - back[96:192] * w_ref[2:3, lanes]) * scale
            for b in range(chunk // 128):
                at = n * (chunk // 128) + b
                part = r_ref[at]
                cut = slice(b * 128, (b + 1) * 128)
                conv, mixed, raw = back[0:32, cut], back[32:64, cut], back[64:96, cut]
                query, key, value, gate = (part[32 * i : 32 * i + 32].astype(F32) for i in range(4))
                gq = (gate * conv).astype(BF16)
                gk = (mixed * value).astype(BF16)
                gv = (mixed * key).astype(BF16)
                pos = pl.ds(at * 128, 128)
                b_ref[0:32, pos] = gq
                b_ref[32:64, pos] = gk
                b_ref[64:96, pos] = gv
                b_ref[96:128, pos] = (query * conv).astype(BF16)
                o_ref[at, 0:32, :] = gq
                o_ref[at, 32:64, :] = gk
                o_ref[at, 64:96, :] = gv
                o_ref[at, 96:128, :] = (raw * (1.0 / math.sqrt(SEQ))).astype(BF16)

    vm = pl.BlockSpec(memory_space=pltpu.VMEM)
    return call(
        kernel,
        in_specs=[vm, pl.BlockSpec(memory_space=pl.ANY), vm, vm],
        out_specs=[vm, vm],
        out_shape=[
            jax.ShapeDtypeStruct((128, SEQ), BF16),
            jax.ShapeDtypeStruct((16, 128, 128), BF16),
        ],
        scratch_shapes=[
            pltpu.VMEM((SEQ, SEQ), BF16),
            pltpu.VMEM((192, SEQ), BF16),
            pltpu.VMEM((192, SEQ), BF16),
            pltpu.SemaphoreType.DMA((n_chunks,)),
        ],
        flops=4 * 192 * SEQ * SEQ,
        bytes_accessed=12 * MIB,
        name="convolve",
    )(received, matrix, rows, flip)


def input_partial(received, weight):
    def kernel(r_ref, w_ref, o_ref, f_ref, g_ref):
        @pl.when(pl.program_id(0) == 0)
        def _():
            for chip in range(8):
                for core in range(2):
                    at = core * 256 + chip * BLOCK
                    for j in range(3):
                        g_ref[j, at : at + BLOCK, :] = r_ref[2 * chip + core, j * BLOCK : (j + 1) * BLOCK, :]
            raw = [r_ref[2 * chip + core, 96:128, :] for core in range(2) for chip in range(8)]
            f_ref[...] = jnp.concatenate(raw, axis=0).astype(F32).T

        total = dot(w_ref[0], g_ref[0]) + dot(w_ref[1], g_ref[1]) + dot(w_ref[2], g_ref[2])
        o_ref[...] = total.astype(BF16).reshape(1, 512, SEQ_DEV)

    return call(
        kernel,
        grid=(8,),
        in_specs=[
            pl.BlockSpec((16, 128, 128), lambda s: (0, 0, 0)),
            pl.BlockSpec((3, 512, 512), lambda s: (0, s, 0)),
        ],
        out_specs=[
            pl.BlockSpec((1, 512, SEQ_DEV), lambda s: (s, 0, 0)),
            pl.BlockSpec((SEQ_DEV, 512), lambda s: (0, 0)),
        ],
        out_shape=[
            jax.ShapeDtypeStruct((8, 512, SEQ_DEV), BF16),
            jax.ShapeDtypeStruct((SEQ_DEV, 512), F32),
        ],
        scratch_shapes=[pltpu.VMEM((3, 512, SEQ_DEV), BF16)],
        flops=2 * 128 * 4096 * 1536,
        bytes_accessed=14 * MIB,
        name="input_partial",
    )(received, weight)


def sum_partials(parts):
    def kernel(p_ref, o_ref):
        total = p_ref[0].astype(F32)
        for i in range(1, 8):
            total = total + p_ref[i].astype(F32)
        o_ref[...] = total.T.astype(BF16)

    vm = pl.BlockSpec(memory_space=pltpu.VMEM)
    return call(
        kernel,
        in_specs=[vm],
        out_specs=vm,
        out_shape=jax.ShapeDtypeStruct((SEQ_DEV, 512), BF16),
        bytes_accessed=MIB,
        name="sum_partials",
    )(parts)


def turn_columns(received):
    def kernel(r_ref, o_ref):
        for b in range(4):
            for h in range(4):
                block = r_ref[b, h * 128 : (h + 1) * 128, :].astype(F32).T
                o_ref[h * 128 : (h + 1) * 128, b * 128 : (b + 1) * 128] = block.astype(BF16)

    return call(
        kernel,
        grid=(4,),
        in_specs=[pl.BlockSpec((4, 512, 128), lambda s: (s, 0, 0))],
        out_specs=pl.BlockSpec((512, 512), lambda s: (0, s)),
        out_shape=jax.ShapeDtypeStruct((512, SEQ), BF16),
        bytes_accessed=4 * MIB,
        name="turn_columns",
    )(received)


def weight_gradients(place, own_columns, other_columns, blocks):
    n_blocks = len(blocks)
    factor = 1.0 / math.sqrt(SEQ)

    def kernel(place_ref, own_ref, other_ref, *refs):
        block_refs = refs[:n_blocks]
        in_hbm, out_hbm, send_ref, g_ref, res_ref, sem, out_sem = refs[n_blocks:]
        core = place_ref[n_blocks]
        copies = [[], [], [], []]
        for j in range(4):
            for k in range(n_blocks):
                src = block_refs[k].at[pl.ds(j * BLOCK, BLOCK)]
                at = pl.multiple_of(place_ref[k] * BLOCK, BLOCK)
                copies[j].append(pltpu.make_async_copy(src, g_ref.at[j, pl.ds(at, BLOCK)], sem.at[j, k]))
                copies[j][-1].start()
        half = pl.multiple_of(core * 256, 256)
        outs = []
        for j in range(4):
            for copy in copies[j]:
                copy.wait()
            g = g_ref[j]
            if j < 3:
                send_ref[j * 256 : (j + 1) * 256, :] = (dot(other_ref[0:256], g, NT) * factor).astype(BF16)
                res_ref[j] = dot(own_ref[0:256], g, NT) * factor
                dst = in_hbm.at[j, :, pl.ds(half, 256)]
            else:
                send_ref[768:1024, :] = (dot(g, other_ref[256:512], NT) * factor).astype(BF16)
                res_ref[j] = dot(g, own_ref[256:512], NT) * factor
                dst = out_hbm.at[pl.ds(half, 256)]
            outs.append(pltpu.make_async_copy(res_ref.at[j], dst, out_sem.at[j]))
            outs[-1].start()
        for copy in outs:
            copy.wait()

    vm = pl.BlockSpec(memory_space=pltpu.VMEM)
    hbm = pl.BlockSpec(memory_space=pl.ANY)
    return call(
        kernel,
        in_specs=[pl.BlockSpec(memory_space=pltpu.SMEM), vm, vm] + [hbm] * n_blocks,
        out_specs=[hbm, hbm, vm],
        out_shape=[
            jax.ShapeDtypeStruct((3, 256, 512), F32),
            jax.ShapeDtypeStruct((512, 256), F32),
            jax.ShapeDtypeStruct((1024, 256), BF16),
        ],
        scratch_shapes=[
            pltpu.VMEM((4, 256, SEQ), BF16),
            pltpu.VMEM((4, 256, 256), F32),
            pltpu.SemaphoreType.DMA((4, n_blocks)),
            pltpu.SemaphoreType.DMA((4,)),
        ],
        flops=4 * 1024 * 256 * SEQ,
        bytes_accessed=10 * MIB,
        name="weight_gradients",
    )(place, own_columns, other_columns, *blocks)


def fill_halves(place, sent, in_grad, out_grad):
    def kernel(place_ref, s_ref, in_old, out_old, in_hbm, out_hbm, res_ref, sem):
        half = pl.multiple_of((1 - place_ref[8]) * 256, 256)
        outs = []
        for j in range(4):
            res_ref[j] = s_ref[j * 256 : (j + 1) * 256, :].astype(F32)
            dst = in_hbm.at[j, :, pl.ds(half, 256)] if j < 3 else out_hbm.at[pl.ds(half, 256)]
            outs.append(pltpu.make_async_copy(res_ref.at[j], dst, sem.at[j]))
            outs[-1].start()
        for copy in outs:
            copy.wait()

    vm = pl.BlockSpec(memory_space=pltpu.VMEM)
    hbm = pl.BlockSpec(memory_space=pl.ANY)
    return call(
        kernel,
        in_specs=[pl.BlockSpec(memory_space=pltpu.SMEM), vm, hbm, hbm],
        out_specs=[hbm, hbm],
        out_shape=[jax.ShapeDtypeStruct((3, 256, 512), F32), jax.ShapeDtypeStruct((512, 256), F32)],
        scratch_shapes=[pltpu.VMEM((4, 256, 256), F32), pltpu.SemaphoreType.DMA((4,))],
        input_output_aliases={2: 0, 3: 1},
        bytes_accessed=3 * MIB,
        name="fill_halves",
    )(place, sent, in_grad, out_grad)


def chip_hop(x_flip, z_step):
    pairs = []
    for i in range(16):
        x, z, core = i // 8, i // 2 % 4, i % 2
        pairs.append((i, ((x ^ x_flip) * 4 + (z + z_step) % 4) * 2 + core))
    return pairs


def swap_cores(value):
    return lax.ppermute(value, "ctx", [(i, i ^ 1) for i in range(16)])


def swap(pieces, axis):
    return lax.all_to_all(pieces, axis, 0, 0, tiled=True)


def on_device(tokens, out_grad, in_weight, out_weight, filters):
    position = lax.axis_index("ctx")
    chip, core = position // 2, position % 2
    weight = jnp.transpose(in_weight, (1, 0, 2))
    columns = swap(split_columns(tokens, out_grad), "ctx")
    signals = project(tokens, out_grad, weight, out_weight, filters)
    signals = swap(signals.reshape(16, 5 * BLOCK, SEQ_DEV), "ctx")
    columns = turn_columns(columns)
    other_columns = swap_cores(columns)
    flip = jnp.asarray(np.eye(256)[::-1].astype(ml_dtypes.bfloat16))
    block, pieces = convolve(
        signals, jnp.asarray(cosine_matrix()), jnp.asarray(frequency_rows()), flip
    )
    pieces = swap(pieces, "ctx")
    blocks, sources = [block], [chip]
    for x_flip, z_step in ((0, 1), (0, 3), (1, 0), (1, 1), (1, 3), (0, 2), (1, 2)):
        blocks.append(lax.ppermute(block, "ctx", chip_hop(x_flip, z_step)))
        sources.append((chip // 4 ^ x_flip) * 4 + (chip % 4 - z_step) % 4)
    place = jnp.stack(sources + [core]).astype(jnp.int32)
    partial, filter_grad = input_partial(pieces, weight)
    input_grad = sum_partials(swap(partial, "mp"))
    in_grad, out_weight_grad, send = weight_gradients(place, columns, other_columns, blocks)
    in_grad, out_weight_grad = fill_halves(place, swap_cores(send), in_grad, out_weight_grad)
    return (input_grad, jnp.transpose(in_grad, (1, 0, 2)), out_weight_grad, filter_grad)


def solution(mesh):
    in_specs = (P("ctx", None), P("ctx", None), P(None, None, "mp"), P("mp", None), P("ctx", "mp"))
    out_specs = (P("ctx", "mp"), P("ctx", None, "mp"), P("mp", "ctx"), P("ctx", "mp"))
    return jax.shard_map(
        on_device, mesh=mesh, in_specs=in_specs, out_specs=out_specs, check_vma=False
    )
```

profile of v0, /device:TPU:1, one launch (start us, length us, event | category | flops | bytes accessed | tf_op | source)
XLA Modules:
  0.0 159.0 jit_solution(4593908340350683270)
XLA Ops:
  0.6 0.0 copy-start.3
  0.6 1.2 copy-done.3
  1.9 0.0 copy-start.5
  1.9 1.2 copy-done.5
  3.1 0.0 copy-start
  3.1 0.6 split_columns.1
  3.7 37.5 %all_to_all.20.r_ref = bf16[16,512,128]{2,1,0:T(8,128)(2,1)S(1)} all-to-all(bf16[16,512,128]{2,1,0:T(8,128)(2,1)S(1)} %split_columns.1), channel_id=1, replica_groups=mesh['ctx'=16,'mp'=8] {'ctx'}, dimensions={0} | all-to-all | bytes 4194304 | tf_op jit(solution)/shard_map/all_to_all | solution.py:364
  41.2 2.4 %turn_columns.1.own_ref = bf16[512,2048]{1,0:T(8,128)(2,1)} custom-call(bf16[16,512,128]{2,1,0:T(8,128)(2,1)S(1)} %all_to_all.20.r_ref), custom_call_target="tpu_custom_call" | custom-call | bytes 4194304 | tf_op jit(solution)/shard_map/turn_columns/pallas_call | solution.py:257
  43.6 1.2 collective-permute-start
  44.7 0.0 copy-done
  44.7 0.0 copy-start.2
  44.7 2.2 %copy-done.2 = bf16[512,4096]{1,0:T(8,128)(2,1)S(1)} copy-done((bf16[512,4096]{1,0:T(8,128)(2,1)S(1)}, bf16[512,4096]{1,0:T(8,128)(2,1)}, u32[]{:S(2)}) %copy-start.2) | copy-done | bytes 4194328
  46.9 1.2 copy-done.4
  48.1 1.2 copy-done.6
  49.4 0.9 copy-done.7
  50.3 6.3 %project.1 = bf16[8,2,160,128]{3,2,1,0:T(8,128)(2,1)S(1)} custom-call(bf16[128,4096]{1,0:T(8,128)(2,1)S(1)} %copy-done.4, bf16[128,4096]{1,0:T(8,128)(2,1)S(1)} %copy-done.6, bf16[3,4096,512]{2,1,0:T(8,128)(2,1)S(1)} %bitcast.12, bf16[512,4096]{1,0:T(8,128)(2,1)S(1)} %copy-done.2, f32[128,512]{1,0:T(8,128)S(1)} %copy-done.7), custom_call_target="tpu_custom_call" | custom-call | flops 2147483648 | bytes 19922944 | tf_op jit(solution)/shard_map/project/pallas_call | solution.py:78
  56.6 15.9 %all_to_all.21.r_ref = bf16[16,160,128]{2,1,0:T(8,128)(2,1)S(1)} all-to-all(bf16[16,160,128]{2,1,0:T(8,128)(2,1)S(1)} %bitcast.14), channel_id=1, replica_groups=mesh['ctx'=16,'mp'=8] {'ctx'}, dimensions={0} | all-to-all | bytes 1310720 | tf_op jit(solution)/shard_map/all_to_all | solution.py:364
  72.5 0.0 copy-done.8
  72.5 0.0 copy-done.9
  72.5 0.0 copy-done.10
  72.5 8.1 %convolve.1 = (bf16[128,2048]{1,0:T(8,128)(2,1)S(1)}, bf16[16,128,128]{2,1,0:T(8,128)(2,1)}) custom-call(bf16[16,160,128]{2,1,0:T(8,128)(2,1)S(1)} %all_to_all.21.r_ref, bf16[2048,2048]{1,0:T(8,128)(2,1)S(1)} %copy-done.8, f32[8,2048]{1,0:T(8,128)S(1)} %copy-done.10, bf16[256,256]{1,0:T(8,128)(2,1)S(1)} %copy-done.9), custom_call_target="tpu_custom_call" | custom-call | flops 3221225472 | bytes 12582912 | tf_op jit(solution)/shard_map/convolve/pallas_call | solution.py:175
  80.7 1.4 collective-permute-start.7
  82.1 1.8 %collective-permute-start.6 = (bf16[128,2048]{1,0:T(8,128)(2,1)S(1)}, bf16[128,2048]{1,0:T(8,128)(2,1)S(1)}, u32[]{:S(2)}, u32[]{:S(2)}) collective-permute-start(bf16[128,2048]{1,0:T(8,128)(2,1)S(1)} %get-tuple-element.15.refs_0_), channel_id=1, source_target_pairs={{0,32},{8,40},{16,48},{24,56},{32,0},{40,8},{48,16},{56,24},{64,96... | collective-permute-start | bytes 1572872 | tf_op jit(solution)/shard_map/ppermute | solution.py:383
  83.9 3.3 %collective-permute-start.5 = (bf16[128,2048]{1,0:T(8,128)(2,1)S(1)}, bf16[128,2048]{1,0:T(8,128)(2,1)S(1)}, u32[]{:S(2)}, u32[]{:S(2)}) collective-permute-start(bf16[128,2048]{1,0:T(8,128)(2,1)S(1)} %get-tuple-element.15.refs_0_), channel_id=1, source_target_pairs={{0,112},{8,120},{16,64},{24,72},{32,80},{40,88},{48,96},{56,104},{... | collective-permute-start | bytes 1572872 | tf_op jit(solution)/shard_map/ppermute | solution.py:383
  87.2 4.5 %all-to-all-start.1 = ((bf16[16,128,128]{2,1,0:T(8,128)(2,1)}), bf16[16,128,128]{2,1,0:T(8,128)(2,1)S(1)}, u32[]{:S(2)}, u32[]{:S(2)}) async-start(bf16[16,128,128]{2,1,0:T(8,128)(2,1)} %get-tuple-element.13), calls=%async_computation.1 | async-start | bytes 1048576 | tf_op jit(solution)/shard_map/all_to_all | solution.py:364
  91.7 3.8 %collective-permute-start.4 = (bf16[128,2048]{1,0:T(8,128)(2,1)S(1)}, bf16[128,2048]{1,0:T(8,128)(2,1)}, u32[]{:S(2)}, u32[]{:S(2)}) collective-permute-start(bf16[128,2048]{1,0:T(8,128)(2,1)S(1)} %get-tuple-element.15.refs_0_), channel_id=1, source_target_pairs={{0,80},{8,88},{16,96},{24,104},{32,112},{40,120},{48,64},{56,72},{... | collective-permute-start | bytes 1572872 | tf_op jit(solution)/shard_map/ppermute | solution.py:383
  95.6 1.9 %collective-permute-done.7.refs_7_ = bf16[128,2048]{1,0:T(8,128)(2,1)S(1)} collective-permute-done((bf16[128,2048]{1,0:T(8,128)(2,1)S(1)}, bf16[128,2048]{1,0:T(8,128)(2,1)S(1)}, u32[]{:S(2)}, u32[]{:S(2)}) %collective-permute-start.7) | collective-permute-done | bytes 524320 | tf_op jit(solution)/shard_map/ppermute | solution.py:383
  97.4 0.7 collective-permute-start.3
  98.2 9.5 %collective-permute-done.6.refs_6_ = bf16[128,2048]{1,0:T(8,128)(2,1)S(1)} collective-permute-done((bf16[128,2048]{1,0:T(8,128)(2,1)S(1)}, bf16[128,2048]{1,0:T(8,128)(2,1)S(1)}, u32[]{:S(2)}, u32[]{:S(2)}) %collective-permute-start.6) | collective-permute-done | bytes 524320 | tf_op jit(solution)/shard_map/ppermute | solution.py:383
  107.6 16.6 %collective-permute-start.2 = (bf16[128,2048]{1,0:T(8,128)(2,1)S(1)}, bf16[128,2048]{1,0:T(8,128)(2,1)}, u32[]{:S(2)}, u32[]{:S(2)}) collective-permute-start(bf16[128,2048]{1,0:T(8,128)(2,1)S(1)} %get-tuple-element.15.refs_0_), channel_id=1, source_target_pairs={{0,48},{8,56},{16,0},{24,8},{32,16},{40,24},{48,32},{56,40},{64,11... | collective-permute-start | bytes 1572872 | tf_op jit(solution)/shard_map/ppermute | solution.py:383
  124.2 0.0 collective-permute-done.5.refs_5_
  124.2 0.0 collective-permute-start.1
  124.2 2.1 %all-to-all-done.1.r_ref = bf16[16,128,128]{2,1,0:T(8,128)(2,1)S(1)} async-done(((bf16[16,128,128]{2,1,0:T(8,128)(2,1)}), bf16[16,128,128]{2,1,0:T(8,128)(2,1)S(1)}, u32[]{:S(2)}, u32[]{:S(2)}) %all-to-all-start.1) | async-done | bytes 524320 | tf_op jit(solution)/shard_map/all_to_all | solution.py:364
  126.3 4.6 %copy-done.1 = bf16[4096,3,512]{2,0,1:T(8,128)(2,1)S(1)} copy-done((bf16[4096,3,512]{2,0,1:T(8,128)(2,1)S(1)}, bf16[4096,3,512]{2,0,1:T(8,128)(2,1)}, u32[]{:S(2)}) %copy-start.1) | copy-done | bytes 12582936
  130.9 6.3 %input_partial.1 = (bf16[8,512,128]{2,1,0:T(8,128)(2,1)}, f32[128,512]{1,0:T(8,128)}) custom-call(bf16[16,128,128]{2,1,0:T(8,128)(2,1)S(1)} %all-to-all-done.1.r_ref, bf16[3,4096,512]{2,1,0:T(8,128)(2,1)S(1)} %bitcast.13), custom_call_target="tpu_custom_call" | custom-call | flops 1610612736 | bytes 14680064 | tf_op jit(solution)/shard_map/input_partial/pallas_call | solution.py:210
  137.2 4.2 %all-to-all-start.2 = ((bf16[8,512,128]{2,1,0:T(8,128)(2,1)}), bf16[8,512,128]{2,1,0:T(8,128)(2,1)S(1)}, u32[]{:S(2)}, u32[]{:S(2)}) async-start(bf16[8,512,128]{2,1,0:T(8,128)(2,1)} %get-tuple-element.14), calls=%async_computation.2 | async-start | bytes 2097152 | tf_op jit(solution)/shard_map/all_to_all | solution.py:364
  141.4 0.1 stack.39.place_ref
  141.5 0.0 collective-permute-done.4.refs_4_
  141.5 0.0 collective-permute-done.3.refs_3_
  141.5 0.0 collective-permute-done.2.refs_2_
  141.5 0.0 collective-permute-done.1.refs_1_
  141.5 0.0 collective-permute-done.other_ref
  141.5 9.9 %weight_gradients.1 = (f32[3,256,512]{2,1,0:T(8,128)}, f32[512,256]{1,0:T(8,128)}, bf16[1024,256]{1,0:T(8,128)(2,1)}) custom-call(s32[9]{0:T(128)S(1)} %stack.39.place_ref, bf16[512,2048]{1,0:T(8,128)(2,1)} %turn_columns.1.own_ref, bf16[512,2048]{1,0:T(8,128)(2,1)} %collective-permute-done.other_ref, bf16[128,2048]{1,0:T(8,128)(2,1)S(1)} %get-tuple-element.15.refs_0_, ...), custom_call_target="tpu_custom_call" | custom-call | flops 2147483648 | bytes 10485760 | tf_op jit(solution)/shard_map/weight_gradients/pallas_call | solution.py:304
  151.5 0.5 collective-permute-start.8
  152.0 4.4 %all-to-all-done.2.p_ref = bf16[8,512,128]{2,1,0:T(8,128)(2,1)S(1)} async-done(((bf16[8,512,128]{2,1,0:T(8,128)(2,1)}), bf16[8,512,128]{2,1,0:T(8,128)(2,1)S(1)}, u32[]{:S(2)}, u32[]{:S(2)}) %all-to-all-start.2) | async-done | bytes 1048608 | tf_op jit(solution)/shard_map/all_to_all | solution.py:364
  156.4 0.9 sum_partials.1
  157.3 0.0 collective-permute-done.8.s_ref
  157.3 1.6 fill_halves.1
  (7 shorter events, 0.0 us)
Async XLA Ops:
  0.6 1.2 copy-start.3
  1.9 1.2 copy-start.5
  3.1 41.6 %copy-start = (bf16[4096,3,512]{2,0,1:T(8,128)(2,1)S(1)}, bf16[4096,3,512]{2,0,1:T(8,128)(2,1)}, u32[]{:S(2)}) copy-start(bf16[4096,3,512]{2,0,1:T(8,128)(2,1)} %param.10) | copy-start | bytes 37748740
  43.6 98.0 %collective-permute-start = (bf16[512,2048]{1,0:T(8,128)(2,1)}, bf16[512,2048]{1,0:T(8,128)(2,1)}, u32[]{:S(2)}, u32[]{:S(2)}) collective-permute-start(bf16[512,2048]{1,0:T(8,128)(2,1)} %turn_columns.1.own_ref), channel_id=1, source_target_pairs={{0,8},{8,0},{16,24},{24,16},{32,40},{40,32},{48,56},{56,48},{64,72... | collective-permute-start | bytes 6291464 | tf_op jit(solution)/shard_map/ppermute | solution.py:360
  44.7 2.2 %copy-start.2 = (bf16[512,4096]{1,0:T(8,128)(2,1)S(1)}, bf16[512,4096]{1,0:T(8,128)(2,1)}, u32[]{:S(2)}) copy-start(bf16[512,4096]{1,0:T(8,128)(2,1)} %ow_ref.1) | copy-start | bytes 12582916
  46.9 1.2 copy-start.4
  48.1 1.2 copy-start.6
  49.4 0.9 copy-start.7
  50.3 22.2 %copy-start.8 = (bf16[2048,2048]{1,0:T(8,128)(2,1)S(1)}, bf16[2048,2048]{1,0:T(8,128)(2,1)}, u32[]{:S(2)}) copy-start(bf16[2048,2048]{1,0:T(8,128)(2,1)} %constant.108.clone.m_hbm) | copy-start | bytes 25165828
  50.3 22.2 %copy-start.9 = (bf16[256,256]{1,0:T(8,128)(2,1)S(1)}, bf16[256,256]{1,0:T(8,128)(2,1)}, u32[]{:S(2)}) copy-start(bf16[256,256]{1,0:T(8,128)(2,1)} %constant.107.clone.j_ref) | copy-start | bytes 393220
  50.3 22.2 %copy-start.10 = (f32[8,2048]{1,0:T(8,128)S(1)}, f32[8,2048]{1,0:T(8,128)}, u32[]{:S(2)}) copy-start(f32[8,2048]{1,0:T(8,128)} %constant.109.clone.w_ref) | copy-start | bytes 196612
  80.7 16.8 %collective-permute-start.7 = (bf16[128,2048]{1,0:T(8,128)(2,1)S(1)}, bf16[128,2048]{1,0:T(8,128)(2,1)S(1)}, u32[]{:S(2)}, u32[]{:S(2)}) collective-permute-start(bf16[128,2048]{1,0:T(8,128)(2,1)S(1)} %get-tuple-element.15.refs_0_), channel_id=1, source_target_pairs={{0,96},{8,104},{16,112},{24,120},{32,64},{40,72},{48,80},{56,88},{... | collective-permute-start | bytes 1572872 | tf_op jit(solution)/shard_map/ppermute | solution.py:383
  82.1 25.6 %collective-permute-start.6 = (bf16[128,2048]{1,0:T(8,128)(2,1)S(1)}, bf16[128,2048]{1,0:T(8,128)(2,1)S(1)}, u32[]{:S(2)}, u32[]{:S(2)}) collective-permute-start(bf16[128,2048]{1,0:T(8,128)(2,1)S(1)} %get-tuple-element.15.refs_0_), channel_id=1, source_target_pairs={{0,32},{8,40},{16,48},{24,56},{32,0},{40,8},{48,16},{56,24},{64,96... | collective-permute-start | bytes 1572872 | tf_op jit(solution)/shard_map/ppermute | solution.py:383
  83.9 40.3 %collective-permute-start.5 = (bf16[128,2048]{1,0:T(8,128)(2,1)S(1)}, bf16[128,2048]{1,0:T(8,128)(2,1)S(1)}, u32[]{:S(2)}, u32[]{:S(2)}) collective-permute-start(bf16[128,2048]{1,0:T(8,128)(2,1)S(1)} %get-tuple-element.15.refs_0_), channel_id=1, source_target_pairs={{0,112},{8,120},{16,64},{24,72},{32,80},{40,88},{48,96},{56,104},{... | collective-permute-start | bytes 1572872 | tf_op jit(solution)/shard_map/ppermute | solution.py:383
  87.2 39.1 %all-to-all-start.1 = ((bf16[16,128,128]{2,1,0:T(8,128)(2,1)}), bf16[16,128,128]{2,1,0:T(8,128)(2,1)S(1)}, u32[]{:S(2)}, u32[]{:S(2)}) async-start(bf16[16,128,128]{2,1,0:T(8,128)(2,1)} %get-tuple-element.13), calls=%async_computation.1 | async-start | bytes 1048576 | tf_op jit(solution)/shard_map/all_to_all | solution.py:364
  91.7 49.8 %collective-permute-start.4 = (bf16[128,2048]{1,0:T(8,128)(2,1)S(1)}, bf16[128,2048]{1,0:T(8,128)(2,1)}, u32[]{:S(2)}, u32[]{:S(2)}) collective-permute-start(bf16[128,2048]{1,0:T(8,128)(2,1)S(1)} %get-tuple-element.15.refs_0_), channel_id=1, source_target_pairs={{0,80},{8,88},{16,96},{24,104},{32,112},{40,120},{48,64},{56,72},{... | collective-permute-start | bytes 1572872 | tf_op jit(solution)/shard_map/ppermute | solution.py:383
  97.4 44.1 %collective-permute-start.3 = (bf16[128,2048]{1,0:T(8,128)(2,1)S(1)}, bf16[128,2048]{1,0:T(8,128)(2,1)}, u32[]{:S(2)}, u32[]{:S(2)}) collective-permute-start(bf16[128,2048]{1,0:T(8,128)(2,1)S(1)} %get-tuple-element.15.refs_0_), channel_id=1, source_target_pairs={{0,64},{8,72},{16,80},{24,88},{32,96},{40,104},{48,112},{56,120},{... | collective-permute-start | bytes 1572872 | tf_op jit(solution)/shard_map/ppermute | solution.py:383
  107.6 33.9 %collective-permute-start.2 = (bf16[128,2048]{1,0:T(8,128)(2,1)S(1)}, bf16[128,2048]{1,0:T(8,128)(2,1)}, u32[]{:S(2)}, u32[]{:S(2)}) collective-permute-start(bf16[128,2048]{1,0:T(8,128)(2,1)S(1)} %get-tuple-element.15.refs_0_), channel_id=1, source_target_pairs={{0,48},{8,56},{16,0},{24,8},{32,16},{40,24},{48,32},{56,40},{64,11... | collective-permute-start | bytes 1572872 | tf_op jit(solution)/shard_map/ppermute | solution.py:383
  124.2 17.3 %collective-permute-start.1 = (bf16[128,2048]{1,0:T(8,128)(2,1)S(1)}, bf16[128,2048]{1,0:T(8,128)(2,1)}, u32[]{:S(2)}, u32[]{:S(2)}) collective-permute-start(bf16[128,2048]{1,0:T(8,128)(2,1)S(1)} %get-tuple-element.15.refs_0_), channel_id=1, source_target_pairs={{0,16},{8,24},{16,32},{24,40},{32,48},{40,56},{48,0},{56,8},{64,80... | collective-permute-start | bytes 1572872 | tf_op jit(solution)/shard_map/ppermute | solution.py:383
  126.3 4.6 %copy-start.1 = (bf16[4096,3,512]{2,0,1:T(8,128)(2,1)S(1)}, bf16[4096,3,512]{2,0,1:T(8,128)(2,1)}, u32[]{:S(2)}) copy-start(bf16[4096,3,512]{2,0,1:T(8,128)(2,1)} %param.10) | copy-start | bytes 37748740
  137.2 19.2 %all-to-all-start.2 = ((bf16[8,512,128]{2,1,0:T(8,128)(2,1)}), bf16[8,512,128]{2,1,0:T(8,128)(2,1)S(1)}, u32[]{:S(2)}, u32[]{:S(2)}) async-start(bf16[8,512,128]{2,1,0:T(8,128)(2,1)} %get-tuple-element.14), calls=%async_computation.2 | async-start | bytes 2097152 | tf_op jit(solution)/shard_map/all_to_all | solution.py:364
  151.5 5.8 %collective-permute-start.8 = (bf16[1024,256]{1,0:T(8,128)(2,1)}, bf16[1024,256]{1,0:T(8,128)(2,1)S(1)}, u32[]{:S(2)}, u32[]{:S(2)}) collective-permute-start(bf16[1024,256]{1,0:T(8,128)(2,1)} %get-tuple-element.16), channel_id=1, source_target_pairs={{0,8},{8,0},{16,24},{24,16},{32,40},{40,32},{48,56},{56,48},{64,72... | collective-permute-start | bytes 1572872 | tf_op jit(solution)/shard_map/ppermute | solution.py:360
where the time goes:
time: 160 us; the launch traced here: 159 us
  blocking collectives  53.4 us (33%)
  starting transfers between devices  38.2 us (24%)
  Pallas kernels  36 us (22%)
  waiting for transfers between devices  17.8 us (11%)
  local copies, waits for them, and re-layouts  12.7 us (8%)
    all_to_all x2, blocking collectives, swap(): return lax.all_to_all(pieces, axis, 0, 0, tiled=True)  53.4 us
    ppermute x7, starting transfers between devices, on_device(): blocks.append(lax.ppermute(block, 'ctx', chip_hop(x_flip, z_step)))  27.7 us
    unnamed x22, local copies, waits for them, and re-layouts  12.6 us
    ppermute x7, waiting for transfers between devices, on_device(): blocks.append(lax.ppermute(block, 'ctx', chip_hop(x_flip, z_step)))  11.3 us
    pallas_call x1, Pallas kernels, weight_gradients(): call(kernel, in_specs=[pl.BlockSpec(memory_space=pltpu.SMEM), vm, vm] + [...  9.92 us
    all_to_all x2, starting transfers between devices, swap(): return lax.all_to_all(pieces, axis, 0, 0, tiled=True)  8.76 us
    pallas_call x1, Pallas kernels, convolve(): call(kernel, in_specs=[vm, pl.BlockSpec(memory_space=pl.ANY), vm, vm], ou...  8.13 us
    all_to_all x2, waiting for transfers between devices, swap(): return lax.all_to_all(pieces, axis, 0, 0, tiled=True)  6.47 us
  transfers between devices with their start and end apart: 11, of which 4 were waited for; matrix products, arithmetic and copies ran while one was open for 0% of the time, Pallas kernels for 20%

commit v1 on v0

v1 whole, which is shorter than its diff:
```python
import math

import jax
import jax.numpy as jnp
import ml_dtypes
import numpy as np
from jax import lax
from jax.experimental import pallas as pl
from jax.experimental.pallas import tpu as pltpu
from jax.sharding import PartitionSpec as P

F32 = jnp.float32
BF16 = jnp.bfloat16
NT = (((1,), (1,)), ((), ()))
NN = (((1,), (0,)), ((), ()))
MIB = 1 << 20
BLOCK = 32
SEQ_DEV = 128
SEQ = 2048


def dot(a, b, dims=NN):
    return lax.dot_general(a, b, dims, preferred_element_type=F32)


def in_hbm(value):
    return pltpu.with_memory_space_constraint(value, pltpu.HBM)


def in_vmem(value):
    return pltpu.with_memory_space_constraint(value, pltpu.VMEM)


class Stream:
    def __init__(self, groups, ahead):
        self.groups, self.started, self.ahead = groups, 0, ahead
        self.start(ahead)

    def start(self, upto):
        while self.started < min(upto, len(self.groups)):
            for copy in self.groups[self.started]:
                copy.start()
            self.started += 1

    def wait(self, index):
        for copy in self.groups[index]:
            copy.wait()
        self.start(index + 1 + self.ahead)


def call(kernel, *, flops=0, bytes_accessed=0, vmem=32, **kw):
    return pl.pallas_call(
        kernel,
        compiler_params=pltpu.CompilerParams(vmem_limit_bytes=vmem * MIB),
        cost_estimate=pl.CostEstimate(flops=flops, bytes_accessed=bytes_accessed, transcendentals=0),
        **kw,
    )


def split_columns(quarter, tokens, out_grad):
    def kernel(y_ref, t_hbm, g_hbm, o_ref, sem):
        copies = []
        for chip in range(8):
            lanes = pl.ds(pl.multiple_of(chip * 512 + y_ref[0] * 128, 128), 128)
            copies.append(pltpu.make_async_copy(t_hbm.at[:, lanes], o_ref.at[chip, 0], sem.at[chip, 0]))
            copies.append(pltpu.make_async_copy(g_hbm.at[:, lanes], o_ref.at[chip, 1], sem.at[chip, 1]))
        for copy in copies:
            copy.start()
        for copy in copies:
            copy.wait()

    hbm = pl.BlockSpec(memory_space=pl.ANY)
    return call(
        kernel,
        in_specs=[pl.BlockSpec(memory_space=pltpu.SMEM), hbm, hbm],
        out_specs=pl.BlockSpec(memory_space=pltpu.VMEM),
        out_shape=jax.ShapeDtypeStruct((8, 2, SEQ_DEV, 128), BF16),
        scratch_shapes=[pltpu.SemaphoreType.DMA((8, 2))],
        bytes_accessed=MIB,
        vmem=4,
        name="split_columns",
    )(quarter, in_hbm(tokens), in_hbm(out_grad))


def project(tokens, out_grad, weight, out_weight, filters):
    depth = 2048
    steps = 4096 // depth
    gate = 256

    def kernel(t_hbm, g_hbm, f_hbm, w_hbm, ow_hbm, o_ref, f_ref, t_ref, g_ref, w_ref, ow_ref, sem):
        def fetch(src, dst, at):
            return pltpu.make_async_copy(src, dst, sem.at[at])

        gates = [pl.ds(gate * i, gate) for i in range(512 // gate)]
        groups = [[fetch(ow_hbm.at[rows], ow_ref.at[rows], i)] for i, rows in enumerate(gates)]
        first = len(groups)
        groups[0] = [fetch(f_hbm, f_ref, first), fetch(g_hbm, g_ref, first + 1)] + groups[0]
        for j in range(3):
            for k in range(steps):
                rows = pl.ds(k * depth, depth)
                at = first + 3 + j * steps + k
                groups.append([fetch(w_hbm.at[j, rows], w_ref.at[j, rows], at)])
        groups[first].append(fetch(t_hbm, t_ref, first + 2))
        stream = Stream(groups, 8)

        def put(first, sig, rows):
            n = rows.shape[0] // BLOCK
            core, chip = first // 256, first % 256 // BLOCK
            o_ref[chip : chip + n, core, sig * BLOCK : (sig + 1) * BLOCK, :] = rows.astype(BF16).reshape(
                n, BLOCK, SEQ_DEV
            )

        for i in range(512 // gate):
            stream.wait(i)
            put(i * gate, 3, dot(ow_ref[i * gate : (i + 1) * gate], g_ref[...], NT))
        for c in range(2):
            put(c * 256, 4, f_ref[:, c * 256 : (c + 1) * 256].T)
        for j in range(3):
            total = None
            for k in range(steps):
                stream.wait(first + j * steps + k)
                part = dot(t_ref[:, k * depth : (k + 1) * depth], w_ref[j, k * depth : (k + 1) * depth])
                total = part if total is None else total + part
            for c in range(2):
                put(c * 256, j, total[:, c * 256 : (c + 1) * 256].T)

    vm = pl.BlockSpec(memory_space=pltpu.VMEM)
    hbm = pl.BlockSpec(memory_space=pl.ANY)
    return call(
        kernel,
        in_specs=[hbm] * 5,
        out_specs=vm,
        out_shape=jax.ShapeDtypeStruct((8, 2, 5 * BLOCK, SEQ_DEV), BF16),
        scratch_shapes=[
            pltpu.VMEM((SEQ_DEV, 512), F32),
            pltpu.VMEM((SEQ_DEV, 4096), BF16),
            pltpu.VMEM((SEQ_DEV, 4096), BF16),
            pltpu.VMEM((3, 4096, 512), BF16),
            pltpu.VMEM((512, 4096), BF16),
            pltpu.SemaphoreType.DMA((3 + 512 // gate + 3 * steps,)),
        ],
        flops=2 * 128 * 4096 * 2048,
        bytes_accessed=19 * MIB,
        vmem=28,
        name="project",
    )(in_hbm(tokens), in_hbm(out_grad), in_hbm(filters), in_hbm(weight), in_hbm(out_weight))


def cosine_matrix():
    odd = 2 * np.arange(SEQ, dtype=np.int64) + 1
    turns = np.outer(odd, odd) % (8 * SEQ)
    return np.cos(turns * (2.0 * np.pi / (8 * SEQ))).astype(ml_dtypes.bfloat16)


def frequency_rows():
    half = (2 * np.arange(SEQ) + 1) * (np.pi / (4 * SEQ))
    sign = 1.0 - 2.0 * (np.arange(SEQ) % 2)
    rows = np.zeros((8, SEQ), np.float32)
    rows[0], rows[1], rows[2] = np.cos(half), np.sin(half), sign
    return rows


def convolve(received, matrix, rows, flip):
    chunk = 512
    n_chunks = SEQ // chunk

    def kernel(r_ref, m_hbm, w_ref, j_ref, b_ref, o_ref, m_ref, x_ref, y_ref, sem):
        chunks = [pl.ds(n * chunk, chunk) for n in range(n_chunks)]
        stream = Stream(
            [[pltpu.make_async_copy(m_hbm.at[:, c], m_ref.at[:, c], sem.at[n])] for n, c in enumerate(chunks)], 4
        )
        rev = j_ref[...]
        for b in range(16):
            part = r_ref[b]
            key, value = part[32:64].astype(F32), part[64:96].astype(F32)
            query, gate = part[0:32].astype(F32), part[96:128].astype(F32)
            lanes = pl.ds(b * 128, 128)
            x_ref[0:32, lanes] = part[128:160]
            x_ref[32:64, lanes] = (key * value).astype(BF16)
            x_ref[64:96, lanes] = (gate * query).astype(BF16)
        for b in range(8):
            x_ref[96:192, pl.ds((7 - b) * 256, 256)] = dot(x_ref[0:96, pl.ds(b * 256, 256)], rev).astype(BF16)
        for n in range(n_chunks):
            lanes = pl.ds(n * chunk, chunk)
            stream.wait(n)
            spec = dot(x_ref[...], m_ref[:, lanes])
            wr, wi, sign = w_ref[0:1, lanes], w_ref[1:2, lanes], w_ref[2:3, lanes]
            hr, mr, gr = spec[0:32], spec[32:64], spec[64:96]
            neg = -sign
            hi, mi, gi = spec[96:128] * neg, spec[128:160] * neg, spec[160:192] * neg
            hwr, hwi = hr * wr - hi * wi, hr * wi + hi * wr
            mwr, mwi = mr * wr - mi * wi, mr * wi + mi * wr
            y_ref[0:32, lanes] = (hwr * mr - hwi * mi).astype(BF16)
            y_ref[32:64, lanes] = (gr * hwr + gi * hwi).astype(BF16)
            y_ref[64:96, lanes] = (gr * mwr + gi * mwi).astype(BF16)
            imag = jnp.concatenate(
                [hwr * mi + hwi * mr, gi * hwr - gr * hwi, gi * mwr - gr * mwi], axis=0
            ).astype(BF16)
            for b in range(chunk // 256):
                at = SEQ - (n * chunk + (b + 1) * 256)
                y_ref[96:192, pl.ds(at, 256)] = dot(imag[:, b * 256 : (b + 1) * 256], rev).astype(BF16)
        scale = 1.0 / SEQ
        for n in range(n_chunks):
            lanes = pl.ds(n * chunk, chunk)
            back = dot(y_ref[...], m_ref[:, lanes])
            back = (back[0:96] - back[96:192] * w_ref[2:3, lanes]) * scale
            for b in range(chunk // 128):
                at = n * (chunk // 128) + b
                part = r_ref[at]
                cut = slice(b * 128, (b + 1) * 128)
                conv, mixed, raw = back[0:32, cut], back[32:64, cut], back[64:96, cut]
                query, key, value, gate = (part[32 * i : 32 * i + 32].astype(F32) for i in range(4))
                gq = (gate * conv).astype(BF16)
                gk = (mixed * value).astype(BF16)
                gv = (mixed * key).astype(BF16)
                pos = pl.ds((at % 2 * 8 + at // 2) * 128, 128)
                b_ref[0:32, pos] = gq
                b_ref[32:64, pos] = gk
                b_ref[64:96, pos] = gv
                b_ref[96:128, pos] = (query * conv).astype(BF16)
                o_ref[at, 0:32, :] = gq
                o_ref[at, 32:64, :] = gk
                o_ref[at, 64:96, :] = gv
                o_ref[at, 96:128, :] = (raw * (1.0 / math.sqrt(SEQ))).astype(BF16)

    vm = pl.BlockSpec(memory_space=pltpu.VMEM)
    return call(
        kernel,
        in_specs=[vm, pl.BlockSpec(memory_space=pl.ANY), vm, vm],
        out_specs=[vm, vm],
        out_shape=[
            jax.ShapeDtypeStruct((128, SEQ), BF16),
            jax.ShapeDtypeStruct((16, 128, 128), BF16),
        ],
        scratch_shapes=[
            pltpu.VMEM((SEQ, SEQ), BF16),
            pltpu.VMEM((192, SEQ), BF16),
            pltpu.VMEM((192, SEQ), BF16),
            pltpu.SemaphoreType.DMA((n_chunks,)),
        ],
        flops=4 * 192 * SEQ * SEQ,
        bytes_accessed=12 * MIB,
        vmem=20,
        name="convolve",
    )(received, in_hbm(matrix), rows, flip)


def input_partial(received, weight):
    steps = 8
    depth = 4096 // steps

    def kernel(r_ref, w_hbm, o_ref, f_ref, w_ref, g_ref, sem):
        groups = []
        for s in range(steps):
            rows = pl.ds(s * depth, depth)
            groups.append(
                [
                    pltpu.make_async_copy(w_hbm.at[j, rows], w_ref.at[rows, pl.ds(j * 512, 512)], sem.at[s, j])
                    for j in range(3)
                ]
            )
        stream = Stream(groups, steps)
        for chip in range(8):
            for core in range(2):
                at = core * 256 + chip * BLOCK
                for j in range(4):
                    g_ref[j * 512 + at : j * 512 + at + BLOCK, :] = r_ref[
                        2 * chip + core, j * BLOCK : (j + 1) * BLOCK, :
                    ]
        grads = g_ref[0:1536].astype(F32).T.astype(BF16)
        f_ref[...] = g_ref[1536:2048].astype(F32).T
        for s in range(steps):
            stream.wait(s)
            o_ref[s] = dot(grads, w_ref[s * depth : (s + 1) * depth], NT).astype(BF16)

    vm = pl.BlockSpec(memory_space=pltpu.VMEM)
    return call(
        kernel,
        in_specs=[vm, pl.BlockSpec(memory_space=pl.ANY)],
        out_specs=[vm, vm],
        out_shape=[
            jax.ShapeDtypeStruct((8, SEQ_DEV, 512), BF16),
            jax.ShapeDtypeStruct((SEQ_DEV, 512), F32),
        ],
        scratch_shapes=[
            pltpu.VMEM((4096, 1536), BF16),
            pltpu.VMEM((2048, SEQ_DEV), BF16),
            pltpu.SemaphoreType.DMA((steps, 3)),
        ],
        flops=2 * 128 * 4096 * 1536,
        bytes_accessed=14 * MIB,
        vmem=24,
        name="input_partial",
    )(received, in_hbm(weight))


def sum_partials(parts):
    def kernel(p_ref, o_ref):
        total = p_ref[0].astype(F32)
        for i in range(1, 8):
            total = total + p_ref[i].astype(F32)
        o_ref[...] = total.astype(BF16)

    vm = pl.BlockSpec(memory_space=pltpu.VMEM)
    return call(
        kernel,
        in_specs=[vm],
        out_specs=vm,
        out_shape=jax.ShapeDtypeStruct((SEQ_DEV, 512), BF16),
        bytes_accessed=MIB,
        name="sum_partials",
    )(parts)


def pair(first, second, third, fourth):
    def kernel(a, b, c, d, o_ref, p_ref, sem):
        copies = []
        for i, (src, out) in enumerate(((a, o_ref), (b, o_ref), (c, p_ref), (d, p_ref))):
            copies.append(pltpu.make_async_copy(src, out.at[pl.ds(i % 2 * 128, 128)], sem.at[i]))
        for copy in copies:
            copy.start()
        for copy in copies:
            copy.wait()

    hbm = pl.BlockSpec(memory_space=pl.ANY)
    return call(
        kernel,
        in_specs=[hbm] * 4,
        out_specs=[pl.BlockSpec(memory_space=pltpu.VMEM)] * 2,
        out_shape=[jax.ShapeDtypeStruct((256, SEQ), BF16)] * 2,
        scratch_shapes=[pltpu.SemaphoreType.DMA((4,))],
        bytes_accessed=4 * MIB,
        vmem=8,
        name="pair",
    )(in_hbm(first), in_hbm(second), in_hbm(third), in_hbm(fourth))


def weight_gradients(place, columns, blocks):
    factor = 1.0 / math.sqrt(SEQ)
    first_rows = [first for _, first in blocks]

    def kernel(place_ref, *refs):
        column_refs, block_refs = refs[:8], refs[8:16]
        in_hbm, out_hbm, send_ref, t_ref, g_ref, res_ref, t_sem, sem, out_sem = refs[16:]
        core = place_ref[8]
        t_copies = [[], []]
        for j in range(2):
            for i in range(8):
                lanes = pl.ds(pl.multiple_of(place_ref[9 + i % 4] * 128, 128), 128)
                t_copies[j].append(
                    pltpu.make_async_copy(
                        column_refs[i].at[:, j], t_ref.at[j, i // 4, :, :, lanes], t_sem.at[j, i]
                    )
                )
        copies = [[], [], [], []]
        for j in range(4):
            for k in range(8):
                at = pl.multiple_of(place_ref[k] * BLOCK, BLOCK)
                copies[j].append(
                    pltpu.make_async_copy(
                        block_refs[k].at[pl.ds(first_rows[k] + j * BLOCK, BLOCK)], g_ref.at[j, pl.ds(at, BLOCK)], sem.at[j, k]
                    )
                )
        for copy in t_copies[0] + copies[0] + copies[1] + copies[2] + t_copies[1] + copies[3]:
            copy.start()
        half = pl.multiple_of(core * 256, 256)
        rest = pl.multiple_of((1 - core) * 256, 256)
        outs = []
        for j in range(4):
            for copy in copies[j] + (t_copies[j // 3] if j % 3 == 0 else []):
                copy.wait()
            own = g_ref[j, :, pl.ds(pl.multiple_of(core * 1024, 1024), 1024)]
            other = g_ref[j, :, pl.ds(pl.multiple_of((1 - core) * 1024, 1024), 1024)]
            total = dot(own, t_ref[j // 3, 0].reshape(1024, 512)) + dot(other, t_ref[j // 3, 1].reshape(1024, 512))
            total = total * factor
            if j < 3:
                res_ref[j] = total.T
                send_ref[j * 256 : (j + 1) * 256, :] = res_ref[j, pl.ds(rest, 256), :].astype(BF16)
                src, dst = res_ref.at[j, pl.ds(half, 256)], in_hbm.at[j, :, pl.ds(half, 256)]
            else:
                res_ref[3, 0:256] = total[:, 0:256]
                res_ref[3, 256:512] = total[:, 256:512]
                send_ref[768:1024, :] = res_ref[3, pl.ds(rest, 256), :].astype(BF16)
                src, dst = res_ref.at[3, pl.ds(half, 256)], out_hbm.at[pl.ds(half, 256)]
            outs.append(pltpu.make_async_copy(src, dst, out_sem.at[j]))
            outs[-1].start()
        for copy in outs:
            copy.wait()

    vm = pl.BlockSpec(memory_space=pltpu.VMEM)
    hbm = pl.BlockSpec(memory_space=pl.ANY)
    return call(
        kernel,
        in_specs=[pl.BlockSpec(memory_space=pltpu.SMEM)] + [hbm] * 16,
        out_specs=[hbm, hbm, vm],
        out_shape=[
            jax.ShapeDtypeStruct((3, 256, 512), F32),
            jax.ShapeDtypeStruct((512, 256), F32),
            jax.ShapeDtypeStruct((1024, 256), BF16),
        ],
        scratch_shapes=[
            pltpu.VMEM((2, 2, 8, SEQ_DEV, 512), BF16),
            pltpu.VMEM((4, 256, SEQ), BF16),
            pltpu.VMEM((4, 512, 256), F32),
            pltpu.SemaphoreType.DMA((2, 8)),
            pltpu.SemaphoreType.DMA((4, 8)),
            pltpu.SemaphoreType.DMA((4,)),
        ],
        flops=4 * 1024 * 256 * SEQ,
        bytes_accessed=10 * MIB,
        vmem=24,
        name="weight_gradients",
    )(place, *[in_hbm(value) for value in columns + [block for block, _ in blocks]])


def fill_halves(place, sent, in_grad, out_grad):
    def kernel(place_ref, s_ref, in_old, out_old, in_hbm, out_hbm, res_ref, sem):
        half = pl.multiple_of((1 - place_ref[8]) * 256, 256)
        outs = []
        for j in range(4):
            res_ref[j] = s_ref[j * 256 : (j + 1) * 256, :].astype(F32)
            dst = in_hbm.at[j, :, pl.ds(half, 256)] if j < 3 else out_hbm.at[pl.ds(half, 256)]
            outs.append(pltpu.make_async_copy(res_ref.at[j], dst, sem.at[j]))
            outs[-1].start()
        for copy in outs:
            copy.wait()

    vm = pl.BlockSpec(memory_space=pltpu.VMEM)
    hbm = pl.BlockSpec(memory_space=pl.ANY)
    return call(
        kernel,
        in_specs=[pl.BlockSpec(memory_space=pltpu.SMEM), vm, hbm, hbm],
        out_specs=[hbm, hbm],
        out_shape=[jax.ShapeDtypeStruct((3, 256, 512), F32), jax.ShapeDtypeStruct((512, 256), F32)],
        scratch_shapes=[pltpu.VMEM((4, 256, 256), F32), pltpu.SemaphoreType.DMA((4,))],
        input_output_aliases={2: 0, 3: 1},
        bytes_accessed=3 * MIB,
        vmem=8,
        name="fill_halves",
    )(place, sent, in_hbm(in_grad), in_hbm(out_grad))


def chip_hop(x_flip, z_step):
    pairs = []
    for i in range(16):
        x, z, core = i // 8, i // 2 % 4, i % 2
        pairs.append((i, ((x ^ x_flip) * 4 + (z + z_step) % 4) * 2 + core))
    return pairs


def swap_cores(value):
    return lax.ppermute(value, "ctx", [(i, i ^ 1) for i in range(16)])


def swap(pieces, axis, groups=None):
    return lax.all_to_all(pieces, axis, 0, 0, axis_index_groups=groups, tiled=True)


HOPS = ((0, 0), (0, 1), (0, 3), (1, 0), (0, 2), (1, 1), (1, 3), (1, 2))


def hop(value, x_flip, z_step):
    return lax.ppermute(value, "ctx", chip_hop(x_flip, z_step))


def after(value, *others):
    return lax.optimization_barrier((value,) + others)[0]


def hop_y(value, step):
    return lax.ppermute(value, "mp", [(i, i // 4 * 4 + (i % 4 + step) % 4) for i in range(8)])


def on_device(tokens, out_grad, in_weight, out_weight, filters):
    position = lax.axis_index("ctx")
    core, x, z = position & 1, position >> 3, (position >> 1) & 3
    y = lax.axis_index("mp") & 3
    place = [((x ^ f) << 2) + ((z - s) & 3) for f, s in HOPS] + [core] + [(y - s) & 3 for s in range(4)]
    place = jnp.stack(place).astype(jnp.int32)
    weight = jnp.transpose(in_weight, (1, 0, 2))
    columns = split_columns(y.astype(jnp.int32)[None], tokens, out_grad)
    signals = project(after(tokens, columns), out_grad, weight, out_weight, filters)
    columns = swap(columns, "ctx", [list(range(c, 16, 2)) for c in range(2)])
    signals, columns = lax.optimization_barrier((signals, columns))
    signals = swap(signals.reshape(16, 5 * BLOCK, SEQ_DEV), "ctx")
    columns = [columns] + [hop_y(columns, s) for s in (1, 2, 3)]
    flip = jnp.asarray(np.eye(256)[::-1].astype(ml_dtypes.bfloat16))
    block, pieces = convolve(
        signals, jnp.asarray(cosine_matrix()), jnp.asarray(frequency_rows()), flip
    )
    up, down, flipped = hop(block, 0, 1), hop(block, 0, 3), hop(block, 1, 0)
    pieces = swap(pieces, "ctx")
    up, down, flipped, pieces, *columns = lax.optimization_barrier((up, down, flipped, pieces, *columns))
    across, two = pair(up, down, block, flipped)
    across, two = hop(across, 1, 0), hop(two, 0, 2)
    partial, filter_grad = input_partial(pieces, weight)
    parts = swap(partial, "mp")
    parts, across, two = lax.optimization_barrier((parts, across, two))
    columns += [swap_cores(value) for value in columns]
    input_grad = sum_partials(parts)
    blocks = [(block, 0), (up, 0), (down, 0), (flipped, 0), (two, 0), (across, 0), (across, 128), (two, 128)]
    in_grad, out_weight_grad, send = weight_gradients(after(place, input_grad), columns, blocks)
    in_grad, out_weight_grad = fill_halves(place, swap_cores(send), in_grad, out_weight_grad)
    return (input_grad, jnp.transpose(in_grad, (1, 0, 2)), out_weight_grad, filter_grad)


def solution(mesh):
    in_specs = (P("ctx", None), P("ctx", None), P(None, None, "mp"), P("mp", None), P("ctx", "mp"))
    out_specs = (P("ctx", "mp"), P("ctx", None, "mp"), P("mp", "ctx"), P("ctx", "mp"))
    return jax.shard_map(
        on_device, mesh=mesh, in_specs=in_specs, out_specs=out_specs, check_vma=False
    )
```

time: 160 us -> 129 us (0.81)
  blocking collectives: 53.4 us -> 0 us
  waiting for transfers between devices: 17.8 us -> 43.9 us
  local copies, waits for them, and re-layouts: 12.7 us -> 1.05 us
  starting transfers between devices: 38.2 us -> 45.4 us
    all_to_all x2 -> x0, blocking collectives: 53.4 us -> none  [swap(): return lax.all_to_all(pieces, axis, 0, 0, tiled=True)]
    all_to_all x2 -> x4, waiting for transfers between devices: 6.47 us -> 32.4 us  [swap(): lax.all_to_all(pieces, axis, 0, 0, axis_index_groups=groups, tiled=True)]
    all_to_all x2 -> x4, starting transfers between devices: 8.76 us -> 28.8 us  [swap(): lax.all_to_all(pieces, axis, 0, 0, axis_index_groups=groups, tiled=True)]
    ppermute x7 -> x8, starting transfers between devices: 27.7 us -> 10.5 us  [the longest x5 6.71 us: hop(): return lax.ppermute(value, 'ctx', chip_hop(x_flip, z_step))]
    unnamed x22 -> x12, local copies, waits for them, and re-layouts: 12.6 us -> 0.97 us
    ppermute x2 -> x5, starting transfers between devices: 1.72 us -> 6.13 us  [swap_cores(): return lax.ppermute(value, 'ctx', [(i, i ^ 1) for i in range(16)])]
    pallas_call x5, Pallas kernels: 25.5 us -> 27.5 us  [the longest x1 8.3 us: project(): call(kernel, in_specs=[hbm] * 5, out_specs=vm, out_shape=jax.ShapeDtypeSt...]
    ppermute x7 -> x8, waiting for transfers between devices: 11.3 us -> 9.93 us  [the longest x5 7.12 us: hop(): return lax.ppermute(value, 'ctx', chip_hop(x_flip, z_step))]
  transfers between devices with their start and end apart: 11 -> 17, of which waited for: 4 -> 7; matrix products, arithmetic and copies ran while one was open for 0% -> 0% of each run, Pallas kernels for 20% -> 19%
where the time goes in v1:
time: 129 us
  starting transfers between devices  45.4 us (35%)
  waiting for transfers between devices  43.9 us (34%)
  Pallas kernels  37.3 us (29%)
    all_to_all x4, waiting for transfers between devices, swap(): lax.all_to_all(pieces, axis, 0, 0, axis_index_groups=groups, tiled=True)  32.4 us
    all_to_all x4, starting transfers between devices, swap(): lax.all_to_all(pieces, axis, 0, 0, axis_index_groups=groups, tiled=True)  28.8 us
    pallas_call x1, Pallas kernels, project(): call(kernel, in_specs=[hbm] * 5, out_specs=vm, out_shape=jax.ShapeDtypeSt...  8.3 us
    pallas_call x1, Pallas kernels, input_partial(): call(kernel, in_specs=[vm, pl.BlockSpec(memory_space=pl.ANY)], out_specs=...  7.78 us
    pallas_call x1, Pallas kernels, convolve(): call(kernel, in_specs=[vm, pl.BlockSpec(memory_space=pl.ANY), vm, vm], ou...  7.46 us
    ppermute x5, waiting for transfers between devices, hop(): return lax.ppermute(value, 'ctx', chip_hop(x_flip, z_step))  7.12 us
    pallas_call x1, Pallas kernels, weight_gradients(): call(kernel, in_specs=[pl.BlockSpec(memory_space=pltpu.SMEM)] + [hbm] * 1...  6.9 us
    ppermute x5, starting transfers between devices, hop(): return lax.ppermute(value, 'ctx', chip_hop(x_flip, z_step))  6.71 us
  transfers between devices with their start and end apart: 17, of which 7 were waited for; matrix products, arithmetic and copies ran while one was open for 0% of the time, Pallas kernels for 19%

profile of v1, /device:TPU:1, one launch (start us, length us, event | category | flops | bytes accessed | tf_op | source)
XLA Modules:
  0.0 128.6 jit_solution(6101228179119746599)
XLA Ops:
  0.6 1.9 %split_columns.1 = bf16[8,2,128,128]{3,2,1,0:T(8,128)(2,1)} custom-call(s32[1]{0:T(128)} %bitcast.y_ref, bf16[128,4096]{1,0:T(8,128)(2,1)} %t_hbm.2, bf16[128,4096]{1,0:T(8,128)(2,1)} %g_hbm.3), custom_call_target="tpu_custom_call" | custom-call | bytes 1048576 | tf_op jit(solution)/shard_map/split_columns/pallas_call | solution.py:73
  2.6 8.3 %all-to-all-start = ((bf16[8,2,128,128]{3,2,1,0:T(8,128)(2,1)}), bf16[8,2,128,128]{3,2,1,0:T(8,128)(2,1)S(1)}, u32[]{:S(2)}, u32[]{:S(2)}) async-start(bf16[8,2,128,128]{3,2,1,0:T(8,128)(2,1)} %split_columns.1), calls=%async_computation | async-start | bytes 1048576 | tf_op jit(solution)/shard_map/all_to_all | solution.py:456
  10.9 0.0 copy-start.2
  10.9 8.3 %project.1 = bf16[8,2,160,128]{3,2,1,0:T(8,128)(2,1)} custom-call(bf16[128,4096]{1,0:T(8,128)(2,1)} %t_hbm.2, bf16[128,4096]{1,0:T(8,128)(2,1)} %g_hbm.3, f32[128,512]{1,0:T(8,128)} %f_hbm.1, bf16[3,4096,512]{2,1,0:T(8,128)(2,1)} %bitcast.17, bf16[512,4096]{1,0:T(8,128)(2,1)} %ow_hbm.1), custom_call_target="tpu_custom_call" | custom-call | flops 2147483648 | bytes 19922944 | tf_op jit(solution)/shard_map/project/pallas_call | solution.py:129
  19.3 0.6 all-to-all-done.refs_0_
  19.9 7.5 %all-to-all-start.1 = ((bf16[16,160,128]{2,1,0:T(8,128)(2,1)}), bf16[16,160,128]{2,1,0:T(8,128)(2,1)S(1)}, u32[]{:S(2)}, u32[]{:S(2)}) async-start(bf16[16,160,128]{2,1,0:T(8,128)(2,1)} %bitcast.2), calls=%async_computation.1 | async-start | bytes 1310720 | tf_op jit(solution)/shard_map/all_to_all | solution.py:456
  27.4 2.7 %collective-permute-start.5 = (bf16[8,2,128,128]{3,2,1,0:T(8,128)(2,1)S(1)}, bf16[8,2,128,128]{3,2,1,0:T(8,128)(2,1)}, u32[]{:S(2)}, u32[]{:S(2)}) collective-permute-start(bf16[8,2,128,128]{3,2,1,0:T(8,128)(2,1)S(1)} %all-to-all-done.refs_0_), channel_id=1, source_target_pairs={{0,3},{1,0},{2,1},{3,2},{4,7},{5,4},{6,5},{7,6},{8,11},{9,8},{10,9... | collective-permute-start | bytes 1572872 | tf_op jit(solution)/shard_map/ppermute | solution.py:471
  30.2 0.3 collective-permute-start.4
  30.5 0.7 collective-permute-start.3
  31.2 8.9 %all-to-all-done.1.r_ref = bf16[16,160,128]{2,1,0:T(8,128)(2,1)S(1)} async-done(((bf16[16,160,128]{2,1,0:T(8,128)(2,1)}), bf16[16,160,128]{2,1,0:T(8,128)(2,1)S(1)}, u32[]{:S(2)}, u32[]{:S(2)}) %all-to-all-start.1) | async-done | bytes 655392 | tf_op jit(solution)/shard_map/all_to_all | solution.py:456
  40.1 0.0 copy-done.1
  40.1 7.5 %convolve.1 = (bf16[128,2048]{1,0:T(8,128)(2,1)S(1)}, bf16[16,128,128]{2,1,0:T(8,128)(2,1)}) custom-call(bf16[16,160,128]{2,1,0:T(8,128)(2,1)S(1)} %all-to-all-done.1.r_ref, bf16[2048,2048]{1,0:T(8,128)(2,1)} %constant.31.clone.m_hbm, f32[8,2048]{1,0:T(8,128)S(1)} %copy-done.2, bf16[256,256]{1,0:T(8,128)(2,1)S(1)} %copy-done.1), custom_call_target="tpu_custom_call" | custom-call | flops 3221225472 | bytes 12582912 | tf_op jit(solution)/shard_map/convolve/pallas_call | solution.py:227
  47.6 0.0 copy-start
  47.6 0.8 collective-permute-start.2
  48.5 1.2 collective-permute-start.1
  49.6 2.8 %collective-permute-done.5.refs_3_ = bf16[8,2,128,128]{3,2,1,0:T(8,128)(2,1)} collective-permute-done((bf16[8,2,128,128]{3,2,1,0:T(8,128)(2,1)S(1)}, bf16[8,2,128,128]{3,2,1,0:T(8,128)(2,1)}, u32[]{:S(2)}, u32[]{:S(2)}) %collective-permute-start.5) | collective-permute-done | bytes 524320 | tf_op jit(solution)/shard_map/ppermute | solution.py:471
  52.4 1.2 collective-permute-start
  53.6 8.0 %all-to-all-start.2 = ((bf16[16,128,128]{2,1,0:T(8,128)(2,1)}), bf16[16,128,128]{2,1,0:T(8,128)(2,1)S(1)}, u32[]{:S(2)}, u32[]{:S(2)}) async-start(bf16[16,128,128]{2,1,0:T(8,128)(2,1)} %get-tuple-element.33), calls=%async_computation.2 | async-start | bytes 1048576 | tf_op jit(solution)/shard_map/all_to_all | solution.py:456
  61.6 0.0 collective-permute-done.4.refs_2_
  61.6 0.0 collective-permute-done.3.refs_1_
  61.6 11.7 %all-to-all-done.2.r_ref = bf16[16,128,128]{2,1,0:T(8,128)(2,1)S(1)} async-done(((bf16[16,128,128]{2,1,0:T(8,128)(2,1)}), bf16[16,128,128]{2,1,0:T(8,128)(2,1)S(1)}, u32[]{:S(2)}, u32[]{:S(2)}) %all-to-all-start.2) | async-done | bytes 524320 | tf_op jit(solution)/shard_map/all_to_all | solution.py:456
  73.3 0.0 collective-permute-done.2.d.refs_11_
  73.3 0.0 collective-permute-done.1.b.refs_10_
  73.3 0.8 copy-done.5
  74.2 0.0 collective-permute-done.a.refs_9_
  74.2 0.1 copy-done.4
  74.3 2.5 %pair.1 = (bf16[256,2048]{1,0:T(8,128)(2,1)}, bf16[256,2048]{1,0:T(8,128)(2,1)S(1)}) custom-call(bf16[128,2048]{1,0:T(8,128)(2,1)} %collective-permute-done.a.refs_9_, bf16[128,2048]{1,0:T(8,128)(2,1)} %copy-done.5, bf16[128,2048]{1,0:T(8,128)(2,1)} %copy-done, bf16[128,2048]{1,0:T(8,128)(2,1)} %copy-done.4), custom_call_target="tpu_custom_call" | custom-call | bytes 4194304 | tf_op jit(solution)/shard_map/pair/pallas_call | solution.py:326
  76.8 2.9 %collective-permute-start.6 = (bf16[256,2048]{1,0:T(8,128)(2,1)}, bf16[256,2048]{1,0:T(8,128)(2,1)}, u32[]{:S(2)}, u32[]{:S(2)}) collective-permute-start(bf16[256,2048]{1,0:T(8,128)(2,1)} %get-tuple-element.40), channel_id=1, source_target_pairs={{0,64},{8,72},{16,80},{24,88},{32,96},{40,104},{48,112},{56,120},{... | collective-permute-start | bytes 3145736 | tf_op jit(solution)/shard_map/ppermute | solution.py:463
  79.7 0.6 collective-permute-start.7
  80.4 7.8 %input_partial.1 = (bf16[8,128,512]{2,1,0:T(8,128)(2,1)}, f32[128,512]{1,0:T(8,128)}) custom-call(bf16[16,128,128]{2,1,0:T(8,128)(2,1)S(1)} %all-to-all-done.2.r_ref, bf16[3,4096,512]{2,1,0:T(8,128)(2,1)} %bitcast.18), custom_call_target="tpu_custom_call" | custom-call | flops 1610612736 | bytes 14680064 | tf_op jit(solution)/shard_map/input_partial/pallas_call | solution.py:277
  88.1 5.0 %all-to-all-start.3 = ((bf16[8,128,512]{2,1,0:T(8,128)(2,1)}), bf16[8,128,512]{2,1,0:T(8,128)(2,1)S(1)}, u32[]{:S(2)}, u32[]{:S(2)}) async-start(bf16[8,128,512]{2,1,0:T(8,128)(2,1)} %get-tuple-element.36), calls=%async_computation.3 | async-start | bytes 2097152 | tf_op jit(solution)/shard_map/all_to_all | solution.py:456
  93.1 1.9 %collective-permute-start.8 = (bf16[8,2,128,128]{3,2,1,0:T(8,128)(2,1)S(1)}, bf16[8,2,128,128]{3,2,1,0:T(8,128)(2,1)}, u32[]{:S(2)}, u32[]{:S(2)}) collective-permute-start(bf16[8,2,128,128]{3,2,1,0:T(8,128)(2,1)S(1)} %all-to-all-done.refs_0_), channel_id=1, source_target_pairs={{0,8},{8,0},{16,24},{24,16},{32,40},{40,32},{48,56},{56,48},{64,72... | collective-permute-start | bytes 1572872 | tf_op jit(solution)/shard_map/ppermute | solution.py:452
  95.0 0.1 collective-permute-start.9
  95.1 0.4 collective-permute-start.10
  95.6 7.1 %collective-permute-done.6.refs_13_.refs_14_ = bf16[256,2048]{1,0:T(8,128)(2,1)} collective-permute-done((bf16[256,2048]{1,0:T(8,128)(2,1)}, bf16[256,2048]{1,0:T(8,128)(2,1)}, u32[]{:S(2)}, u32[]{:S(2)}) %collective-permute-start.6) | collective-permute-done | bytes 1048608 | tf_op jit(solution)/shard_map/ppermute | solution.py:463
  102.7 2.9 %collective-permute-start.11 = (bf16[8,2,128,128]{3,2,1,0:T(8,128)(2,1)}, bf16[8,2,128,128]{3,2,1,0:T(8,128)(2,1)}, u32[]{:S(2)}, u32[]{:S(2)}) collective-permute-start(bf16[8,2,128,128]{3,2,1,0:T(8,128)(2,1)} %collective-permute-done.5.refs_3_), channel_id=1, source_target_pairs={{0,8},{8,0},{16,24},{24,16},{32,40},{40,32},{48,56},{56,48},{64,72... | collective-permute-start | bytes 1572872 | tf_op jit(solution)/shard_map/ppermute | solution.py:452
  105.5 0.1 stack.55.place_ref
  105.6 11.1 %all-to-all-done.3.p_ref = bf16[8,128,512]{2,1,0:T(8,128)(2,1)S(1)} async-done(((bf16[8,128,512]{2,1,0:T(8,128)(2,1)}), bf16[8,128,512]{2,1,0:T(8,128)(2,1)S(1)}, u32[]{:S(2)}, u32[]{:S(2)}) %all-to-all-start.3) | async-done | bytes 1048608 | tf_op jit(solution)/shard_map/all_to_all | solution.py:456
  116.8 0.0 collective-permute-done.7.refs_12_.refs_15_
  116.8 0.8 sum_partials.1
  117.6 0.0 collective-permute-done.8.refs_4_
  117.6 0.0 collective-permute-done.9.refs_5_
  117.6 0.0 collective-permute-done.10.refs_6_
  117.6 0.0 collective-permute-done.11.refs_7_
  117.6 6.9 %weight_gradients.1 = (f32[3,256,512]{2,1,0:T(8,128)}, f32[512,256]{1,0:T(8,128)}, bf16[1024,256]{1,0:T(8,128)(2,1)S(1)}) custom-call(s32[13]{0:T(128)S(1)} %stack.55.place_ref, bf16[8,2,128,128]{3,2,1,0:T(8,128)(2,1)} %copy-done.3, bf16[8,2,128,128]{3,2,1,0:T(8,128)(2,1)} %collective-permute-done.3.refs_1_, ...), custom_call_target="tpu_custom_call" | custom-call | flops 2147483648 | bytes 10485760 | tf_op jit(solution)/shard_map/weight_gradients/pallas_call | solution.py:392
  124.5 0.8 collective-permute-start.12
  125.3 1.5 %collective-permute-done.12.s_ref = bf16[1024,256]{1,0:T(8,128)(2,1)S(1)} collective-permute-done((bf16[1024,256]{1,0:T(8,128)(2,1)S(1)}, bf16[1024,256]{1,0:T(8,128)(2,1)S(1)}, u32[]{:S(2)}, u32[]{:S(2)}) %collective-permute-start.12) | collective-permute-done | bytes 524320 | tf_op jit(solution)/shard_map/ppermute | solution.py:452
  126.9 1.6 %fill_halves.1 = (f32[3,256,512]{2,1,0:T(8,128)}, f32[512,256]{1,0:T(8,128)}) custom-call(s32[13]{0:T(128)S(1)} %stack.55.place_ref, bf16[1024,256]{1,0:T(8,128)(2,1)S(1)} %collective-permute-done.12.s_ref, f32[3,256,512]{2,1,0:T(8,128)} %get-tuple-element.51.in_old, f32[512,256]{1,0:T(8,128)} %get-tuple-element.52.out_old), custom_call_target="tpu_custom_call", output_to_operand_aliasing={{0}: (2, {}), {1}: (3, {})} | custom-call | bytes 3145728 | tf_op jit(solution)/shard_map/fill_halves/pallas_call | solution.py:430
  (7 shorter events, 0.0 us)
Async XLA Ops:
  2.6 17.3 %all-to-all-start = ((bf16[8,2,128,128]{3,2,1,0:T(8,128)(2,1)}), bf16[8,2,128,128]{3,2,1,0:T(8,128)(2,1)S(1)}, u32[]{:S(2)}, u32[]{:S(2)}) async-start(bf16[8,2,128,128]{3,2,1,0:T(8,128)(2,1)} %split_columns.1), calls=%async_computation | async-start | bytes 1048576 | tf_op jit(solution)/shard_map/all_to_all | solution.py:456
  10.9 29.2 %copy-start.1 = (bf16[256,256]{1,0:T(8,128)(2,1)S(1)}, bf16[256,256]{1,0:T(8,128)(2,1)}, u32[]{:S(2)}) copy-start(bf16[256,256]{1,0:T(8,128)(2,1)} %constant.30.clone.j_ref) | copy-start | bytes 393220
  10.9 29.2 %copy-start.2 = (f32[8,2048]{1,0:T(8,128)S(1)}, f32[8,2048]{1,0:T(8,128)}, u32[]{:S(2)}) copy-start(f32[8,2048]{1,0:T(8,128)} %constant.32.clone.w_ref) | copy-start | bytes 196612
  19.9 73.2 %copy-start.3 = (bf16[8,2,128,128]{3,2,1,0:T(8,128)(2,1)}, bf16[8,2,128,128]{3,2,1,0:T(8,128)(2,1)S(1)}, u32[]{:S(2)}) copy-start(bf16[8,2,128,128]{3,2,1,0:T(8,128)(2,1)S(1)} %all-to-all-done.refs_0_) | copy-start | bytes 1572868
  19.9 20.2 %all-to-all-start.1 = ((bf16[16,160,128]{2,1,0:T(8,128)(2,1)}), bf16[16,160,128]{2,1,0:T(8,128)(2,1)S(1)}, u32[]{:S(2)}, u32[]{:S(2)}) async-start(bf16[16,160,128]{2,1,0:T(8,128)(2,1)} %bitcast.2), calls=%async_computation.1 | async-start | bytes 1310720 | tf_op jit(solution)/shard_map/all_to_all | solution.py:456
  27.4 25.0 %collective-permute-start.5 = (bf16[8,2,128,128]{3,2,1,0:T(8,128)(2,1)S(1)}, bf16[8,2,128,128]{3,2,1,0:T(8,128)(2,1)}, u32[]{:S(2)}, u32[]{:S(2)}) collective-permute-start(bf16[8,2,128,128]{3,2,1,0:T(8,128)(2,1)S(1)} %all-to-all-done.refs_0_), channel_id=1, source_target_pairs={{0,3},{1,0},{2,1},{3,2},{4,7},{5,4},{6,5},{7,6},{8,11},{9,8},{10,9... | collective-permute-start | bytes 1572872 | tf_op jit(solution)/shard_map/ppermute | solution.py:471
  30.2 31.4 %collective-permute-start.4 = (bf16[8,2,128,128]{3,2,1,0:T(8,128)(2,1)S(1)}, bf16[8,2,128,128]{3,2,1,0:T(8,128)(2,1)}, u32[]{:S(2)}, u32[]{:S(2)}) collective-permute-start(bf16[8,2,128,128]{3,2,1,0:T(8,128)(2,1)S(1)} %all-to-all-done.refs_0_), channel_id=1, source_target_pairs={{0,2},{1,3},{2,0},{3,1},{4,6},{5,7},{6,4},{7,5},{8,10},{9,11},{10,... | collective-permute-start | bytes 1572872 | tf_op jit(solution)/shard_map/ppermute | solution.py:471
  30.5 31.1 %collective-permute-start.3 = (bf16[8,2,128,128]{3,2,1,0:T(8,128)(2,1)S(1)}, bf16[8,2,128,128]{3,2,1,0:T(8,128)(2,1)}, u32[]{:S(2)}, u32[]{:S(2)}) collective-permute-start(bf16[8,2,128,128]{3,2,1,0:T(8,128)(2,1)S(1)} %all-to-all-done.refs_0_), channel_id=1, source_target_pairs={{0,1},{1,2},{2,3},{3,0},{4,5},{5,6},{6,7},{7,4},{8,9},{9,10},{10,1... | collective-permute-start | bytes 1572872 | tf_op jit(solution)/shard_map/ppermute | solution.py:471
  47.6 26.6 %copy-start = (bf16[128,2048]{1,0:T(8,128)(2,1)}, bf16[128,2048]{1,0:T(8,128)(2,1)S(1)}, u32[]{:S(2)}) copy-start(bf16[128,2048]{1,0:T(8,128)(2,1)S(1)} %get-tuple-element.32.c.refs_8_) | copy-start | bytes 1572868
  47.6 25.7 %collective-permute-start.2 = (bf16[128,2048]{1,0:T(8,128)(2,1)S(1)}, bf16[128,2048]{1,0:T(8,128)(2,1)S(1)}, u32[]{:S(2)}, u32[]{:S(2)}) collective-permute-start(bf16[128,2048]{1,0:T(8,128)(2,1)S(1)} %get-tuple-element.32.c.refs_8_), channel_id=1, source_target_pairs={{0,64},{8,72},{16,80},{24,88},{32,96},{40,104},{48,112},{56,120},{... | collective-permute-start | bytes 1572872 | tf_op jit(solution)/shard_map/ppermute | solution.py:463
  48.5 24.8 %collective-permute-start.1 = (bf16[128,2048]{1,0:T(8,128)(2,1)S(1)}, bf16[128,2048]{1,0:T(8,128)(2,1)S(1)}, u32[]{:S(2)}, u32[]{:S(2)}) collective-permute-start(bf16[128,2048]{1,0:T(8,128)(2,1)S(1)} %get-tuple-element.32.c.refs_8_), channel_id=1, source_target_pairs={{0,48},{8,56},{16,0},{24,8},{32,16},{40,24},{48,32},{56,40},{64,11... | collective-permute-start | bytes 1572872 | tf_op jit(solution)/shard_map/ppermute | solution.py:463
  52.4 21.7 %collective-permute-start = (bf16[128,2048]{1,0:T(8,128)(2,1)S(1)}, bf16[128,2048]{1,0:T(8,128)(2,1)}, u32[]{:S(2)}, u32[]{:S(2)}) collective-permute-start(bf16[128,2048]{1,0:T(8,128)(2,1)S(1)} %get-tuple-element.32.c.refs_8_), channel_id=1, source_target_pairs={{0,16},{8,24},{16,32},{24,40},{32,48},{40,56},{48,0},{56,8},{64,80... | collective-permute-start | bytes 1572872 | tf_op jit(solution)/shard_map/ppermute | solution.py:463
  53.6 19.7 %all-to-all-start.2 = ((bf16[16,128,128]{2,1,0:T(8,128)(2,1)}), bf16[16,128,128]{2,1,0:T(8,128)(2,1)S(1)}, u32[]{:S(2)}, u32[]{:S(2)}) async-start(bf16[16,128,128]{2,1,0:T(8,128)(2,1)} %get-tuple-element.33), calls=%async_computation.2 | async-start | bytes 1048576 | tf_op jit(solution)/shard_map/all_to_all | solution.py:456
  73.3 1.0 copy-start.4
  73.3 0.9 copy-start.5
  76.8 25.8 %collective-permute-start.6 = (bf16[256,2048]{1,0:T(8,128)(2,1)}, bf16[256,2048]{1,0:T(8,128)(2,1)}, u32[]{:S(2)}, u32[]{:S(2)}) collective-permute-start(bf16[256,2048]{1,0:T(8,128)(2,1)} %get-tuple-element.40), channel_id=1, source_target_pairs={{0,64},{8,72},{16,80},{24,88},{32,96},{40,104},{48,112},{56,120},{... | collective-permute-start | bytes 3145736 | tf_op jit(solution)/shard_map/ppermute | solution.py:463
  79.7 37.0 %collective-permute-start.7 = (bf16[256,2048]{1,0:T(8,128)(2,1)S(1)}, bf16[256,2048]{1,0:T(8,128)(2,1)}, u32[]{:S(2)}, u32[]{:S(2)}) collective-permute-start(bf16[256,2048]{1,0:T(8,128)(2,1)S(1)} %get-tuple-element.41), channel_id=1, source_target_pairs={{0,32},{8,40},{16,48},{24,56},{32,0},{40,8},{48,16},{56,24},{64,96... | collective-permute-start | bytes 3145736 | tf_op jit(solution)/shard_map/ppermute | solution.py:463
  88.1 28.6 %all-to-all-start.3 = ((bf16[8,128,512]{2,1,0:T(8,128)(2,1)}), bf16[8,128,512]{2,1,0:T(8,128)(2,1)S(1)}, u32[]{:S(2)}, u32[]{:S(2)}) async-start(bf16[8,128,512]{2,1,0:T(8,128)(2,1)} %get-tuple-element.36), calls=%async_computation.3 | async-start | bytes 2097152 | tf_op jit(solution)/shard_map/all_to_all | solution.py:456
  93.1 24.4 %collective-permute-start.8 = (bf16[8,2,128,128]{3,2,1,0:T(8,128)(2,1)S(1)}, bf16[8,2,128,128]{3,2,1,0:T(8,128)(2,1)}, u32[]{:S(2)}, u32[]{:S(2)}) collective-permute-start(bf16[8,2,128,128]{3,2,1,0:T(8,128)(2,1)S(1)} %all-to-all-done.refs_0_), channel_id=1, source_target_pairs={{0,8},{8,0},{16,24},{24,16},{32,40},{40,32},{48,56},{56,48},{64,72... | collective-permute-start | bytes 1572872 | tf_op jit(solution)/shard_map/ppermute | solution.py:452
  95.0 22.5 %collective-permute-start.9 = (bf16[8,2,128,128]{3,2,1,0:T(8,128)(2,1)}, bf16[8,2,128,128]{3,2,1,0:T(8,128)(2,1)}, u32[]{:S(2)}, u32[]{:S(2)}) collective-permute-start(bf16[8,2,128,128]{3,2,1,0:T(8,128)(2,1)} %collective-permute-done.3.refs_1_), channel_id=1, source_target_pairs={{0,8},{8,0},{16,24},{24,16},{32,40},{40,32},{48,56},{56,48},{64,72... | collective-permute-start | bytes 1572872 | tf_op jit(solution)/shard_map/ppermute | solution.py:452
  95.1 22.4 %collective-permute-start.10 = (bf16[8,2,128,128]{3,2,1,0:T(8,128)(2,1)}, bf16[8,2,128,128]{3,2,1,0:T(8,128)(2,1)}, u32[]{:S(2)}, u32[]{:S(2)}) collective-permute-start(bf16[8,2,128,128]{3,2,1,0:T(8,128)(2,1)} %collective-permute-done.4.refs_2_), channel_id=1, source_target_pairs={{0,8},{8,0},{16,24},{24,16},{32,40},{40,32},{48,56},{56,48},{64,72... | collective-permute-start | bytes 1572872 | tf_op jit(solution)/shard_map/ppermute | solution.py:452
  102.7 14.9 %collective-permute-start.11 = (bf16[8,2,128,128]{3,2,1,0:T(8,128)(2,1)}, bf16[8,2,128,128]{3,2,1,0:T(8,128)(2,1)}, u32[]{:S(2)}, u32[]{:S(2)}) collective-permute-start(bf16[8,2,128,128]{3,2,1,0:T(8,128)(2,1)} %collective-permute-done.5.refs_3_), channel_id=1, source_target_pairs={{0,8},{8,0},{16,24},{24,16},{32,40},{40,32},{48,56},{56,48},{64,72... | collective-permute-start | bytes 1572872 | tf_op jit(solution)/shard_map/ppermute | solution.py:452
  124.5 2.4 %collective-permute-start.12 = (bf16[1024,256]{1,0:T(8,128)(2,1)S(1)}, bf16[1024,256]{1,0:T(8,128)(2,1)S(1)}, u32[]{:S(2)}, u32[]{:S(2)}) collective-permute-start(bf16[1024,256]{1,0:T(8,128)(2,1)S(1)} %get-tuple-element.50), channel_id=1, source_target_pairs={{0,8},{8,0},{16,24},{24,16},{32,40},{40,32},{48,56},{56,48},{64,72... | collective-permute-start | bytes 1572872 | tf_op jit(solution)/shard_map/ppermute | solution.py:452

commit v2 on v1

--- a/solution.py
+++ b/solution.py
@@ -57,37 +57,12 @@
     )
 
 
-def split_columns(quarter, tokens, out_grad):
-    def kernel(y_ref, t_hbm, g_hbm, o_ref, sem):
-        copies = []
-        for chip in range(8):
-            lanes = pl.ds(pl.multiple_of(chip * 512 + y_ref[0] * 128, 128), 128)
-            copies.append(pltpu.make_async_copy(t_hbm.at[:, lanes], o_ref.at[chip, 0], sem.at[chip, 0]))
-            copies.append(pltpu.make_async_copy(g_hbm.at[:, lanes], o_ref.at[chip, 1], sem.at[chip, 1]))
-        for copy in copies:
-            copy.start()
-        for copy in copies:
-            copy.wait()
-
-    hbm = pl.BlockSpec(memory_space=pl.ANY)
-    return call(
-        kernel,
-        in_specs=[pl.BlockSpec(memory_space=pltpu.SMEM), hbm, hbm],
-        out_specs=pl.BlockSpec(memory_space=pltpu.VMEM),
-        out_shape=jax.ShapeDtypeStruct((8, 2, SEQ_DEV, 128), BF16),
-        scratch_shapes=[pltpu.SemaphoreType.DMA((8, 2))],
-        bytes_accessed=MIB,
-        vmem=4,
-        name="split_columns",
-    )(quarter, in_hbm(tokens), in_hbm(out_grad))
-
-
-def project(tokens, out_grad, weight, out_weight, filters):
+def project(quarter, tokens, out_grad, weight, out_weight, filters):
     depth = 2048
     steps = 4096 // depth
     gate = 256
 
-    def kernel(t_hbm, g_hbm, f_hbm, w_hbm, ow_hbm, o_ref, f_ref, t_ref, g_ref, w_ref, ow_ref, sem):
+    def kernel(y_ref, t_hbm, g_hbm, f_hbm, w_hbm, ow_hbm, o_ref, f_ref, t_ref, g_ref, w_ref, ow_ref, sem):
         def fetch(src, dst, at):
             return pltpu.make_async_copy(src, dst, sem.at[at])
 
@@ -115,12 +90,19 @@
             put(i * gate, 3, dot(ow_ref[i * gate : (i + 1) * gate], g_ref[...], NT))
         for c in range(2):
             put(c * 256, 4, f_ref[:, c * 256 : (c + 1) * 256].T)
+        for chip in range(8):
+            lanes = pl.ds(pl.multiple_of(chip * 512 + y_ref[0] * 128, 128), 128)
+            o_ref[chip, 1, 5 * BLOCK :, :] = g_ref[:, lanes]
         for j in range(3):
             total = None
             for k in range(steps):
                 stream.wait(first + j * steps + k)
                 part = dot(t_ref[:, k * depth : (k + 1) * depth], w_ref[j, k * depth : (k + 1) * depth])
                 total = part if total is None else total + part
+            if j == 0:
+                for chip in range(8):
+                    lanes = pl.ds(pl.multiple_of(chip * 512 + y_ref[0] * 128, 128), 128)
+                    o_ref[chip, 0, 5 * BLOCK :, :] = t_ref[:, lanes]
             for c in range(2):
                 put(c * 256, j, total[:, c * 256 : (c + 1) * 256].T)
 
@@ -128,9 +110,9 @@
     hbm = pl.BlockSpec(memory_space=pl.ANY)
     return call(
         kernel,
-        in_specs=[hbm] * 5,
+        in_specs=[pl.BlockSpec(memory_space=pltpu.SMEM)] + [hbm] * 5,
         out_specs=vm,
-        out_shape=jax.ShapeDtypeStruct((8, 2, 5 * BLOCK, SEQ_DEV), BF16),
+        out_shape=jax.ShapeDtypeStruct((8, 2, 5 * BLOCK + 128, SEQ_DEV), BF16),
         scratch_shapes=[
             pltpu.VMEM((SEQ_DEV, 512), F32),
             pltpu.VMEM((SEQ_DEV, 4096), BF16),
@@ -143,7 +125,7 @@
         bytes_accessed=19 * MIB,
         vmem=28,
         name="project",
-    )(in_hbm(tokens), in_hbm(out_grad), in_hbm(filters), in_hbm(weight), in_hbm(out_weight))
+    )(quarter, in_hbm(tokens), in_hbm(out_grad), in_hbm(filters), in_hbm(weight), in_hbm(out_weight))
 
 
 def cosine_matrix():
@@ -164,12 +146,13 @@
     chunk = 512
     n_chunks = SEQ // chunk
 
-    def kernel(r_ref, m_hbm, w_ref, j_ref, b_ref, o_ref, m_ref, x_ref, y_ref, sem):
+    def kernel(r_ref, m_hbm, w_ref, j_ref, b_ref, o_ref, c_ref, m_ref, x_ref, y_ref, sem):
         chunks = [pl.ds(n * chunk, chunk) for n in range(n_chunks)]
         stream = Stream(
             [[pltpu.make_async_copy(m_hbm.at[:, c], m_ref.at[:, c], sem.at[n])] for n, c in enumerate(chunks)], 4
         )
         rev = j_ref[...]
+        c_ref[...] = r_ref[:, 5 * BLOCK :, :]
         for b in range(16):
             part = r_ref[b]
             key, value = part[32:64].astype(F32), part[64:96].astype(F32)
@@ -221,16 +204,20 @@
                 o_ref[at, 0:32, :] = gq
                 o_ref[at, 32:64, :] = gk
                 o_ref[at, 64:96, :] = gv
-                o_ref[at, 96:128, :] = (raw * (1.0 / math.sqrt(SEQ))).astype(BF16)
+                raw = raw * (1.0 / math.sqrt(SEQ))
+                high = raw.astype(BF16)
+                o_ref[at, 96:128, :] = high
+                o_ref[at, 128:160, :] = (raw - high.astype(F32)).astype(BF16)
 
     vm = pl.BlockSpec(memory_space=pltpu.VMEM)
     return call(
         kernel,
         in_specs=[vm, pl.BlockSpec(memory_space=pl.ANY), vm, vm],
-        out_specs=[vm, vm],
+        out_specs=[vm, vm, vm],
         out_shape=[
             jax.ShapeDtypeStruct((128, SEQ), BF16),
-            jax.ShapeDtypeStruct((16, 128, 128), BF16),
+            jax.ShapeDtypeStruct((16, 160, 128), BF16),
+            jax.ShapeDtypeStruct((16, SEQ_DEV, 128), BF16),
         ],
         scratch_shapes=[
             pltpu.VMEM((SEQ, SEQ), BF16),
@@ -263,12 +250,12 @@
         for chip in range(8):
             for core in range(2):
                 at = core * 256 + chip * BLOCK
-                for j in range(4):
+                for j in range(5):
                     g_ref[j * 512 + at : j * 512 + at + BLOCK, :] = r_ref[
                         2 * chip + core, j * BLOCK : (j + 1) * BLOCK, :
                     ]
         grads = g_ref[0:1536].astype(F32).T.astype(BF16)
-        f_ref[...] = g_ref[1536:2048].astype(F32).T
+        f_ref[...] = (g_ref[1536:2048].astype(F32) + g_ref[2048:2560].astype(F32)).T
         for s in range(steps):
             stream.wait(s)
             o_ref[s] = dot(grads, w_ref[s * depth : (s + 1) * depth], NT).astype(BF16)
@@ -284,7 +271,7 @@
         ],
         scratch_shapes=[
             pltpu.VMEM((4096, 1536), BF16),
-            pltpu.VMEM((2048, SEQ_DEV), BF16),
+            pltpu.VMEM((2560, SEQ_DEV), BF16),
             pltpu.SemaphoreType.DMA((steps, 3)),
         ],
         flops=2 * 128 * 4096 * 1536,
@@ -329,10 +316,9 @@
         out_specs=[pl.BlockSpec(memory_space=pltpu.VMEM)] * 2,
         out_shape=[jax.ShapeDtypeStruct((256, SEQ), BF16)] * 2,
         scratch_shapes=[pltpu.SemaphoreType.DMA((4,))],
-        bytes_accessed=4 * MIB,
-        vmem=8,
+        vmem=4,
         name="pair",
-    )(in_hbm(first), in_hbm(second), in_hbm(third), in_hbm(fourth))
+    )(first, second, third, fourth)
 
 
 def weight_gradients(place, columns, blocks):
@@ -343,15 +329,13 @@
         column_refs, block_refs = refs[:8], refs[8:16]
         in_hbm, out_hbm, send_ref, t_ref, g_ref, res_ref, t_sem, sem, out_sem = refs[16:]
         core = place_ref[8]
-        t_copies = [[], []]
-        for j in range(2):
-            for i in range(8):
-                lanes = pl.ds(pl.multiple_of(place_ref[9 + i % 4] * 128, 128), 128)
-                t_copies[j].append(
-                    pltpu.make_async_copy(
-                        column_refs[i].at[:, j], t_ref.at[j, i // 4, :, :, lanes], t_sem.at[j, i]
-                    )
-                )
+        t_copies = []
+        for i in range(8):
+            lanes = pl.ds(pl.multiple_of(place_ref[9 + i % 4] * 128, 128), 128)
+            kind = core if i < 4 else 1 - core
+            for c in range(2):
+                src = column_refs[i].at[:, c]
+                t_copies.append(pltpu.make_async_copy(src, t_ref.at[kind, c, :, :, lanes], t_sem.at[c, i]))
         copies = [[], [], [], []]
         for j in range(4):
             for k in range(8):
@@ -361,17 +345,15 @@
                         block_refs[k].at[pl.ds(first_rows[k] + j * BLOCK, BLOCK)], g_ref.at[j, pl.ds(at, BLOCK)], sem.at[j, k]
                     )
                 )
-        for copy in t_copies[0] + copies[0] + copies[1] + copies[2] + t_copies[1] + copies[3]:
+        for copy in t_copies + copies[0] + copies[1] + copies[2] + copies[3]:
             copy.start()
         half = pl.multiple_of(core * 256, 256)
         rest = pl.multiple_of((1 - core) * 256, 256)
         outs = []
         for j in range(4):
-            for copy in copies[j] + (t_copies[j // 3] if j % 3 == 0 else []):
+            for copy in copies[j] + (t_copies if j == 0 else []):
                 copy.wait()
-            own = g_ref[j, :, pl.ds(pl.multiple_of(core * 1024, 1024), 1024)]
-            other = g_ref[j, :, pl.ds(pl.multiple_of((1 - core) * 1024, 1024), 1024)]
-            total = dot(own, t_ref[j // 3, 0].reshape(1024, 512)) + dot(other, t_ref[j // 3, 1].reshape(1024, 512))
+            total = dot(g_ref[j], t_ref[j // 3].reshape(SEQ, 512))
             total = total * factor
             if j < 3:
                 res_ref[j] = total.T
@@ -406,11 +388,9 @@
             pltpu.SemaphoreType.DMA((4, 8)),
             pltpu.SemaphoreType.DMA((4,)),
         ],
-        flops=4 * 1024 * 256 * SEQ,
-        bytes_accessed=10 * MIB,
         vmem=24,
         name="weight_gradients",
-    )(place, *[in_hbm(value) for value in columns + [block for block, _ in blocks]])
+    )(place, *[in_hbm(value.reshape(8, 2, SEQ_DEV, 128)) for value in columns], *[in_hbm(block) for block, _ in blocks])
 
 
 def fill_halves(place, sent, in_grad, out_grad):
@@ -434,7 +414,6 @@
         out_shape=[jax.ShapeDtypeStruct((3, 256, 512), F32), jax.ShapeDtypeStruct((512, 256), F32)],
         scratch_shapes=[pltpu.VMEM((4, 256, 256), F32), pltpu.SemaphoreType.DMA((4,))],
         input_output_aliases={2: 0, 3: 1},
-        bytes_accessed=3 * MIB,
         vmem=8,
         name="fill_halves",
     )(place, sent, in_hbm(in_grad), in_hbm(out_grad))
@@ -478,28 +457,26 @@
     place = [((x ^ f) << 2) + ((z - s) & 3) for f, s in HOPS] + [core] + [(y - s) & 3 for s in range(4)]
     place = jnp.stack(place).astype(jnp.int32)
     weight = jnp.transpose(in_weight, (1, 0, 2))
-    columns = split_columns(y.astype(jnp.int32)[None], tokens, out_grad)
-    signals = project(after(tokens, columns), out_grad, weight, out_weight, filters)
-    columns = swap(columns, "ctx", [list(range(c, 16, 2)) for c in range(2)])
-    signals, columns = lax.optimization_barrier((signals, columns))
-    signals = swap(signals.reshape(16, 5 * BLOCK, SEQ_DEV), "ctx")
-    columns = [columns] + [hop_y(columns, s) for s in (1, 2, 3)]
+    signals = project(y.astype(jnp.int32)[None], tokens, out_grad, weight, out_weight, filters)
+    signals = swap(signals.reshape(16, 5 * BLOCK + 128, SEQ_DEV), "ctx")
     flip = jnp.asarray(np.eye(256)[::-1].astype(ml_dtypes.bfloat16))
-    block, pieces = convolve(
+    block, pieces, columns = convolve(
         signals, jnp.asarray(cosine_matrix()), jnp.asarray(frequency_rows()), flip
     )
+    columns = [columns] + [hop_y(columns, s) for s in (1, 2, 3)]
     up, down, flipped = hop(block, 0, 1), hop(block, 0, 3), hop(block, 1, 0)
     pieces = swap(pieces, "ctx")
-    up, down, flipped, pieces, *columns = lax.optimization_barrier((up, down, flipped, pieces, *columns))
-    across, two = pair(up, down, block, flipped)
-    across, two = hop(across, 1, 0), hop(two, 0, 2)
+    up, down, flipped, pieces = lax.optimization_barrier((up, down, flipped, pieces))
+    near, here = pair(up, down, block, flipped)
+    across, two = hop(near, 1, 0), hop(here, 0, 2)
+    pieces = after(pieces, near)
     partial, filter_grad = input_partial(pieces, weight)
     parts = swap(partial, "mp")
-    parts, across, two = lax.optimization_barrier((parts, across, two))
+    columns = columns[:2] + [after(value, partial) for value in columns[2:]]
     columns += [swap_cores(value) for value in columns]
     input_grad = sum_partials(parts)
     blocks = [(block, 0), (up, 0), (down, 0), (flipped, 0), (two, 0), (across, 0), (across, 128), (two, 128)]
-    in_grad, out_weight_grad, send = weight_gradients(after(place, input_grad), columns, blocks)
+    in_grad, out_weight_grad, send = weight_gradients(place, columns, blocks)
     in_grad, out_weight_grad = fill_halves(place, swap_cores(send), in_grad, out_weight_grad)
     return (input_grad, jnp.transpose(in_grad, (1, 0, 2)), out_weight_grad, filter_grad)
 

time: 129 us -> 120 us (0.930)
  blocking collectives: 0 us -> 28.1 us
  waiting for transfers between devices: 43.9 us -> 23.9 us
  starting transfers between devices: 45.4 us -> 31.7 us
  Pallas kernels: 37.3 us -> 33.4 us
    all_to_all x4 -> x2, waiting for transfers between devices: 32.4 us -> 1.96 us  [swap(): lax.all_to_all(pieces, axis, 0, 0, axis_index_groups=groups, tiled=True)]
    all_to_all x0 -> x1, blocking collectives: none -> 28.1 us  [swap(): lax.all_to_all(pieces, axis, 0, 0, axis_index_groups=groups, tiled=True)]
    all_to_all x4 -> x2, starting transfers between devices: 28.8 us -> 7.6 us  [swap(): lax.all_to_all(pieces, axis, 0, 0, axis_index_groups=groups, tiled=True)]
    ppermute x5, waiting for transfers between devices: 7.12 us -> 13.8 us  [hop(): return lax.ppermute(value, 'ctx', chip_hop(x_flip, z_step))]
    ppermute x3, waiting for transfers between devices: 2.8 us -> 8.15 us  [hop_y(): lax.ppermute(value, 'mp', [(i, i // 4 * 4 + (i % 4 + step) % 4) for i in...]
    ppermute x5, starting transfers between devices: 6.13 us -> 9.03 us  [swap_cores(): return lax.ppermute(value, 'ctx', [(i, i ^ 1) for i in range(16)])]
    ppermute x3, starting transfers between devices: 3.78 us -> 6.65 us  [hop_y(): lax.ppermute(value, 'mp', [(i, i // 4 * 4 + (i % 4 + step) % 4) for i in...]
    pallas_call x2 -> x1, Pallas kernels: 10.2 us -> 7.55 us  [project(): call(kernel, in_specs=[pl.BlockSpec(memory_space=pltpu.SMEM)] + [hbm] * 5...]
  transfers between devices with their start and end apart: 17 -> 15, of which waited for: 7 -> 4; matrix products, arithmetic and copies ran while one was open for 0% -> 0% of each run, Pallas kernels for 19% -> 14%
where the time goes in v2:
time: 120 us
  Pallas kernels  33.4 us (28%)
  starting transfers between devices  31.7 us (26%)
  blocking collectives  28.1 us (23%)
  waiting for transfers between devices  23.9 us (20%)
  local copies, waits for them, and re-layouts  2.08 us (2%)
    all_to_all x1, blocking collectives, swap(): lax.all_to_all(pieces, axis, 0, 0, axis_index_groups=groups, tiled=True)  28.1 us
    ppermute x5, waiting for transfers between devices, hop(): return lax.ppermute(value, 'ctx', chip_hop(x_flip, z_step))  13.8 us
    ppermute x5, starting transfers between devices, swap_cores(): return lax.ppermute(value, 'ctx', [(i, i ^ 1) for i in range(16)])  9.03 us
    ppermute x5, starting transfers between devices, hop(): return lax.ppermute(value, 'ctx', chip_hop(x_flip, z_step))  8.43 us
    ppermute x3, waiting for transfers between devices, hop_y(): lax.ppermute(value, 'mp', [(i, i // 4 * 4 + (i % 4 + step) % 4) for i in...  8.15 us
    all_to_all x2, starting transfers between devices, swap(): lax.all_to_all(pieces, axis, 0, 0, axis_index_groups=groups, tiled=True)  7.6 us
    pallas_call x1, Pallas kernels, project(): call(kernel, in_specs=[pl.BlockSpec(memory_space=pltpu.SMEM)] + [hbm] * 5...  7.55 us
    pallas_call x1, Pallas kernels, weight_gradients(): call(kernel, in_specs=[pl.BlockSpec(memory_space=pltpu.SMEM)] + [hbm] * 1...  7.52 us
  transfers between devices with their start and end apart: 15, of which 4 were waited for; matrix products, arithmetic and copies ran while one was open for 0% of the time, Pallas kernels for 14%

profile of v2, /device:TPU:1, one launch (start us, length us, event | category | flops | bytes accessed | tf_op | source)
XLA Modules:
  0.0 120.2 jit_solution(8415100349085417332)
XLA Ops:
  0.6 7.6 %project.1 = bf16[8,2,288,128]{3,2,1,0:T(8,128)(2,1)S(1)} custom-call(s32[1]{0:T(128)} %bitcast.y_ref, bf16[128,4096]{1,0:T(8,128)(2,1)} %t_hbm.1, bf16[128,4096]{1,0:T(8,128)(2,1)} %g_hbm.1, f32[128,512]{1,0:T(8,128)} %f_hbm.1, bf16[3,4096,512]{2,1,0:T(8,128)(2,1)} %bitcast.27, bf16[512,4096]{1,0:T(8,128)(2,1)} %ow_hbm.1), custom_call_target="tpu_custom_call" | custom-call | flops 2147483648 | bytes 19922944 | tf_op jit(solution)/shard_map/project/pallas_call | solution.py:111
  8.2 0.0 copy-start.6
  8.2 0.0 copy-start.7
  8.2 28.1 %all_to_all.15.r_ref = bf16[16,288,128]{2,1,0:T(8,128)(2,1)S(1)} all-to-all(bf16[16,288,128]{2,1,0:T(8,128)(2,1)S(1)} %bitcast.25), channel_id=1, replica_groups=mesh['ctx'=16,'mp'=8] {'ctx'}, dimensions={0} | all-to-all | bytes 2359296 | tf_op jit(solution)/shard_map/all_to_all | solution.py:435
  36.3 7.5 %convolve.1 = (bf16[128,2048]{1,0:T(8,128)(2,1)S(1)}, bf16[16,160,128]{2,1,0:T(8,128)(2,1)}, bf16[16,128,128]{2,1,0:T(8,128)(2,1)S(1)}) custom-call(bf16[16,288,128]{2,1,0:T(8,128)(2,1)S(1)} %all_to_all.15.r_ref, bf16[2048,2048]{1,0:T(8,128)(2,1)} %constant.31.clone.m_hbm, f32[8,2048]{1,0:T(8,128)S(1)} %copy-done.7, bf16[256,256]{1,0:T(8,128)(2,1)S(1)} %copy-done.6), custom_call_target="tpu_custom_call" | custom-call | flops 3221225472 | bytes 12582912 | tf_op jit(solution)/shard_map/convolve/pallas_call | solution.py:213
  43.9 0.8 copy-done.5
  44.7 4.0 %all-to-all-start.1 = ((bf16[16,160,128]{2,1,0:T(8,128)(2,1)}), bf16[16,160,128]{2,1,0:T(8,128)(2,1)S(1)}, u32[]{:S(2)}, u32[]{:S(2)}) async-start(bf16[16,160,128]{2,1,0:T(8,128)(2,1)} %get-tuple-element.24), calls=%async_computation.1 | async-start | bytes 1310720 | tf_op jit(solution)/shard_map/all_to_all | solution.py:435
  48.7 2.9 %collective-permute-start.2 = (bf16[128,2048]{1,0:T(8,128)(2,1)S(1)}, bf16[128,2048]{1,0:T(8,128)(2,1)S(1)}, u32[]{:S(2)}, u32[]{:S(2)}) collective-permute-start(bf16[128,2048]{1,0:T(8,128)(2,1)S(1)} %get-tuple-element.23.c.refs_8_), channel_id=1, source_target_pairs={{0,64},{8,72},{16,80},{24,88},{32,96},{40,104},{48,112},{56,120},{... | collective-permute-start | bytes 1572872 | tf_op jit(solution)/shard_map/ppermute | solution.py:442
  51.6 2.4 %collective-permute-start.1 = (bf16[128,2048]{1,0:T(8,128)(2,1)S(1)}, bf16[128,2048]{1,0:T(8,128)(2,1)S(1)}, u32[]{:S(2)}, u32[]{:S(2)}) collective-permute-start(bf16[128,2048]{1,0:T(8,128)(2,1)S(1)} %get-tuple-element.23.c.refs_8_), channel_id=1, source_target_pairs={{0,48},{8,56},{16,0},{24,8},{32,16},{40,24},{48,32},{56,40},{64,11... | collective-permute-start | bytes 1572872 | tf_op jit(solution)/shard_map/ppermute | solution.py:442
  54.1 0.0 collective-permute-start
  54.1 2.7 %collective-permute-start.5 = (bf16[16,128,128]{2,1,0:T(8,128)(2,1)}, bf16[16,128,128]{2,1,0:T(8,128)(2,1)}, u32[]{:S(2)}, u32[]{:S(2)}) collective-permute-start(bf16[16,128,128]{2,1,0:T(8,128)(2,1)} %copy-done.5), channel_id=1, source_target_pairs={{0,3},{1,0},{2,1},{3,2},{4,7},{5,4},{6,5},{7,6},{8,11},{9,8},{10,9... | collective-permute-start | bytes 1572872 | tf_op jit(solution)/shard_map/ppermute | solution.py:450
  56.8 1.2 collective-permute-start.6
  58.0 12.9 %collective-permute-done.2.d.refs_11_ = bf16[128,2048]{1,0:T(8,128)(2,1)S(1)} collective-permute-done((bf16[128,2048]{1,0:T(8,128)(2,1)S(1)}, bf16[128,2048]{1,0:T(8,128)(2,1)S(1)}, u32[]{:S(2)}, u32[]{:S(2)}) %collective-permute-start.2) | collective-permute-done | bytes 524320 | tf_op jit(solution)/shard_map/ppermute | solution.py:442
  70.9 1.3 %collective-permute-start.3 = (bf16[16,128,128]{2,1,0:T(8,128)(2,1)}, bf16[16,128,128]{2,1,0:T(8,128)(2,1)}, u32[]{:S(2)}, u32[]{:S(2)}) collective-permute-start(bf16[16,128,128]{2,1,0:T(8,128)(2,1)} %copy-done.5), channel_id=1, source_target_pairs={{0,1},{1,2},{2,3},{3,0},{4,5},{5,6},{6,7},{7,4},{8,9},{9,10},{10,1... | collective-permute-start | bytes 1572872 | tf_op jit(solution)/shard_map/ppermute | solution.py:450
  72.2 0.0 collective-permute-done.1.b.refs_10_
  72.2 2.6 %collective-permute-start.4 = (bf16[16,128,128]{2,1,0:T(8,128)(2,1)}, bf16[16,128,128]{2,1,0:T(8,128)(2,1)}, u32[]{:S(2)}, u32[]{:S(2)}) collective-permute-start(bf16[16,128,128]{2,1,0:T(8,128)(2,1)} %copy-done.5), channel_id=1, source_target_pairs={{0,2},{1,3},{2,0},{3,1},{4,6},{5,7},{6,4},{7,5},{8,10},{9,11},{10,... | collective-permute-start | bytes 1572872 | tf_op jit(solution)/shard_map/ppermute | solution.py:450
  74.8 0.0 collective-permute-done.a.refs_9_
  74.8 0.0 all-to-all-done.1.r_ref
  74.8 1.5 %pair.1 = (bf16[256,2048]{1,0:T(8,128)(2,1)}, bf16[256,2048]{1,0:T(8,128)(2,1)}) custom-call(bf16[128,2048]{1,0:T(8,128)(2,1)S(1)} %collective-permute-done.a.refs_9_, bf16[128,2048]{1,0:T(8,128)(2,1)S(1)} %collective-permute-done.1.b.refs_10_, bf16[128,2048]{1,0:T(8,128)(2,1)S(1)} %get-tuple-element.23.c.refs_8_, ...), custom_call_target="tpu_custom_call" | custom-call | tf_op jit(solution)/shard_map/pair/pallas_call | solution.py:313
  76.3 0.0 copy-done
  76.3 2.8 %collective-permute-start.10 = (bf16[256,2048]{1,0:T(8,128)(2,1)}, bf16[256,2048]{1,0:T(8,128)(2,1)}, u32[]{:S(2)}, u32[]{:S(2)}) collective-permute-start(bf16[256,2048]{1,0:T(8,128)(2,1)} %get-tuple-element.35), channel_id=1, source_target_pairs={{0,32},{8,40},{16,48},{24,56},{32,0},{40,8},{48,16},{56,24},{64,96... | collective-permute-start | bytes 3145736 | tf_op jit(solution)/shard_map/ppermute | solution.py:442
  79.1 0.0 collective-permute-done.5
  79.1 0.3 collective-permute-start.11
  79.4 6.9 %input_partial.1 = (bf16[8,128,512]{2,1,0:T(8,128)(2,1)S(1)}, f32[128,512]{1,0:T(8,128)}) custom-call(bf16[16,160,128]{2,1,0:T(8,128)(2,1)S(1)} %all-to-all-done.1.r_ref, bf16[3,4096,512]{2,1,0:T(8,128)(2,1)} %bitcast.28), custom_call_target="tpu_custom_call" | custom-call | flops 1610612736 | bytes 14680064 | tf_op jit(solution)/shard_map/input_partial/pallas_call | solution.py:264
  86.3 0.0 copy-done.1
  86.3 0.0 copy-done.2
  86.3 0.0 copy-done.3
  86.4 1.0 copy-done.4
  87.3 0.0 collective-permute-done.3
  87.3 2.0 %collective-permute-start.7 = (bf16[16,128,128]{2,1,0:T(8,128)(2,1)}, bf16[16,128,128]{2,1,0:T(8,128)(2,1)S(1)}, u32[]{:S(2)}, u32[]{:S(2)}) collective-permute-start(bf16[16,128,128]{2,1,0:T(8,128)(2,1)} %collective-permute-done.3), channel_id=1, source_target_pairs={{0,8},{8,0},{16,24},{24,16},{32,40},{40,32},{48,56},{56,48},{64,72... | collective-permute-start | bytes 1572872 | tf_op jit(solution)/shard_map/ppermute | solution.py:431
  89.3 8.1 %collective-permute-done.4 = bf16[16,128,128]{2,1,0:T(8,128)(2,1)} collective-permute-done((bf16[16,128,128]{2,1,0:T(8,128)(2,1)}, bf16[16,128,128]{2,1,0:T(8,128)(2,1)}, u32[]{:S(2)}, u32[]{:S(2)}) %collective-permute-start.4) | collective-permute-done | bytes 524320 | tf_op jit(solution)/shard_map/ppermute | solution.py:450
  97.4 1.8 %collective-permute-start.8 = (bf16[16,128,128]{2,1,0:T(8,128)(2,1)}, bf16[16,128,128]{2,1,0:T(8,128)(2,1)S(1)}, u32[]{:S(2)}, u32[]{:S(2)}) collective-permute-start(bf16[16,128,128]{2,1,0:T(8,128)(2,1)} %collective-permute-done.4), channel_id=1, source_target_pairs={{0,8},{8,0},{16,24},{24,16},{32,40},{40,32},{48,56},{56,48},{64,72... | collective-permute-start | bytes 1572872 | tf_op jit(solution)/shard_map/ppermute | solution.py:431
  99.2 0.0 collective-permute-done.6
  99.2 0.0 collective-permute-start.9
  99.2 3.6 %all-to-all-start.2 = ((bf16[8,128,512]{2,1,0:T(8,128)(2,1)}), bf16[8,128,512]{2,1,0:T(8,128)(2,1)S(1)}, u32[]{:S(2)}, u32[]{:S(2)}) async-start(bf16[8,128,512]{2,1,0:T(8,128)(2,1)} %copy-done.4), calls=%async_computation.2 | async-start | bytes 2097152 | tf_op jit(solution)/shard_map/all_to_all | solution.py:435
  102.8 0.1 stack.55.place_ref
  102.9 0.0 collective-permute-done.7
  102.9 0.0 collective-permute-done.8
  102.9 0.0 collective-permute-done.9
  103.0 0.0 collective-permute-done.10.refs_12_.refs_15_
  103.0 0.9 collective-permute-done.11.refs_13_.refs_14_
  103.9 0.2 copy-done.10
  104.1 7.5 %weight_gradients.1 = (f32[3,256,512]{2,1,0:T(8,128)}, f32[512,256]{1,0:T(8,128)}, bf16[1024,256]{1,0:T(8,128)(2,1)S(1)}) custom-call(s32[13]{0:T(128)S(1)} %stack.55.place_ref, bf16[8,2,128,128]{3,2,1,0:T(8,128)(2,1)} %bitcast.26, bf16[8,2,128,128]{3,2,1,0:T(8,128)(2,1)} %bitcast.17.refs_1_, bf16[8,2,128,128]{3,2,1,0:T(8,128)(2,1)} %bitcast.18.refs_2_, ...), custom_call_target="tpu_custom_call" | custom-call | tf_op jit(solution)/shard_map/weight_gradients/pallas_call | solution.py:374
  111.6 4.1 %collective-permute-start.12 = (bf16[1024,256]{1,0:T(8,128)(2,1)S(1)}, bf16[1024,256]{1,0:T(8,128)(2,1)S(1)}, u32[]{:S(2)}, u32[]{:S(2)}) collective-permute-start(bf16[1024,256]{1,0:T(8,128)(2,1)S(1)} %get-tuple-element.36), channel_id=1, source_target_pairs={{0,8},{8,0},{16,24},{24,16},{32,40},{40,32},{48,56},{56,48},{64,72... | collective-permute-start | bytes 1572872 | tf_op jit(solution)/shard_map/ppermute | solution.py:431
  115.7 2.0 %all-to-all-done.2.p_ref = bf16[8,128,512]{2,1,0:T(8,128)(2,1)S(1)} async-done(((bf16[8,128,512]{2,1,0:T(8,128)(2,1)}), bf16[8,128,512]{2,1,0:T(8,128)(2,1)S(1)}, u32[]{:S(2)}, u32[]{:S(2)}) %all-to-all-start.2) | async-done | bytes 1048608 | tf_op jit(solution)/shard_map/all_to_all | solution.py:435
  117.7 0.8 sum_partials.1
  118.5 0.0 collective-permute-done.12.s_ref
  118.5 1.6 %fill_halves.1 = (f32[3,256,512]{2,1,0:T(8,128)}, f32[512,256]{1,0:T(8,128)}) custom-call(s32[13]{0:T(128)S(1)} %stack.55.place_ref, bf16[1024,256]{1,0:T(8,128)(2,1)S(1)} %collective-permute-done.12.s_ref, f32[3,256,512]{2,1,0:T(8,128)} %get-tuple-element.37.in_old, f32[512,256]{1,0:T(8,128)} %get-tuple-element.38.out_old), custom_call_target="tpu_custom_call", output_to_operand_aliasing={{0}: (2, {}), {1}: (3, {})} | custom-call | tf_op jit(solution)/shard_map/fill_halves/pallas_call | solution.py:410
  (13 shorter events, 0.0 us)
Async XLA Ops:
  8.2 28.1 %copy-start.6 = (bf16[256,256]{1,0:T(8,128)(2,1)S(1)}, bf16[256,256]{1,0:T(8,128)(2,1)}, u32[]{:S(2)}) copy-start(bf16[256,256]{1,0:T(8,128)(2,1)} %constant.30.clone.j_ref) | copy-start | bytes 393220
  8.2 28.1 %copy-start.7 = (f32[8,2048]{1,0:T(8,128)S(1)}, f32[8,2048]{1,0:T(8,128)}, u32[]{:S(2)}) copy-start(f32[8,2048]{1,0:T(8,128)} %constant.32.clone.w_ref) | copy-start | bytes 196612
  43.8 0.8 copy-start.5
  44.7 31.7 %copy-start = (bf16[128,2048]{1,0:T(8,128)(2,1)}, bf16[128,2048]{1,0:T(8,128)(2,1)S(1)}, u32[]{:S(2)}) copy-start(bf16[128,2048]{1,0:T(8,128)(2,1)S(1)} %get-tuple-element.23.c.refs_8_) | copy-start | bytes 1572868
  44.7 30.1 %all-to-all-start.1 = ((bf16[16,160,128]{2,1,0:T(8,128)(2,1)}), bf16[16,160,128]{2,1,0:T(8,128)(2,1)S(1)}, u32[]{:S(2)}, u32[]{:S(2)}) async-start(bf16[16,160,128]{2,1,0:T(8,128)(2,1)} %get-tuple-element.24), calls=%async_computation.1 | async-start | bytes 1310720 | tf_op jit(solution)/shard_map/all_to_all | solution.py:435
  48.7 22.2 %collective-permute-start.2 = (bf16[128,2048]{1,0:T(8,128)(2,1)S(1)}, bf16[128,2048]{1,0:T(8,128)(2,1)S(1)}, u32[]{:S(2)}, u32[]{:S(2)}) collective-permute-start(bf16[128,2048]{1,0:T(8,128)(2,1)S(1)} %get-tuple-element.23.c.refs_8_), channel_id=1, source_target_pairs={{0,64},{8,72},{16,80},{24,88},{32,96},{40,104},{48,112},{56,120},{... | collective-permute-start | bytes 1572872 | tf_op jit(solution)/shard_map/ppermute | solution.py:442
  51.6 20.5 %collective-permute-start.1 = (bf16[128,2048]{1,0:T(8,128)(2,1)S(1)}, bf16[128,2048]{1,0:T(8,128)(2,1)S(1)}, u32[]{:S(2)}, u32[]{:S(2)}) collective-permute-start(bf16[128,2048]{1,0:T(8,128)(2,1)S(1)} %get-tuple-element.23.c.refs_8_), channel_id=1, source_target_pairs={{0,48},{8,56},{16,0},{24,8},{32,16},{40,24},{48,32},{56,40},{64,11... | collective-permute-start | bytes 1572872 | tf_op jit(solution)/shard_map/ppermute | solution.py:442
  54.1 20.7 %collective-permute-start = (bf16[128,2048]{1,0:T(8,128)(2,1)S(1)}, bf16[128,2048]{1,0:T(8,128)(2,1)S(1)}, u32[]{:S(2)}, u32[]{:S(2)}) collective-permute-start(bf16[128,2048]{1,0:T(8,128)(2,1)S(1)} %get-tuple-element.23.c.refs_8_), channel_id=1, source_target_pairs={{0,16},{8,24},{16,32},{24,40},{32,48},{40,56},{48,0},{56,8},{64,80... | collective-permute-start | bytes 1572872 | tf_op jit(solution)/shard_map/ppermute | solution.py:442
  54.1 25.1 %collective-permute-start.5 = (bf16[16,128,128]{2,1,0:T(8,128)(2,1)}, bf16[16,128,128]{2,1,0:T(8,128)(2,1)}, u32[]{:S(2)}, u32[]{:S(2)}) collective-permute-start(bf16[16,128,128]{2,1,0:T(8,128)(2,1)} %copy-done.5), channel_id=1, source_target_pairs={{0,3},{1,0},{2,1},{3,2},{4,7},{5,4},{6,5},{7,6},{8,11},{9,8},{10,9... | collective-permute-start | bytes 1572872 | tf_op jit(solution)/shard_map/ppermute | solution.py:450
  56.8 42.4 %collective-permute-start.6 = (bf16[16,128,128]{2,1,0:T(8,128)(2,1)}, bf16[16,128,128]{2,1,0:T(8,128)(2,1)}, u32[]{:S(2)}, u32[]{:S(2)}) collective-permute-start(bf16[16,128,128]{2,1,0:T(8,128)(2,1)} %copy-done.5), channel_id=1, source_target_pairs={{0,8},{8,0},{16,24},{24,16},{32,40},{40,32},{48,56},{56,48},{64,72... | collective-permute-start | bytes 1572872 | tf_op jit(solution)/shard_map/ppermute | solution.py:431
  70.9 15.5 %copy-start.1 = (bf16[128,2048]{1,0:T(8,128)(2,1)}, bf16[128,2048]{1,0:T(8,128)(2,1)S(1)}, u32[]{:S(2)}) copy-start(bf16[128,2048]{1,0:T(8,128)(2,1)S(1)} %collective-permute-done.2.d.refs_11_) | copy-start | bytes 1572868
  70.9 16.5 %collective-permute-start.3 = (bf16[16,128,128]{2,1,0:T(8,128)(2,1)}, bf16[16,128,128]{2,1,0:T(8,128)(2,1)}, u32[]{:S(2)}, u32[]{:S(2)}) collective-permute-start(bf16[16,128,128]{2,1,0:T(8,128)(2,1)} %copy-done.5), channel_id=1, source_target_pairs={{0,1},{1,2},{2,3},{3,0},{4,5},{5,6},{6,7},{7,4},{8,9},{9,10},{10,1... | collective-permute-start | bytes 1572872 | tf_op jit(solution)/shard_map/ppermute | solution.py:450
  72.2 14.2 %copy-start.2 = (bf16[128,2048]{1,0:T(8,128)(2,1)}, bf16[128,2048]{1,0:T(8,128)(2,1)S(1)}, u32[]{:S(2)}) copy-start(bf16[128,2048]{1,0:T(8,128)(2,1)S(1)} %collective-permute-done.1.b.refs_10_) | copy-start | bytes 1572868
  72.2 25.3 %collective-permute-start.4 = (bf16[16,128,128]{2,1,0:T(8,128)(2,1)}, bf16[16,128,128]{2,1,0:T(8,128)(2,1)}, u32[]{:S(2)}, u32[]{:S(2)}) collective-permute-start(bf16[16,128,128]{2,1,0:T(8,128)(2,1)} %copy-done.5), channel_id=1, source_target_pairs={{0,2},{1,3},{2,0},{3,1},{4,6},{5,7},{6,4},{7,5},{8,10},{9,11},{10,... | collective-permute-start | bytes 1572872 | tf_op jit(solution)/shard_map/ppermute | solution.py:450
  74.8 11.6 %copy-start.3 = (bf16[128,2048]{1,0:T(8,128)(2,1)}, bf16[128,2048]{1,0:T(8,128)(2,1)S(1)}, u32[]{:S(2)}) copy-start(bf16[128,2048]{1,0:T(8,128)(2,1)S(1)} %collective-permute-done.a.refs_9_) | copy-start | bytes 1572868
  76.3 26.6 %collective-permute-start.10 = (bf16[256,2048]{1,0:T(8,128)(2,1)}, bf16[256,2048]{1,0:T(8,128)(2,1)}, u32[]{:S(2)}, u32[]{:S(2)}) collective-permute-start(bf16[256,2048]{1,0:T(8,128)(2,1)} %get-tuple-element.35), channel_id=1, source_target_pairs={{0,32},{8,40},{16,48},{24,56},{32,0},{40,8},{48,16},{56,24},{64,96... | collective-permute-start | bytes 3145736 | tf_op jit(solution)/shard_map/ppermute | solution.py:442
  79.1 24.8 %collective-permute-start.11 = (bf16[256,2048]{1,0:T(8,128)(2,1)}, bf16[256,2048]{1,0:T(8,128)(2,1)}, u32[]{:S(2)}, u32[]{:S(2)}) collective-permute-start(bf16[256,2048]{1,0:T(8,128)(2,1)} %get-tuple-element.29), channel_id=1, source_target_pairs={{0,64},{8,72},{16,80},{24,88},{32,96},{40,104},{48,112},{56,120},{... | collective-permute-start | bytes 3145736 | tf_op jit(solution)/shard_map/ppermute | solution.py:442
  86.4 1.0 copy-start.4
  87.3 15.6 %collective-permute-start.7 = (bf16[16,128,128]{2,1,0:T(8,128)(2,1)}, bf16[16,128,128]{2,1,0:T(8,128)(2,1)S(1)}, u32[]{:S(2)}, u32[]{:S(2)}) collective-permute-start(bf16[16,128,128]{2,1,0:T(8,128)(2,1)} %collective-permute-done.3), channel_id=1, source_target_pairs={{0,8},{8,0},{16,24},{24,16},{32,40},{40,32},{48,56},{56,48},{64,72... | collective-permute-start | bytes 1572872 | tf_op jit(solution)/shard_map/ppermute | solution.py:431
  97.4 5.5 %collective-permute-start.8 = (bf16[16,128,128]{2,1,0:T(8,128)(2,1)}, bf16[16,128,128]{2,1,0:T(8,128)(2,1)S(1)}, u32[]{:S(2)}, u32[]{:S(2)}) collective-permute-start(bf16[16,128,128]{2,1,0:T(8,128)(2,1)} %collective-permute-done.4), channel_id=1, source_target_pairs={{0,8},{8,0},{16,24},{24,16},{32,40},{40,32},{48,56},{56,48},{64,72... | collective-permute-start | bytes 1572872 | tf_op jit(solution)/shard_map/ppermute | solution.py:431
  99.2 3.7 %collective-permute-start.9 = (bf16[16,128,128]{2,1,0:T(8,128)(2,1)}, bf16[16,128,128]{2,1,0:T(8,128)(2,1)S(1)}, u32[]{:S(2)}, u32[]{:S(2)}) collective-permute-start(bf16[16,128,128]{2,1,0:T(8,128)(2,1)} %collective-permute-done.5), channel_id=1, source_target_pairs={{0,8},{8,0},{16,24},{24,16},{32,40},{40,32},{48,56},{56,48},{64,72... | collective-permute-start | bytes 1572872 | tf_op jit(solution)/shard_map/ppermute | solution.py:431
  99.2 18.5 %all-to-all-start.2 = ((bf16[8,128,512]{2,1,0:T(8,128)(2,1)}), bf16[8,128,512]{2,1,0:T(8,128)(2,1)S(1)}, u32[]{:S(2)}, u32[]{:S(2)}) async-start(bf16[8,128,512]{2,1,0:T(8,128)(2,1)} %copy-done.4), calls=%async_computation.2 | async-start | bytes 2097152 | tf_op jit(solution)/shard_map/all_to_all | solution.py:435
  102.9 1.0 copy-start.8
  102.9 1.0 copy-start.9
  102.9 1.1 copy-start.10
  111.6 6.9 %collective-permute-start.12 = (bf16[1024,256]{1,0:T(8,128)(2,1)S(1)}, bf16[1024,256]{1,0:T(8,128)(2,1)S(1)}, u32[]{:S(2)}, u32[]{:S(2)}) collective-permute-start(bf16[1024,256]{1,0:T(8,128)(2,1)S(1)} %get-tuple-element.36), channel_id=1, source_target_pairs={{0,8},{8,0},{16,24},{24,16},{32,40},{40,32},{48,56},{56,48},{64,72... | collective-permute-start | bytes 1572872 | tf_op jit(solution)/shard_map/ppermute | solution.py:431

commit v3 on v2

--- a/solution.py
+++ b/solution.py
@@ -146,13 +146,9 @@
     chunk = 512
     n_chunks = SEQ // chunk
 
-    def kernel(r_ref, m_hbm, w_ref, j_ref, b_ref, o_ref, c_ref, m_ref, x_ref, y_ref, sem):
-        chunks = [pl.ds(n * chunk, chunk) for n in range(n_chunks)]
-        stream = Stream(
-            [[pltpu.make_async_copy(m_hbm.at[:, c], m_ref.at[:, c], sem.at[n])] for n, c in enumerate(chunks)], 4
-        )
+    def kernel(r_ref, m_ref, w_ref, j_ref, b_ref, o_ref, c_ref, x_ref, y_ref):
         rev = j_ref[...]
-        c_ref[...] = r_ref[:, 5 * BLOCK :, :]
+        c_ref[...] = r_ref[:, 5 * BLOCK :, :].reshape(8, 2, SEQ_DEV, 128)
         for b in range(16):
             part = r_ref[b]
             key, value = part[32:64].astype(F32), part[64:96].astype(F32)
@@ -165,7 +161,6 @@
             x_ref[96:192, pl.ds((7 - b) * 256, 256)] = dot(x_ref[0:96, pl.ds(b * 256, 256)], rev).astype(BF16)
         for n in range(n_chunks):
             lanes = pl.ds(n * chunk, chunk)
-            stream.wait(n)
             spec = dot(x_ref[...], m_ref[:, lanes])
             wr, wi, sign = w_ref[0:1, lanes], w_ref[1:2, lanes], w_ref[2:3, lanes]
             hr, mr, gr = spec[0:32], spec[32:64], spec[64:96]
@@ -212,24 +207,22 @@
     vm = pl.BlockSpec(memory_space=pltpu.VMEM)
     return call(
         kernel,
-        in_specs=[vm, pl.BlockSpec(memory_space=pl.ANY), vm, vm],
+        in_specs=[vm, vm, vm, vm],
         out_specs=[vm, vm, vm],
         out_shape=[
             jax.ShapeDtypeStruct((128, SEQ), BF16),
             jax.ShapeDtypeStruct((16, 160, 128), BF16),
-            jax.ShapeDtypeStruct((16, SEQ_DEV, 128), BF16),
+            jax.ShapeDtypeStruct((8, 2, SEQ_DEV, 128), BF16),
         ],
         scratch_shapes=[
-            pltpu.VMEM((SEQ, SEQ), BF16),
             pltpu.VMEM((192, SEQ), BF16),
             pltpu.VMEM((192, SEQ), BF16),
-            pltpu.SemaphoreType.DMA((n_chunks,)),
         ],
         flops=4 * 192 * SEQ * SEQ,
         bytes_accessed=12 * MIB,
         vmem=20,
         name="convolve",
-    )(received, in_hbm(matrix), rows, flip)
+    )(received, in_vmem(matrix), rows, flip)
 
 
 def input_partial(received, weight):
@@ -390,7 +383,7 @@
         ],
         vmem=24,
         name="weight_gradients",
-    )(place, *[in_hbm(value.reshape(8, 2, SEQ_DEV, 128)) for value in columns], *[in_hbm(block) for block, _ in blocks])
+    )(place, columns[0], *map(in_hbm, columns[1:]), blocks[0][0], *[in_hbm(block) for block, _ in blocks[1:]])
 
 
 def fill_halves(place, sent, in_grad, out_grad):
@@ -454,7 +447,7 @@
     position = lax.axis_index("ctx")
     core, x, z = position & 1, position >> 3, (position >> 1) & 3
     y = lax.axis_index("mp") & 3
-    place = [((x ^ f) << 2) + ((z - s) & 3) for f, s in HOPS] + [core] + [(y - s) & 3 for s in range(4)]
+    place = [((x ^ f) << 2) + ((z - s) & 3) for f, s in HOPS] + [core] + [(y - s) & 3 for s in (0, 1, 3, 2)]
     place = jnp.stack(place).astype(jnp.int32)
     weight = jnp.transpose(in_weight, (1, 0, 2))
     signals = project(y.astype(jnp.int32)[None], tokens, out_grad, weight, out_weight, filters)
@@ -463,7 +456,7 @@
     block, pieces, columns = convolve(
         signals, jnp.asarray(cosine_matrix()), jnp.asarray(frequency_rows()), flip
     )
-    columns = [columns] + [hop_y(columns, s) for s in (1, 2, 3)]
+    columns = [columns] + [hop_y(columns, s) for s in (1, 3, 2)]
     up, down, flipped = hop(block, 0, 1), hop(block, 0, 3), hop(block, 1, 0)
     pieces = swap(pieces, "ctx")
     up, down, flipped, pieces = lax.optimization_barrier((up, down, flipped, pieces))

time: 120 us -> 116 us (0.967)
  Pallas kernels: 33.4 us -> 31.3 us
  starting transfers between devices: 31.7 us -> 30.3 us
    ppermute x5, waiting for transfers between devices: 13.8 us -> 22.9 us  [hop(): return lax.ppermute(value, 'ctx', chip_hop(x_flip, z_step))]
    ppermute x3, waiting for transfers between devices: 8.15 us -> 0.01 us  [hop_y(): lax.ppermute(value, 'mp', [(i, i // 4 * 4 + (i % 4 + step) % 4) for i in...]
    pallas_call x1, Pallas kernels: 7.51 us -> 5.42 us  [convolve(): call(kernel, in_specs=[vm, vm, vm, vm], out_specs=[vm, vm, vm], out_shape...]
    all_to_all x2, waiting for transfers between devices: 1.96 us -> 0.01 us  [swap(): lax.all_to_all(pieces, axis, 0, 0, axis_index_groups=groups, tiled=True)]
    ppermute x5, starting transfers between devices: 9.03 us -> 7.67 us  [swap_cores(): return lax.ppermute(value, 'ctx', [(i, i ^ 1) for i in range(16)])]
where the time goes in v3:
time: 116 us
  Pallas kernels  31.3 us (27%)
  starting transfers between devices  30.3 us (26%)
  blocking collectives  28.1 us (24%)
  waiting for transfers between devices  23.7 us (20%)
    all_to_all x1, blocking collectives, swap(): lax.all_to_all(pieces, axis, 0, 0, axis_index_groups=groups, tiled=True)  28.1 us
    ppermute x5, waiting for transfers between devices, hop(): return lax.ppermute(value, 'ctx', chip_hop(x_flip, z_step))  22.9 us
    ppermute x5, starting transfers between devices, hop(): return lax.ppermute(value, 'ctx', chip_hop(x_flip, z_step))  9.36 us
    pallas_call x1, Pallas kernels, project(): call(kernel, in_specs=[pl.BlockSpec(memory_space=pltpu.SMEM)] + [hbm] * 5...  7.68 us
    ppermute x5, starting transfers between devices, swap_cores(): return lax.ppermute(value, 'ctx', [(i, i ^ 1) for i in range(16)])  7.67 us
    all_to_all x2, starting transfers between devices, swap(): lax.all_to_all(pieces, axis, 0, 0, axis_index_groups=groups, tiled=True)  7.6 us
    pallas_call x1, Pallas kernels, weight_gradients(): call(kernel, in_specs=[pl.BlockSpec(memory_space=pltpu.SMEM)] + [hbm] * 1...  7.46 us
    pallas_call x1, Pallas kernels, input_partial(): call(kernel, in_specs=[vm, pl.BlockSpec(memory_space=pl.ANY)], out_specs=...  6.91 us
  transfers between devices with their start and end apart: 15, of which 4 were waited for; matrix products, arithmetic and copies ran while one was open for 0% of the time, Pallas kernels for 14%

profile of v3, /device:TPU:1, one launch (start us, length us, event | category | flops | bytes accessed | tf_op | source)
XLA Modules:
  0.0 115.6 jit_solution(11779420800398205502)
XLA Ops:
  0.6 0.0 copy-start.4
  0.7 7.7 %project.1 = bf16[8,2,288,128]{3,2,1,0:T(8,128)(2,1)S(1)} custom-call(s32[1]{0:T(128)} %bitcast.y_ref, bf16[128,4096]{1,0:T(8,128)(2,1)} %t_hbm.1, bf16[128,4096]{1,0:T(8,128)(2,1)} %g_hbm.1, f32[128,512]{1,0:T(8,128)} %f_hbm.1, bf16[3,4096,512]{2,1,0:T(8,128)(2,1)} %bitcast.18, bf16[512,4096]{1,0:T(8,128)(2,1)} %ow_hbm.1), custom_call_target="tpu_custom_call" | custom-call | flops 2147483648 | bytes 19922944 | tf_op jit(solution)/shard_map/project/pallas_call | solution.py:111
  8.3 0.0 copy-start.5
  8.4 0.0 copy-start.6
  8.4 28.1 %all_to_all.15.r_ref = bf16[16,288,128]{2,1,0:T(8,128)(2,1)S(1)} all-to-all(bf16[16,288,128]{2,1,0:T(8,128)(2,1)S(1)} %bitcast.17), channel_id=1, replica_groups=mesh['ctx'=16,'mp'=8] {'ctx'}, dimensions={0} | all-to-all | bytes 2359296 | tf_op jit(solution)/shard_map/all_to_all | solution.py:428
  36.5 0.0 copy-done.4
  36.5 0.0 copy-done.5
  36.5 0.0 copy-done.6
  36.5 5.4 %convolve.1 = (bf16[128,2048]{1,0:T(8,128)(2,1)S(1)}, bf16[16,160,128]{2,1,0:T(8,128)(2,1)}, bf16[8,2,128,128]{3,2,1,0:T(8,128)(2,1)S(1)}) custom-call(bf16[16,288,128]{2,1,0:T(8,128)(2,1)S(1)} %all_to_all.15.r_ref, bf16[2048,2048]{1,0:T(8,128)(2,1)S(1)} %copy-done.4, f32[8,2048]{1,0:T(8,128)S(1)} %copy-done.6, bf16[256,256]{1,0:T(8,128)(2,1)S(1)} %copy-done.5), custom_call_target="tpu_custom_call" | custom-call | flops 3221225472 | bytes 12582912 | tf_op jit(solution)/shard_map/convolve/pallas_call | solution.py:208
  41.9 4.0 %all-to-all-start.1 = ((bf16[16,160,128]{2,1,0:T(8,128)(2,1)}), bf16[16,160,128]{2,1,0:T(8,128)(2,1)S(1)}, u32[]{:S(2)}, u32[]{:S(2)}) async-start(bf16[16,160,128]{2,1,0:T(8,128)(2,1)} %get-tuple-element.24), calls=%async_computation.1 | async-start | bytes 1310720 | tf_op jit(solution)/shard_map/all_to_all | solution.py:428
  45.9 2.9 %collective-permute-start.2 = (bf16[128,2048]{1,0:T(8,128)(2,1)S(1)}, bf16[128,2048]{1,0:T(8,128)(2,1)S(1)}, u32[]{:S(2)}, u32[]{:S(2)}) collective-permute-start(bf16[128,2048]{1,0:T(8,128)(2,1)S(1)} %get-tuple-element.23.c.refs_8_), channel_id=1, source_target_pairs={{0,64},{8,72},{16,80},{24,88},{32,96},{40,104},{48,112},{56,120},{... | collective-permute-start | bytes 1572872 | tf_op jit(solution)/shard_map/ppermute | solution.py:435
  48.9 2.4 %collective-permute-start.1 = (bf16[128,2048]{1,0:T(8,128)(2,1)S(1)}, bf16[128,2048]{1,0:T(8,128)(2,1)S(1)}, u32[]{:S(2)}, u32[]{:S(2)}) collective-permute-start(bf16[128,2048]{1,0:T(8,128)(2,1)S(1)} %get-tuple-element.23.c.refs_8_), channel_id=1, source_target_pairs={{0,48},{8,56},{16,0},{24,8},{32,16},{40,24},{48,32},{56,40},{64,11... | collective-permute-start | bytes 1572872 | tf_op jit(solution)/shard_map/ppermute | solution.py:435
  51.3 0.0 collective-permute-start
  51.3 2.9 %collective-permute-start.5 = (bf16[8,2,128,128]{3,2,1,0:T(8,128)(2,1)S(1)}, bf16[8,2,128,128]{3,2,1,0:T(8,128)(2,1)}, u32[]{:S(2)}, u32[]{:S(2)}) collective-permute-start(bf16[8,2,128,128]{3,2,1,0:T(8,128)(2,1)S(1)} %get-tuple-element.32.refs_0_), channel_id=1, source_target_pairs={{0,2},{1,3},{2,0},{3,1},{4,6},{5,7},{6,4},{7,5},{8,10},{9,11},{10,... | collective-permute-start | bytes 1572872 | tf_op jit(solution)/shard_map/ppermute | solution.py:443
  54.2 1.2 %collective-permute-start.6 = (bf16[8,2,128,128]{3,2,1,0:T(8,128)(2,1)S(1)}, bf16[8,2,128,128]{3,2,1,0:T(8,128)(2,1)}, u32[]{:S(2)}, u32[]{:S(2)}) collective-permute-start(bf16[8,2,128,128]{3,2,1,0:T(8,128)(2,1)S(1)} %get-tuple-element.32.refs_0_), channel_id=1, source_target_pairs={{0,8},{8,0},{16,24},{24,16},{32,40},{40,32},{48,56},{56,48},{64,72... | collective-permute-start | bytes 1572872 | tf_op jit(solution)/shard_map/ppermute | solution.py:424
  55.4 12.7 %collective-permute-done.2.d.refs_11_ = bf16[128,2048]{1,0:T(8,128)(2,1)S(1)} collective-permute-done((bf16[128,2048]{1,0:T(8,128)(2,1)S(1)}, bf16[128,2048]{1,0:T(8,128)(2,1)S(1)}, u32[]{:S(2)}, u32[]{:S(2)}) %collective-permute-start.2) | collective-permute-done | bytes 524320 | tf_op jit(solution)/shard_map/ppermute | solution.py:435
  68.1 1.3 %collective-permute-start.3 = (bf16[8,2,128,128]{3,2,1,0:T(8,128)(2,1)S(1)}, bf16[8,2,128,128]{3,2,1,0:T(8,128)(2,1)}, u32[]{:S(2)}, u32[]{:S(2)}) collective-permute-start(bf16[8,2,128,128]{3,2,1,0:T(8,128)(2,1)S(1)} %get-tuple-element.32.refs_0_), channel_id=1, source_target_pairs={{0,1},{1,2},{2,3},{3,0},{4,5},{5,6},{6,7},{7,4},{8,9},{9,10},{10,1... | collective-permute-start | bytes 1572872 | tf_op jit(solution)/shard_map/ppermute | solution.py:443
  69.4 0.0 collective-permute-done.1.b.refs_10_
  69.4 1.5 %collective-permute-start.4 = (bf16[8,2,128,128]{3,2,1,0:T(8,128)(2,1)S(1)}, bf16[8,2,128,128]{3,2,1,0:T(8,128)(2,1)}, u32[]{:S(2)}, u32[]{:S(2)}) collective-permute-start(bf16[8,2,128,128]{3,2,1,0:T(8,128)(2,1)S(1)} %get-tuple-element.32.refs_0_), channel_id=1, source_target_pairs={{0,3},{1,0},{2,1},{3,2},{4,7},{5,4},{6,5},{7,6},{8,11},{9,8},{10,9... | collective-permute-start | bytes 1572872 | tf_op jit(solution)/shard_map/ppermute | solution.py:443
  70.9 0.0 collective-permute-done.a.refs_9_
  70.9 0.0 all-to-all-done.1.r_ref
  70.9 1.5 %pair.1 = (bf16[256,2048]{1,0:T(8,128)(2,1)}, bf16[256,2048]{1,0:T(8,128)(2,1)}) custom-call(bf16[128,2048]{1,0:T(8,128)(2,1)S(1)} %collective-permute-done.a.refs_9_, bf16[128,2048]{1,0:T(8,128)(2,1)S(1)} %collective-permute-done.1.b.refs_10_, bf16[128,2048]{1,0:T(8,128)(2,1)S(1)} %get-tuple-element.23.c.refs_8_, ...), custom_call_target="tpu_custom_call" | custom-call | tf_op jit(solution)/shard_map/pair/pallas_call | solution.py:306
  72.5 2.8 %collective-permute-start.10 = (bf16[256,2048]{1,0:T(8,128)(2,1)}, bf16[256,2048]{1,0:T(8,128)(2,1)}, u32[]{:S(2)}, u32[]{:S(2)}) collective-permute-start(bf16[256,2048]{1,0:T(8,128)(2,1)} %get-tuple-element.35), channel_id=1, source_target_pairs={{0,32},{8,40},{16,48},{24,56},{32,0},{40,8},{48,16},{56,24},{64,96... | collective-permute-start | bytes 3145736 | tf_op jit(solution)/shard_map/ppermute | solution.py:435
  75.3 0.0 collective-permute-done.5.refs_3_
  75.3 1.2 %collective-permute-start.11 = (bf16[256,2048]{1,0:T(8,128)(2,1)}, bf16[256,2048]{1,0:T(8,128)(2,1)}, u32[]{:S(2)}, u32[]{:S(2)}) collective-permute-start(bf16[256,2048]{1,0:T(8,128)(2,1)} %get-tuple-element.29), channel_id=1, source_target_pairs={{0,64},{8,72},{16,80},{24,88},{32,96},{40,104},{48,112},{56,120},{... | collective-permute-start | bytes 3145736 | tf_op jit(solution)/shard_map/ppermute | solution.py:435
  76.5 6.9 %input_partial.1 = (bf16[8,128,512]{2,1,0:T(8,128)(2,1)S(1)}, f32[128,512]{1,0:T(8,128)}) custom-call(bf16[16,160,128]{2,1,0:T(8,128)(2,1)S(1)} %all-to-all-done.1.r_ref, bf16[3,4096,512]{2,1,0:T(8,128)(2,1)} %bitcast.19), custom_call_target="tpu_custom_call" | custom-call | flops 1610612736 | bytes 14680064 | tf_op jit(solution)/shard_map/input_partial/pallas_call | solution.py:257
  83.4 0.0 copy-done
  83.4 1.0 copy-done.3
  84.4 0.0 collective-permute-done.3.refs_1_
  84.4 1.3 %collective-permute-start.7 = (bf16[8,2,128,128]{3,2,1,0:T(8,128)(2,1)}, bf16[8,2,128,128]{3,2,1,0:T(8,128)(2,1)S(1)}, u32[]{:S(2)}, u32[]{:S(2)}) collective-permute-start(bf16[8,2,128,128]{3,2,1,0:T(8,128)(2,1)} %collective-permute-done.3.refs_1_), channel_id=1, source_target_pairs={{0,8},{8,0},{16,24},{24,16},{32,40},{40,32},{48,56},{56,48},{64,72... | collective-permute-start | bytes 1572872 | tf_op jit(solution)/shard_map/ppermute | solution.py:424
  85.7 0.0 collective-permute-done.4.refs_2_
  85.7 0.1 collective-permute-start.8
  85.8 0.0 collective-permute-done.6.refs_4_
  85.8 0.4 collective-permute-start.9
  86.2 3.6 %all-to-all-start.2 = ((bf16[8,128,512]{2,1,0:T(8,128)(2,1)}), bf16[8,128,512]{2,1,0:T(8,128)(2,1)S(1)}, u32[]{:S(2)}, u32[]{:S(2)}) async-start(bf16[8,128,512]{2,1,0:T(8,128)(2,1)} %copy-done.3), calls=%async_computation.2 | async-start | bytes 2097152 | tf_op jit(solution)/shard_map/all_to_all | solution.py:428
  89.8 0.1 stack.55.place_ref
  89.9 0.0 collective-permute-done.7.refs_5_
  89.9 0.0 collective-permute-done.8.refs_6_
  89.9 0.0 copy-start.8
  89.9 0.0 collective-permute-done.9.refs_7_
  89.9 7.8 %collective-permute-done.10.refs_12_.refs_15_ = bf16[256,2048]{1,0:T(8,128)(2,1)} collective-permute-done((bf16[256,2048]{1,0:T(8,128)(2,1)}, bf16[256,2048]{1,0:T(8,128)(2,1)}, u32[]{:S(2)}, u32[]{:S(2)}) %collective-permute-start.10) | collective-permute-done | bytes 1048608 | tf_op jit(solution)/shard_map/ppermute | solution.py:435
  97.7 2.4 %collective-permute-done.11.refs_13_.refs_14_ = bf16[256,2048]{1,0:T(8,128)(2,1)} collective-permute-done((bf16[256,2048]{1,0:T(8,128)(2,1)}, bf16[256,2048]{1,0:T(8,128)(2,1)}, u32[]{:S(2)}, u32[]{:S(2)}) %collective-permute-start.11) | collective-permute-done | bytes 1048608 | tf_op jit(solution)/shard_map/ppermute | solution.py:435
  100.2 7.5 %weight_gradients.1 = (f32[3,256,512]{2,1,0:T(8,128)}, f32[512,256]{1,0:T(8,128)}, bf16[1024,256]{1,0:T(8,128)(2,1)S(1)}) custom-call(s32[13]{0:T(128)S(1)} %stack.55.place_ref, bf16[8,2,128,128]{3,2,1,0:T(8,128)(2,1)S(1)} %get-tuple-element.32.refs_0_, bf16[8,2,128,128]{3,2,1,0:T(8,128)(2,1)} %collective-permute-done.3.refs_1_, ...), custom_call_target="tpu_custom_call" | custom-call | tf_op jit(solution)/shard_map/weight_gradients/pallas_call | solution.py:367
  107.6 4.7 %collective-permute-start.12 = (bf16[1024,256]{1,0:T(8,128)(2,1)S(1)}, bf16[1024,256]{1,0:T(8,128)(2,1)S(1)}, u32[]{:S(2)}, u32[]{:S(2)}) collective-permute-start(bf16[1024,256]{1,0:T(8,128)(2,1)S(1)} %get-tuple-element.36), channel_id=1, source_target_pairs={{0,8},{8,0},{16,24},{24,16},{32,40},{40,32},{48,56},{56,48},{64,72... | collective-permute-start | bytes 1572872 | tf_op jit(solution)/shard_map/ppermute | solution.py:424
  112.3 0.0 all-to-all-done.2.p_ref
  112.3 0.8 sum_partials.1
  113.1 0.7 collective-permute-done.12.s_ref
  113.8 1.6 %fill_halves.1 = (f32[3,256,512]{2,1,0:T(8,128)}, f32[512,256]{1,0:T(8,128)}) custom-call(s32[13]{0:T(128)S(1)} %stack.55.place_ref, bf16[1024,256]{1,0:T(8,128)(2,1)S(1)} %collective-permute-done.12.s_ref, f32[3,256,512]{2,1,0:T(8,128)} %get-tuple-element.37.in_old, f32[512,256]{1,0:T(8,128)} %get-tuple-element.38.out_old), custom_call_target="tpu_custom_call", output_to_operand_aliasing={{0}: (2, {}), {1}: (3, {})} | custom-call | tf_op jit(solution)/shard_map/fill_halves/pallas_call | solution.py:403
  (9 shorter events, 0.0 us)
Async XLA Ops:
  0.6 35.8 %copy-start.4 = (bf16[2048,2048]{1,0:T(8,128)(2,1)S(1)}, bf16[2048,2048]{1,0:T(8,128)(2,1)}, u32[]{:S(2)}) copy-start(bf16[2048,2048]{1,0:T(8,128)(2,1)} %constant.31.clone.m_ref) | copy-start | bytes 25165828
  8.3 28.1 %copy-start.5 = (bf16[256,256]{1,0:T(8,128)(2,1)S(1)}, bf16[256,256]{1,0:T(8,128)(2,1)}, u32[]{:S(2)}) copy-start(bf16[256,256]{1,0:T(8,128)(2,1)} %constant.30.clone.j_ref) | copy-start | bytes 393220
  8.4 28.1 %copy-start.6 = (f32[8,2048]{1,0:T(8,128)S(1)}, f32[8,2048]{1,0:T(8,128)}, u32[]{:S(2)}) copy-start(f32[8,2048]{1,0:T(8,128)} %constant.32.clone.w_ref) | copy-start | bytes 196612
  41.9 29.0 %all-to-all-start.1 = ((bf16[16,160,128]{2,1,0:T(8,128)(2,1)}), bf16[16,160,128]{2,1,0:T(8,128)(2,1)S(1)}, u32[]{:S(2)}, u32[]{:S(2)}) async-start(bf16[16,160,128]{2,1,0:T(8,128)(2,1)} %get-tuple-element.24), calls=%async_computation.1 | async-start | bytes 1310720 | tf_op jit(solution)/shard_map/all_to_all | solution.py:428
  45.9 22.2 %collective-permute-start.2 = (bf16[128,2048]{1,0:T(8,128)(2,1)S(1)}, bf16[128,2048]{1,0:T(8,128)(2,1)S(1)}, u32[]{:S(2)}, u32[]{:S(2)}) collective-permute-start(bf16[128,2048]{1,0:T(8,128)(2,1)S(1)} %get-tuple-element.23.c.refs_8_), channel_id=1, source_target_pairs={{0,64},{8,72},{16,80},{24,88},{32,96},{40,104},{48,112},{56,120},{... | collective-permute-start | bytes 1572872 | tf_op jit(solution)/shard_map/ppermute | solution.py:435
  48.9 20.5 %collective-permute-start.1 = (bf16[128,2048]{1,0:T(8,128)(2,1)S(1)}, bf16[128,2048]{1,0:T(8,128)(2,1)S(1)}, u32[]{:S(2)}, u32[]{:S(2)}) collective-permute-start(bf16[128,2048]{1,0:T(8,128)(2,1)S(1)} %get-tuple-element.23.c.refs_8_), channel_id=1, source_target_pairs={{0,48},{8,56},{16,0},{24,8},{32,16},{40,24},{48,32},{56,40},{64,11... | collective-permute-start | bytes 1572872 | tf_op jit(solution)/shard_map/ppermute | solution.py:435
  51.3 19.6 %collective-permute-start = (bf16[128,2048]{1,0:T(8,128)(2,1)S(1)}, bf16[128,2048]{1,0:T(8,128)(2,1)S(1)}, u32[]{:S(2)}, u32[]{:S(2)}) collective-permute-start(bf16[128,2048]{1,0:T(8,128)(2,1)S(1)} %get-tuple-element.23.c.refs_8_), channel_id=1, source_target_pairs={{0,16},{8,24},{16,32},{24,40},{32,48},{40,56},{48,0},{56,8},{64,80... | collective-permute-start | bytes 1572872 | tf_op jit(solution)/shard_map/ppermute | solution.py:435
  51.3 23.9 %collective-permute-start.5 = (bf16[8,2,128,128]{3,2,1,0:T(8,128)(2,1)S(1)}, bf16[8,2,128,128]{3,2,1,0:T(8,128)(2,1)}, u32[]{:S(2)}, u32[]{:S(2)}) collective-permute-start(bf16[8,2,128,128]{3,2,1,0:T(8,128)(2,1)S(1)} %get-tuple-element.32.refs_0_), channel_id=1, source_target_pairs={{0,2},{1,3},{2,0},{3,1},{4,6},{5,7},{6,4},{7,5},{8,10},{9,11},{10,... | collective-permute-start | bytes 1572872 | tf_op jit(solution)/shard_map/ppermute | solution.py:443
  54.2 31.5 %collective-permute-start.6 = (bf16[8,2,128,128]{3,2,1,0:T(8,128)(2,1)S(1)}, bf16[8,2,128,128]{3,2,1,0:T(8,128)(2,1)}, u32[]{:S(2)}, u32[]{:S(2)}) collective-permute-start(bf16[8,2,128,128]{3,2,1,0:T(8,128)(2,1)S(1)} %get-tuple-element.32.refs_0_), channel_id=1, source_target_pairs={{0,8},{8,0},{16,24},{24,16},{32,40},{40,32},{48,56},{56,48},{64,72... | collective-permute-start | bytes 1572872 | tf_op jit(solution)/shard_map/ppermute | solution.py:424
  68.1 15.3 %copy-start = (bf16[128,2048]{1,0:T(8,128)(2,1)}, bf16[128,2048]{1,0:T(8,128)(2,1)S(1)}, u32[]{:S(2)}) copy-start(bf16[128,2048]{1,0:T(8,128)(2,1)S(1)} %collective-permute-done.2.d.refs_11_) | copy-start | bytes 1572868
  68.1 16.3 %collective-permute-start.3 = (bf16[8,2,128,128]{3,2,1,0:T(8,128)(2,1)S(1)}, bf16[8,2,128,128]{3,2,1,0:T(8,128)(2,1)}, u32[]{:S(2)}, u32[]{:S(2)}) collective-permute-start(bf16[8,2,128,128]{3,2,1,0:T(8,128)(2,1)S(1)} %get-tuple-element.32.refs_0_), channel_id=1, source_target_pairs={{0,1},{1,2},{2,3},{3,0},{4,5},{5,6},{6,7},{7,4},{8,9},{9,10},{10,1... | collective-permute-start | bytes 1572872 | tf_op jit(solution)/shard_map/ppermute | solution.py:443
  69.4 14.0 %copy-start.1 = (bf16[128,2048]{1,0:T(8,128)(2,1)}, bf16[128,2048]{1,0:T(8,128)(2,1)S(1)}, u32[]{:S(2)}) copy-start(bf16[128,2048]{1,0:T(8,128)(2,1)S(1)} %collective-permute-done.1.b.refs_10_) | copy-start | bytes 1572868
  69.4 16.3 %collective-permute-start.4 = (bf16[8,2,128,128]{3,2,1,0:T(8,128)(2,1)S(1)}, bf16[8,2,128,128]{3,2,1,0:T(8,128)(2,1)}, u32[]{:S(2)}, u32[]{:S(2)}) collective-permute-start(bf16[8,2,128,128]{3,2,1,0:T(8,128)(2,1)S(1)} %get-tuple-element.32.refs_0_), channel_id=1, source_target_pairs={{0,3},{1,0},{2,1},{3,2},{4,7},{5,4},{6,5},{7,6},{8,11},{9,8},{10,9... | collective-permute-start | bytes 1572872 | tf_op jit(solution)/shard_map/ppermute | solution.py:443
  70.9 12.5 %copy-start.2 = (bf16[128,2048]{1,0:T(8,128)(2,1)}, bf16[128,2048]{1,0:T(8,128)(2,1)S(1)}, u32[]{:S(2)}) copy-start(bf16[128,2048]{1,0:T(8,128)(2,1)S(1)} %collective-permute-done.a.refs_9_) | copy-start | bytes 1572868
  72.5 25.3 %collective-permute-start.10 = (bf16[256,2048]{1,0:T(8,128)(2,1)}, bf16[256,2048]{1,0:T(8,128)(2,1)}, u32[]{:S(2)}, u32[]{:S(2)}) collective-permute-start(bf16[256,2048]{1,0:T(8,128)(2,1)} %get-tuple-element.35), channel_id=1, source_target_pairs={{0,32},{8,40},{16,48},{24,56},{32,0},{40,8},{48,16},{56,24},{64,96... | collective-permute-start | bytes 3145736 | tf_op jit(solution)/shard_map/ppermute | solution.py:435
  75.3 24.9 %collective-permute-start.11 = (bf16[256,2048]{1,0:T(8,128)(2,1)}, bf16[256,2048]{1,0:T(8,128)(2,1)}, u32[]{:S(2)}, u32[]{:S(2)}) collective-permute-start(bf16[256,2048]{1,0:T(8,128)(2,1)} %get-tuple-element.29), channel_id=1, source_target_pairs={{0,64},{8,72},{16,80},{24,88},{32,96},{40,104},{48,112},{56,120},{... | collective-permute-start | bytes 3145736 | tf_op jit(solution)/shard_map/ppermute | solution.py:435
  83.4 1.0 copy-start.3
  84.4 5.5 %collective-permute-start.7 = (bf16[8,2,128,128]{3,2,1,0:T(8,128)(2,1)}, bf16[8,2,128,128]{3,2,1,0:T(8,128)(2,1)S(1)}, u32[]{:S(2)}, u32[]{:S(2)}) collective-permute-start(bf16[8,2,128,128]{3,2,1,0:T(8,128)(2,1)} %collective-permute-done.3.refs_1_), channel_id=1, source_target_pairs={{0,8},{8,0},{16,24},{24,16},{32,40},{40,32},{48,56},{56,48},{64,72... | collective-permute-start | bytes 1572872 | tf_op jit(solution)/shard_map/ppermute | solution.py:424
  85.7 4.2 %collective-permute-start.8 = (bf16[8,2,128,128]{3,2,1,0:T(8,128)(2,1)}, bf16[8,2,128,128]{3,2,1,0:T(8,128)(2,1)S(1)}, u32[]{:S(2)}, u32[]{:S(2)}) collective-permute-start(bf16[8,2,128,128]{3,2,1,0:T(8,128)(2,1)} %collective-permute-done.4.refs_2_), channel_id=1, source_target_pairs={{0,8},{8,0},{16,24},{24,16},{32,40},{40,32},{48,56},{56,48},{64,72... | collective-permute-start | bytes 1572872 | tf_op jit(solution)/shard_map/ppermute | solution.py:424
  85.8 4.1 %collective-permute-start.9 = (bf16[8,2,128,128]{3,2,1,0:T(8,128)(2,1)}, bf16[8,2,128,128]{3,2,1,0:T(8,128)(2,1)}, u32[]{:S(2)}, u32[]{:S(2)}) collective-permute-start(bf16[8,2,128,128]{3,2,1,0:T(8,128)(2,1)} %collective-permute-done.5.refs_3_), channel_id=1, source_target_pairs={{0,8},{8,0},{16,24},{24,16},{32,40},{40,32},{48,56},{56,48},{64,72... | collective-permute-start | bytes 1572872 | tf_op jit(solution)/shard_map/ppermute | solution.py:424
  86.2 26.1 %all-to-all-start.2 = ((bf16[8,128,512]{2,1,0:T(8,128)(2,1)}), bf16[8,128,512]{2,1,0:T(8,128)(2,1)S(1)}, u32[]{:S(2)}, u32[]{:S(2)}) async-start(bf16[8,128,512]{2,1,0:T(8,128)(2,1)} %copy-done.3), calls=%async_computation.2 | async-start | bytes 2097152 | tf_op jit(solution)/shard_map/all_to_all | solution.py:428
  89.9 10.3 %copy-start.7 = (bf16[8,2,128,128]{3,2,1,0:T(8,128)(2,1)}, bf16[8,2,128,128]{3,2,1,0:T(8,128)(2,1)S(1)}, u32[]{:S(2)}) copy-start(bf16[8,2,128,128]{3,2,1,0:T(8,128)(2,1)S(1)} %collective-permute-done.7.refs_5_) | copy-start | bytes 1572868
  89.9 7.8 %copy-start.8 = (bf16[8,2,128,128]{3,2,1,0:T(8,128)(2,1)}, bf16[8,2,128,128]{3,2,1,0:T(8,128)(2,1)S(1)}, u32[]{:S(2)}) copy-start(bf16[8,2,128,128]{3,2,1,0:T(8,128)(2,1)S(1)} %collective-permute-done.8.refs_6_) | copy-start | bytes 1572868
  107.6 6.2 %collective-permute-start.12 = (bf16[1024,256]{1,0:T(8,128)(2,1)S(1)}, bf16[1024,256]{1,0:T(8,128)(2,1)S(1)}, u32[]{:S(2)}, u32[]{:S(2)}) collective-permute-start(bf16[1024,256]{1,0:T(8,128)(2,1)S(1)} %get-tuple-element.36), channel_id=1, source_target_pairs={{0,8},{8,0},{16,24},{24,16},{32,40},{40,32},{48,56},{56,48},{64,72... | collective-permute-start | bytes 1572872 | tf_op jit(solution)/shard_map/ppermute | solution.py:424

commit v4 on v3

--- a/solution.py
+++ b/solution.py
@@ -314,40 +314,94 @@
     )(first, second, third, fourth)
 
 
-def weight_gradients(place, columns, blocks):
+def gather_columns(place_ref, column_refs, t_ref, t_sem):
+    core = place_ref[8]
+    copies = []
+    for i in range(8):
+        lanes = pl.ds(pl.multiple_of(place_ref[9 + i % 4] * 128, 128), 128)
+        kind = core if i < 4 else 1 - core
+        for c in range(2):
+            src = column_refs[i].at[:, c]
+            copies.append(pltpu.make_async_copy(src, t_ref.at[kind, c, :, :, lanes], t_sem.at[c, i]))
+    return copies
+
+
+def gather_blocks(block_refs, first_rows, g_ref, sem):
+    copies = [[], [], [], []]
+    for j in range(4):
+        for k in range(4):
+            src = block_refs[k].at[pl.ds(first_rows[k] + j * BLOCK, BLOCK)]
+            copies[j].append(pltpu.make_async_copy(src, g_ref.at[j, pl.ds(k * BLOCK, BLOCK)], sem.at[j, k]))
+    return copies
+
+
+COLUMN_SCRATCH = (
+    pltpu.VMEM((2, 2, 8, SEQ_DEV, 512), BF16),
+    pltpu.VMEM((4, 128, SEQ), BF16),
+    pltpu.SemaphoreType.DMA((2, 8)),
+    pltpu.SemaphoreType.DMA((4, 4)),
+)
+
+
+def first_products(place, columns, blocks):
+    first_rows = [first for _, first in blocks]
+
+    def kernel(place_ref, *refs):
+        o_ref, t_hbm, t_ref, g_ref, t_sem, sem, out_sem = refs[12:]
+        t_copies = gather_columns(place_ref, refs[:8], t_ref, t_sem)
+        copies = gather_blocks(refs[8:12], first_rows, g_ref, sem)
+        for copy in t_copies + copies[0] + copies[1] + copies[2] + copies[3]:
+            copy.start()
+        for j in range(4):
+            for copy in copies[j] + (t_copies if j == 0 else []):
+                copy.wait()
+            if j == 0:
+                keep = pltpu.make_async_copy(t_ref, t_hbm, out_sem)
+                keep.start()
+            o_ref[j] = dot(g_ref[j], t_ref[j // 3].reshape(SEQ, 512))
+        keep.wait()
+
+    hbm = pl.BlockSpec(memory_space=pl.ANY)
+    return call(
+        kernel,
+        in_specs=[pl.BlockSpec(memory_space=pltpu.SMEM)] + [hbm] * 12,
+        out_specs=[pl.BlockSpec(memory_space=pltpu.VMEM), hbm],
+        out_shape=[
+            jax.ShapeDtypeStruct((4, 128, 512), F32),
+            jax.ShapeDtypeStruct((2, 2, 8, SEQ_DEV, 512), BF16),
+        ],
+        scratch_shapes=list(COLUMN_SCRATCH) + [pltpu.SemaphoreType.DMA],
+        vmem=16,
+        name="first_products",
+    )(place, columns[0], *map(in_hbm, columns[1:]), blocks[0][0], *[in_hbm(block) for block, _ in blocks[1:]])
+
+
+def weight_gradients(place, columns, products, blocks):
     factor = 1.0 / math.sqrt(SEQ)
     first_rows = [first for _, first in blocks]
 
-    def kernel(place_ref, *refs):
-        column_refs, block_refs = refs[:8], refs[8:16]
-        in_hbm, out_hbm, send_ref, t_ref, g_ref, res_ref, t_sem, sem, out_sem = refs[16:]
+    def kernel(place_ref, p_ref, *refs):
+        t_hbm, in_hbm, out_hbm, send_ref, t_ref, g_ref, t_sem, sem, all_ref, res_ref, out_sem = refs[4:]
         core = place_ref[8]
-        t_copies = []
-        for i in range(8):
-            lanes = pl.ds(pl.multiple_of(place_ref[9 + i % 4] * 128, 128), 128)
-            kind = core if i < 4 else 1 - core
-            for c in range(2):
-                src = column_refs[i].at[:, c]
-                t_copies.append(pltpu.make_async_copy(src, t_ref.at[kind, c, :, :, lanes], t_sem.at[c, i]))
-        copies = [[], [], [], []]
-        for j in range(4):
-            for k in range(8):
-                at = pl.multiple_of(place_ref[k] * BLOCK, BLOCK)
-                copies[j].append(
-                    pltpu.make_async_copy(
-                        block_refs[k].at[pl.ds(first_rows[k] + j * BLOCK, BLOCK)], g_ref.at[j, pl.ds(at, BLOCK)], sem.at[j, k]
-                    )
-                )
-        for copy in t_copies + copies[0] + copies[1] + copies[2] + copies[3]:
+        t_copies = [pltpu.make_async_copy(t_hbm.at[i], t_ref.at[i], t_sem.at[i, 0]) for i in range(2)]
+        copies = gather_blocks(refs[:4], first_rows, g_ref, sem)
+        for copy in [t_copies[0]] + copies[0] + copies[1] + copies[2] + [t_copies[1]] + copies[3]:
             copy.start()
         half = pl.multiple_of(core * 256, 256)
         rest = pl.multiple_of((1 - core) * 256, 256)
+        for j in range(4):
+            for k in range(4):
+                at = pl.multiple_of(place_ref[k] * BLOCK, BLOCK)
+                all_ref[j, pl.ds(at, BLOCK), :] = p_ref[j, k * BLOCK : (k + 1) * BLOCK, :]
         outs = []
         for j in range(4):
-            for copy in copies[j] + (t_copies if j == 0 else []):
+            for copy in copies[j] + ([t_copies[j // 3]] if j % 3 == 0 else []):
                 copy.wait()
-            total = dot(g_ref[j], t_ref[j // 3].reshape(SEQ, 512))
-            total = total * factor
+            more = dot(g_ref[j], t_ref[j // 3].reshape(SEQ, 512))
+            for k in range(4):
+                at = pl.multiple_of(place_ref[4 + k] * BLOCK, BLOCK)
+                all_ref[j, pl.ds(at, BLOCK), :] = more[k * BLOCK : (k + 1) * BLOCK]
+            total = all_ref[j] * factor
             if j < 3:
                 res_ref[j] = total.T
                 send_ref[j * 256 : (j + 1) * 256, :] = res_ref[j, pl.ds(rest, 256), :].astype(BF16)
@@ -366,24 +420,22 @@
     hbm = pl.BlockSpec(memory_space=pl.ANY)
     return call(
         kernel,
-        in_specs=[pl.BlockSpec(memory_space=pltpu.SMEM)] + [hbm] * 16,
+        in_specs=[pl.BlockSpec(memory_space=pltpu.SMEM), vm] + [hbm] * 5,
         out_specs=[hbm, hbm, vm],
         out_shape=[
             jax.ShapeDtypeStruct((3, 256, 512), F32),
             jax.ShapeDtypeStruct((512, 256), F32),
             jax.ShapeDtypeStruct((1024, 256), BF16),
         ],
-        scratch_shapes=[
-            pltpu.VMEM((2, 2, 8, SEQ_DEV, 512), BF16),
-            pltpu.VMEM((4, 256, SEQ), BF16),
+        scratch_shapes=list(COLUMN_SCRATCH)
+        + [
+            pltpu.VMEM((4, 256, 512), F32),
             pltpu.VMEM((4, 512, 256), F32),
-            pltpu.SemaphoreType.DMA((2, 8)),
-            pltpu.SemaphoreType.DMA((4, 8)),
             pltpu.SemaphoreType.DMA((4,)),
         ],
         vmem=24,
         name="weight_gradients",
-    )(place, columns[0], *map(in_hbm, columns[1:]), blocks[0][0], *[in_hbm(block) for block, _ in blocks[1:]])
+    )(place, products, *[in_hbm(block) for block, _ in blocks], in_hbm(columns))
 
 
 def fill_halves(place, sent, in_grad, out_grad):
@@ -469,7 +521,8 @@
     columns += [swap_cores(value) for value in columns]
     input_grad = sum_partials(parts)
     blocks = [(block, 0), (up, 0), (down, 0), (flipped, 0), (two, 0), (across, 0), (across, 128), (two, 128)]
-    in_grad, out_weight_grad, send = weight_gradients(place, columns, blocks)
+    products, columns = first_products(place, columns, blocks[:4])
+    in_grad, out_weight_grad, send = weight_gradients(place, columns, products, blocks[4:])
     in_grad, out_weight_grad = fill_halves(place, swap_cores(send), in_grad, out_weight_grad)
     return (input_grad, jnp.transpose(in_grad, (1, 0, 2)), out_weight_grad, filter_grad)
 

time: 116 us -> 115 us (level)
  waiting for transfers between devices: 23.7 us -> 15.5 us
  Pallas kernels: 31.3 us -> 35.4 us
  local copies, waits for them, and re-layouts: 1.11 us -> 4.08 us
    ppermute x5, waiting for transfers between devices: 22.9 us -> 14.7 us  [hop(): return lax.ppermute(value, 'ctx', chip_hop(x_flip, z_step))]
    pallas_call x1 -> x2, Pallas kernels: 7.46 us -> 11.5 us  [the longest x1 6.35 us: weight_gradients(): call(kernel, in_specs=[pl.BlockSpec(memory_space=pltpu.SMEM), vm] + [hbm]...]
    unnamed x18 -> x20, local copies, waits for them, and re-layouts: 1.02 us -> 4 us
  transfers between devices with their start and end apart: 15 -> 15, of which waited for: 4 -> 3; matrix products, arithmetic and copies ran while one was open for 0% -> 0% of each run, Pallas kernels for 14% -> 18%
where the time goes in v4:
time: 115 us; the launch traced here: 114 us
  Pallas kernels  35.4 us (31%)
  starting transfers between devices  30.3 us (26%)
  blocking collectives  28.1 us (24%)
  waiting for transfers between devices  15.5 us (13%)
  local copies, waits for them, and re-layouts  4.08 us (4%)
    all_to_all x1, blocking collectives, swap(): lax.all_to_all(pieces, axis, 0, 0, axis_index_groups=groups, tiled=True)  28.1 us
    ppermute x5, waiting for transfers between devices, hop(): return lax.ppermute(value, 'ctx', chip_hop(x_flip, z_step))  14.7 us
    ppermute x5, starting transfers between devices, hop(): return lax.ppermute(value, 'ctx', chip_hop(x_flip, z_step))  9.36 us
    pallas_call x1, Pallas kernels, project(): call(kernel, in_specs=[pl.BlockSpec(memory_space=pltpu.SMEM)] + [hbm] * 5...  7.68 us
    ppermute x5, starting transfers between devices, swap_cores(): return lax.ppermute(value, 'ctx', [(i, i ^ 1) for i in range(16)])  7.67 us
    all_to_all x2, starting transfers between devices, swap(): lax.all_to_all(pieces, axis, 0, 0, axis_index_groups=groups, tiled=True)  7.6 us
    pallas_call x1, Pallas kernels, input_partial(): call(kernel, in_specs=[vm, pl.BlockSpec(memory_space=pl.ANY)], out_specs=...  6.91 us
    pallas_call x1, Pallas kernels, weight_gradients(): call(kernel, in_specs=[pl.BlockSpec(memory_space=pltpu.SMEM), vm] + [hbm]...  6.35 us
  transfers between devices with their start and end apart: 15, of which 3 were waited for; matrix products, arithmetic and copies ran while one was open for 0% of the time, Pallas kernels for 18%

profile of v4, /device:TPU:1, one launch (start us, length us, event | category | flops | bytes accessed | tf_op | source)
XLA Modules:
  0.0 114.5 jit_solution(4922242016391774936)
XLA Ops:
  0.6 0.0 copy-start.5
  0.7 0.0 copy-start.6
  0.7 0.0 copy-start.7
  0.7 7.7 %project.1 = bf16[8,2,288,128]{3,2,1,0:T(8,128)(2,1)S(1)} custom-call(s32[1]{0:T(128)} %bitcast.y_ref, bf16[128,4096]{1,0:T(8,128)(2,1)} %t_hbm.1, bf16[128,4096]{1,0:T(8,128)(2,1)} %g_hbm.1, f32[128,512]{1,0:T(8,128)} %f_hbm.1, bf16[3,4096,512]{2,1,0:T(8,128)(2,1)} %bitcast.18, bf16[512,4096]{1,0:T(8,128)(2,1)} %ow_hbm.1), custom_call_target="tpu_custom_call" | custom-call | flops 2147483648 | bytes 19922944 | tf_op jit(solution)/shard_map/project/pallas_call | solution.py:111
  8.4 28.1 %all_to_all.15.r_ref = bf16[16,288,128]{2,1,0:T(8,128)(2,1)S(1)} all-to-all(bf16[16,288,128]{2,1,0:T(8,128)(2,1)S(1)} %bitcast.17), channel_id=1, replica_groups=mesh['ctx'=16,'mp'=8] {'ctx'}, dimensions={0} | all-to-all | bytes 2359296 | tf_op jit(solution)/shard_map/all_to_all | solution.py:480
  36.5 5.4 %convolve.1 = (bf16[128,2048]{1,0:T(8,128)(2,1)S(1)}, bf16[16,160,128]{2,1,0:T(8,128)(2,1)}, bf16[8,2,128,128]{3,2,1,0:T(8,128)(2,1)S(1)}) custom-call(bf16[16,288,128]{2,1,0:T(8,128)(2,1)S(1)} %all_to_all.15.r_ref, bf16[2048,2048]{1,0:T(8,128)(2,1)S(1)} %copy-done.5, f32[8,2048]{1,0:T(8,128)S(1)} %copy-done.7, bf16[256,256]{1,0:T(8,128)(2,1)S(1)} %copy-done.6), custom_call_target="tpu_custom_call" | custom-call | flops 3221225472 | bytes 12582912 | tf_op jit(solution)/shard_map/convolve/pallas_call | solution.py:208
  41.9 4.0 %all-to-all-start.1 = ((bf16[16,160,128]{2,1,0:T(8,128)(2,1)}), bf16[16,160,128]{2,1,0:T(8,128)(2,1)S(1)}, u32[]{:S(2)}, u32[]{:S(2)}) async-start(bf16[16,160,128]{2,1,0:T(8,128)(2,1)} %get-tuple-element.26), calls=%async_computation.1 | async-start | bytes 1310720 | tf_op jit(solution)/shard_map/all_to_all | solution.py:480
  45.9 2.9 %collective-permute-start.2 = (bf16[128,2048]{1,0:T(8,128)(2,1)S(1)}, bf16[128,2048]{1,0:T(8,128)(2,1)S(1)}, u32[]{:S(2)}, u32[]{:S(2)}) collective-permute-start(bf16[128,2048]{1,0:T(8,128)(2,1)S(1)} %get-tuple-element.25.c.refs_8_), channel_id=1, source_target_pairs={{0,64},{8,72},{16,80},{24,88},{32,96},{40,104},{48,112},{56,120},{... | collective-permute-start | bytes 1572872 | tf_op jit(solution)/shard_map/ppermute | solution.py:487
  48.9 2.4 %collective-permute-start.1 = (bf16[128,2048]{1,0:T(8,128)(2,1)S(1)}, bf16[128,2048]{1,0:T(8,128)(2,1)S(1)}, u32[]{:S(2)}, u32[]{:S(2)}) collective-permute-start(bf16[128,2048]{1,0:T(8,128)(2,1)S(1)} %get-tuple-element.25.c.refs_8_), channel_id=1, source_target_pairs={{0,48},{8,56},{16,0},{24,8},{32,16},{40,24},{48,32},{56,40},{64,11... | collective-permute-start | bytes 1572872 | tf_op jit(solution)/shard_map/ppermute | solution.py:487
  51.3 0.0 collective-permute-start
  51.3 2.9 %collective-permute-start.5 = (bf16[8,2,128,128]{3,2,1,0:T(8,128)(2,1)S(1)}, bf16[8,2,128,128]{3,2,1,0:T(8,128)(2,1)}, u32[]{:S(2)}, u32[]{:S(2)}) collective-permute-start(bf16[8,2,128,128]{3,2,1,0:T(8,128)(2,1)S(1)} %get-tuple-element.34.refs_0_), channel_id=1, source_target_pairs={{0,2},{1,3},{2,0},{3,1},{4,6},{5,7},{6,4},{7,5},{8,10},{9,11},{10,... | collective-permute-start | bytes 1572872 | tf_op jit(solution)/shard_map/ppermute | solution.py:495
  54.2 1.2 %collective-permute-start.6 = (bf16[8,2,128,128]{3,2,1,0:T(8,128)(2,1)S(1)}, bf16[8,2,128,128]{3,2,1,0:T(8,128)(2,1)}, u32[]{:S(2)}, u32[]{:S(2)}) collective-permute-start(bf16[8,2,128,128]{3,2,1,0:T(8,128)(2,1)S(1)} %get-tuple-element.34.refs_0_), channel_id=1, source_target_pairs={{0,8},{8,0},{16,24},{24,16},{32,40},{40,32},{48,56},{56,48},{64,72... | collective-permute-start | bytes 1572872 | tf_op jit(solution)/shard_map/ppermute | solution.py:476
  55.4 12.7 %collective-permute-done.2.d.refs_11_ = bf16[128,2048]{1,0:T(8,128)(2,1)S(1)} collective-permute-done((bf16[128,2048]{1,0:T(8,128)(2,1)S(1)}, bf16[128,2048]{1,0:T(8,128)(2,1)S(1)}, u32[]{:S(2)}, u32[]{:S(2)}) %collective-permute-start.2) | collective-permute-done | bytes 524320 | tf_op jit(solution)/shard_map/ppermute | solution.py:487
  68.1 1.3 %collective-permute-start.3 = (bf16[8,2,128,128]{3,2,1,0:T(8,128)(2,1)S(1)}, bf16[8,2,128,128]{3,2,1,0:T(8,128)(2,1)}, u32[]{:S(2)}, u32[]{:S(2)}) collective-permute-start(bf16[8,2,128,128]{3,2,1,0:T(8,128)(2,1)S(1)} %get-tuple-element.34.refs_0_), channel_id=1, source_target_pairs={{0,1},{1,2},{2,3},{3,0},{4,5},{5,6},{6,7},{7,4},{8,9},{9,10},{10,1... | collective-permute-start | bytes 1572872 | tf_op jit(solution)/shard_map/ppermute | solution.py:495
  69.4 0.0 collective-permute-done.1.b.refs_10_
  69.4 1.5 %collective-permute-start.4 = (bf16[8,2,128,128]{3,2,1,0:T(8,128)(2,1)S(1)}, bf16[8,2,128,128]{3,2,1,0:T(8,128)(2,1)}, u32[]{:S(2)}, u32[]{:S(2)}) collective-permute-start(bf16[8,2,128,128]{3,2,1,0:T(8,128)(2,1)S(1)} %get-tuple-element.34.refs_0_), channel_id=1, source_target_pairs={{0,3},{1,0},{2,1},{3,2},{4,7},{5,4},{6,5},{7,6},{8,11},{9,8},{10,9... | collective-permute-start | bytes 1572872 | tf_op jit(solution)/shard_map/ppermute | solution.py:495
  70.9 0.0 collective-permute-done.a.refs_9_
  70.9 0.0 all-to-all-done.1.r_ref
  70.9 1.5 %pair.1 = (bf16[256,2048]{1,0:T(8,128)(2,1)}, bf16[256,2048]{1,0:T(8,128)(2,1)}) custom-call(bf16[128,2048]{1,0:T(8,128)(2,1)S(1)} %collective-permute-done.a.refs_9_, bf16[128,2048]{1,0:T(8,128)(2,1)S(1)} %collective-permute-done.1.b.refs_10_, bf16[128,2048]{1,0:T(8,128)(2,1)S(1)} %get-tuple-element.25.c.refs_8_, ...), custom_call_target="tpu_custom_call" | custom-call | tf_op jit(solution)/shard_map/pair/pallas_call | solution.py:306
  72.5 2.8 %collective-permute-start.10 = (bf16[256,2048]{1,0:T(8,128)(2,1)}, bf16[256,2048]{1,0:T(8,128)(2,1)}, u32[]{:S(2)}, u32[]{:S(2)}) collective-permute-start(bf16[256,2048]{1,0:T(8,128)(2,1)} %get-tuple-element.38), channel_id=1, source_target_pairs={{0,32},{8,40},{16,48},{24,56},{32,0},{40,8},{48,16},{56,24},{64,96... | collective-permute-start | bytes 3145736 | tf_op jit(solution)/shard_map/ppermute | solution.py:487
  75.3 0.0 collective-permute-done.5.refs_3_
  75.3 1.2 %collective-permute-start.11 = (bf16[256,2048]{1,0:T(8,128)(2,1)}, bf16[256,2048]{1,0:T(8,128)(2,1)}, u32[]{:S(2)}, u32[]{:S(2)}) collective-permute-start(bf16[256,2048]{1,0:T(8,128)(2,1)} %get-tuple-element.31), channel_id=1, source_target_pairs={{0,64},{8,72},{16,80},{24,88},{32,96},{40,104},{48,112},{56,120},{... | collective-permute-start | bytes 3145736 | tf_op jit(solution)/shard_map/ppermute | solution.py:487
  76.5 6.9 %input_partial.1 = (bf16[8,128,512]{2,1,0:T(8,128)(2,1)S(1)}, f32[128,512]{1,0:T(8,128)}) custom-call(bf16[16,160,128]{2,1,0:T(8,128)(2,1)S(1)} %all-to-all-done.1.r_ref, bf16[3,4096,512]{2,1,0:T(8,128)(2,1)} %bitcast.19), custom_call_target="tpu_custom_call" | custom-call | flops 1610612736 | bytes 14680064 | tf_op jit(solution)/shard_map/input_partial/pallas_call | solution.py:257
  83.4 1.0 copy-done.4
  84.4 0.0 collective-permute-done.3.refs_1_
  84.4 1.3 %collective-permute-start.7 = (bf16[8,2,128,128]{3,2,1,0:T(8,128)(2,1)}, bf16[8,2,128,128]{3,2,1,0:T(8,128)(2,1)S(1)}, u32[]{:S(2)}, u32[]{:S(2)}) collective-permute-start(bf16[8,2,128,128]{3,2,1,0:T(8,128)(2,1)} %collective-permute-done.3.refs_1_), channel_id=1, source_target_pairs={{0,8},{8,0},{16,24},{24,16},{32,40},{40,32},{48,56},{56,48},{64,72... | collective-permute-start | bytes 1572872 | tf_op jit(solution)/shard_map/ppermute | solution.py:476
  85.7 0.0 collective-permute-done.4.refs_2_
  85.7 0.1 collective-permute-start.8
  85.8 0.0 collective-permute-done.6.refs_4_
  85.8 0.4 collective-permute-start.9
  86.2 3.6 %all-to-all-start.2 = ((bf16[8,128,512]{2,1,0:T(8,128)(2,1)}), bf16[8,128,512]{2,1,0:T(8,128)(2,1)S(1)}, u32[]{:S(2)}, u32[]{:S(2)}) async-start(bf16[8,128,512]{2,1,0:T(8,128)(2,1)} %copy-done.4), calls=%async_computation.2 | async-start | bytes 2097152 | tf_op jit(solution)/shard_map/all_to_all | solution.py:480
  89.8 0.1 stack.55.place_ref
  89.9 0.0 collective-permute-done.7.refs_5_
  89.9 0.0 copy-start.8
  89.9 0.0 collective-permute-done.8.refs_6_
  90.0 0.0 collective-permute-done.9.refs_7_
  90.0 0.8 copy-done.8
  90.7 0.2 copy-done.9
  91.0 5.2 %first_products.1 = (f32[4,128,512]{2,1,0:T(8,128)S(1)}, bf16[2,2,8,128,512]{4,3,2,1,0:T(8,128)(2,1)S(1)}) custom-call(s32[13]{0:T(128)S(1)} %stack.55.place_ref, bf16[8,2,128,128]{3,2,1,0:T(8,128)(2,1)S(1)} %get-tuple-element.34.refs_0_, bf16[8,2,128,128]{3,2,1,0:T(8,128)(2,1)} %collective-permute-done.3.refs_1_, ...), custom_call_target="tpu_custom_call" | custom-call | tf_op jit(solution)/shard_map/first_products/pallas_call | solution.py:365
  96.2 2.0 %copy-done = bf16[2,2,8,128,512]{4,3,2,1,0:T(8,128)(2,1)} copy-done((bf16[2,2,8,128,512]{4,3,2,1,0:T(8,128)(2,1)}, bf16[2,2,8,128,512]{4,3,2,1,0:T(8,128)(2,1)S(1)}, u32[]{:S(2)}) %copy-start) | copy-done | bytes 4194328
  98.1 0.0 collective-permute-done.10.refs_0_.refs_3_
  98.1 2.0 %collective-permute-done.11.refs_1_.refs_2_ = bf16[256,2048]{1,0:T(8,128)(2,1)} collective-permute-done((bf16[256,2048]{1,0:T(8,128)(2,1)}, bf16[256,2048]{1,0:T(8,128)(2,1)}, u32[]{:S(2)}, u32[]{:S(2)}) %collective-permute-start.11) | collective-permute-done | bytes 1048608 | tf_op jit(solution)/shard_map/ppermute | solution.py:487
  100.2 6.3 %weight_gradients.1 = (f32[3,256,512]{2,1,0:T(8,128)}, f32[512,256]{1,0:T(8,128)}, bf16[1024,256]{1,0:T(8,128)(2,1)S(1)}) custom-call(s32[13]{0:T(128)S(1)} %stack.55.place_ref, f32[4,128,512]{2,1,0:T(8,128)S(1)} %get-tuple-element.37.p_ref, bf16[256,2048]{1,0:T(8,128)(2,1)} %collective-permute-done.10.refs_0_.refs_3_, ...), custom_call_target="tpu_custom_call" | custom-call | tf_op jit(solution)/shard_map/weight_gradients/pallas_call | solution.py:421
  106.5 4.7 %collective-permute-start.12 = (bf16[1024,256]{1,0:T(8,128)(2,1)S(1)}, bf16[1024,256]{1,0:T(8,128)(2,1)S(1)}, u32[]{:S(2)}, u32[]{:S(2)}) collective-permute-start(bf16[1024,256]{1,0:T(8,128)(2,1)S(1)} %get-tuple-element.40), channel_id=1, source_target_pairs={{0,8},{8,0},{16,24},{24,16},{32,40},{40,32},{48,56},{56,48},{64,72... | collective-permute-start | bytes 1572872 | tf_op jit(solution)/shard_map/ppermute | solution.py:476
  111.2 0.0 all-to-all-done.2.p_ref
  111.2 0.8 sum_partials.1
  112.0 0.7 collective-permute-done.12.s_ref
  112.7 1.6 %fill_halves.1 = (f32[3,256,512]{2,1,0:T(8,128)}, f32[512,256]{1,0:T(8,128)}) custom-call(s32[13]{0:T(128)S(1)} %stack.55.place_ref, bf16[1024,256]{1,0:T(8,128)(2,1)S(1)} %collective-permute-done.12.s_ref, f32[3,256,512]{2,1,0:T(8,128)} %get-tuple-element.41.in_old, f32[512,256]{1,0:T(8,128)} %get-tuple-element.42.out_old), custom_call_target="tpu_custom_call", output_to_operand_aliasing={{0}: (2, {}), {1}: (3, {})} | custom-call | tf_op jit(solution)/shard_map/fill_halves/pallas_call | solution.py:455
  (12 shorter events, 0.0 us)
Async XLA Ops:
  0.6 35.8 %copy-start.5 = (bf16[2048,2048]{1,0:T(8,128)(2,1)S(1)}, bf16[2048,2048]{1,0:T(8,128)(2,1)}, u32[]{:S(2)}) copy-start(bf16[2048,2048]{1,0:T(8,128)(2,1)} %constant.31.clone.m_ref) | copy-start | bytes 25165828
  0.7 35.8 %copy-start.6 = (bf16[256,256]{1,0:T(8,128)(2,1)S(1)}, bf16[256,256]{1,0:T(8,128)(2,1)}, u32[]{:S(2)}) copy-start(bf16[256,256]{1,0:T(8,128)(2,1)} %constant.30.clone.j_ref) | copy-start | bytes 393220
  0.7 35.8 %copy-start.7 = (f32[8,2048]{1,0:T(8,128)S(1)}, f32[8,2048]{1,0:T(8,128)}, u32[]{:S(2)}) copy-start(f32[8,2048]{1,0:T(8,128)} %constant.32.clone.w_ref) | copy-start | bytes 196612
  41.9 29.0 %all-to-all-start.1 = ((bf16[16,160,128]{2,1,0:T(8,128)(2,1)}), bf16[16,160,128]{2,1,0:T(8,128)(2,1)S(1)}, u32[]{:S(2)}, u32[]{:S(2)}) async-start(bf16[16,160,128]{2,1,0:T(8,128)(2,1)} %get-tuple-element.26), calls=%async_computation.1 | async-start | bytes 1310720 | tf_op jit(solution)/shard_map/all_to_all | solution.py:480
  45.9 22.2 %collective-permute-start.2 = (bf16[128,2048]{1,0:T(8,128)(2,1)S(1)}, bf16[128,2048]{1,0:T(8,128)(2,1)S(1)}, u32[]{:S(2)}, u32[]{:S(2)}) collective-permute-start(bf16[128,2048]{1,0:T(8,128)(2,1)S(1)} %get-tuple-element.25.c.refs_8_), channel_id=1, source_target_pairs={{0,64},{8,72},{16,80},{24,88},{32,96},{40,104},{48,112},{56,120},{... | collective-permute-start | bytes 1572872 | tf_op jit(solution)/shard_map/ppermute | solution.py:487
  48.9 20.5 %collective-permute-start.1 = (bf16[128,2048]{1,0:T(8,128)(2,1)S(1)}, bf16[128,2048]{1,0:T(8,128)(2,1)S(1)}, u32[]{:S(2)}, u32[]{:S(2)}) collective-permute-start(bf16[128,2048]{1,0:T(8,128)(2,1)S(1)} %get-tuple-element.25.c.refs_8_), channel_id=1, source_target_pairs={{0,48},{8,56},{16,0},{24,8},{32,16},{40,24},{48,32},{56,40},{64,11... | collective-permute-start | bytes 1572872 | tf_op jit(solution)/shard_map/ppermute | solution.py:487
  51.3 19.6 %collective-permute-start = (bf16[128,2048]{1,0:T(8,128)(2,1)S(1)}, bf16[128,2048]{1,0:T(8,128)(2,1)S(1)}, u32[]{:S(2)}, u32[]{:S(2)}) collective-permute-start(bf16[128,2048]{1,0:T(8,128)(2,1)S(1)} %get-tuple-element.25.c.refs_8_), channel_id=1, source_target_pairs={{0,16},{8,24},{16,32},{24,40},{32,48},{40,56},{48,0},{56,8},{64,80... | collective-permute-start | bytes 1572872 | tf_op jit(solution)/shard_map/ppermute | solution.py:487
  51.3 24.0 %collective-permute-start.5 = (bf16[8,2,128,128]{3,2,1,0:T(8,128)(2,1)S(1)}, bf16[8,2,128,128]{3,2,1,0:T(8,128)(2,1)}, u32[]{:S(2)}, u32[]{:S(2)}) collective-permute-start(bf16[8,2,128,128]{3,2,1,0:T(8,128)(2,1)S(1)} %get-tuple-element.34.refs_0_), channel_id=1, source_target_pairs={{0,2},{1,3},{2,0},{3,1},{4,6},{5,7},{6,4},{7,5},{8,10},{9,11},{10,... | collective-permute-start | bytes 1572872 | tf_op jit(solution)/shard_map/ppermute | solution.py:495
  54.2 31.6 %collective-permute-start.6 = (bf16[8,2,128,128]{3,2,1,0:T(8,128)(2,1)S(1)}, bf16[8,2,128,128]{3,2,1,0:T(8,128)(2,1)}, u32[]{:S(2)}, u32[]{:S(2)}) collective-permute-start(bf16[8,2,128,128]{3,2,1,0:T(8,128)(2,1)S(1)} %get-tuple-element.34.refs_0_), channel_id=1, source_target_pairs={{0,8},{8,0},{16,24},{24,16},{32,40},{40,32},{48,56},{56,48},{64,72... | collective-permute-start | bytes 1572872 | tf_op jit(solution)/shard_map/ppermute | solution.py:476
  68.1 15.3 %copy-start.1 = (bf16[128,2048]{1,0:T(8,128)(2,1)}, bf16[128,2048]{1,0:T(8,128)(2,1)S(1)}, u32[]{:S(2)}) copy-start(bf16[128,2048]{1,0:T(8,128)(2,1)S(1)} %collective-permute-done.2.d.refs_11_) | copy-start | bytes 1572868
  68.1 16.3 %collective-permute-start.3 = (bf16[8,2,128,128]{3,2,1,0:T(8,128)(2,1)S(1)}, bf16[8,2,128,128]{3,2,1,0:T(8,128)(2,1)}, u32[]{:S(2)}, u32[]{:S(2)}) collective-permute-start(bf16[8,2,128,128]{3,2,1,0:T(8,128)(2,1)S(1)} %get-tuple-element.34.refs_0_), channel_id=1, source_target_pairs={{0,1},{1,2},{2,3},{3,0},{4,5},{5,6},{6,7},{7,4},{8,9},{9,10},{10,1... | collective-permute-start | bytes 1572872 | tf_op jit(solution)/shard_map/ppermute | solution.py:495
  69.4 14.0 %copy-start.2 = (bf16[128,2048]{1,0:T(8,128)(2,1)}, bf16[128,2048]{1,0:T(8,128)(2,1)S(1)}, u32[]{:S(2)}) copy-start(bf16[128,2048]{1,0:T(8,128)(2,1)S(1)} %collective-permute-done.1.b.refs_10_) | copy-start | bytes 1572868
  69.4 16.3 %collective-permute-start.4 = (bf16[8,2,128,128]{3,2,1,0:T(8,128)(2,1)S(1)}, bf16[8,2,128,128]{3,2,1,0:T(8,128)(2,1)}, u32[]{:S(2)}, u32[]{:S(2)}) collective-permute-start(bf16[8,2,128,128]{3,2,1,0:T(8,128)(2,1)S(1)} %get-tuple-element.34.refs_0_), channel_id=1, source_target_pairs={{0,3},{1,0},{2,1},{3,2},{4,7},{5,4},{6,5},{7,6},{8,11},{9,8},{10,9... | collective-permute-start | bytes 1572872 | tf_op jit(solution)/shard_map/ppermute | solution.py:495
  70.9 12.5 %copy-start.3 = (bf16[128,2048]{1,0:T(8,128)(2,1)}, bf16[128,2048]{1,0:T(8,128)(2,1)S(1)}, u32[]{:S(2)}) copy-start(bf16[128,2048]{1,0:T(8,128)(2,1)S(1)} %collective-permute-done.a.refs_9_) | copy-start | bytes 1572868
  72.5 25.7 %collective-permute-start.10 = (bf16[256,2048]{1,0:T(8,128)(2,1)}, bf16[256,2048]{1,0:T(8,128)(2,1)}, u32[]{:S(2)}, u32[]{:S(2)}) collective-permute-start(bf16[256,2048]{1,0:T(8,128)(2,1)} %get-tuple-element.38), channel_id=1, source_target_pairs={{0,32},{8,40},{16,48},{24,56},{32,0},{40,8},{48,16},{56,24},{64,96... | collective-permute-start | bytes 3145736 | tf_op jit(solution)/shard_map/ppermute | solution.py:487
  75.3 24.9 %collective-permute-start.11 = (bf16[256,2048]{1,0:T(8,128)(2,1)}, bf16[256,2048]{1,0:T(8,128)(2,1)}, u32[]{:S(2)}, u32[]{:S(2)}) collective-permute-start(bf16[256,2048]{1,0:T(8,128)(2,1)} %get-tuple-element.31), channel_id=1, source_target_pairs={{0,64},{8,72},{16,80},{24,88},{32,96},{40,104},{48,112},{56,120},{... | collective-permute-start | bytes 3145736 | tf_op jit(solution)/shard_map/ppermute | solution.py:487
  83.4 1.0 copy-start.4
  84.4 5.5 %collective-permute-start.7 = (bf16[8,2,128,128]{3,2,1,0:T(8,128)(2,1)}, bf16[8,2,128,128]{3,2,1,0:T(8,128)(2,1)S(1)}, u32[]{:S(2)}, u32[]{:S(2)}) collective-permute-start(bf16[8,2,128,128]{3,2,1,0:T(8,128)(2,1)} %collective-permute-done.3.refs_1_), channel_id=1, source_target_pairs={{0,8},{8,0},{16,24},{24,16},{32,40},{40,32},{48,56},{56,48},{64,72... | collective-permute-start | bytes 1572872 | tf_op jit(solution)/shard_map/ppermute | solution.py:476
  85.7 4.2 %collective-permute-start.8 = (bf16[8,2,128,128]{3,2,1,0:T(8,128)(2,1)}, bf16[8,2,128,128]{3,2,1,0:T(8,128)(2,1)S(1)}, u32[]{:S(2)}, u32[]{:S(2)}) collective-permute-start(bf16[8,2,128,128]{3,2,1,0:T(8,128)(2,1)} %collective-permute-done.4.refs_2_), channel_id=1, source_target_pairs={{0,8},{8,0},{16,24},{24,16},{32,40},{40,32},{48,56},{56,48},{64,72... | collective-permute-start | bytes 1572872 | tf_op jit(solution)/shard_map/ppermute | solution.py:476
  85.8 4.2 %collective-permute-start.9 = (bf16[8,2,128,128]{3,2,1,0:T(8,128)(2,1)}, bf16[8,2,128,128]{3,2,1,0:T(8,128)(2,1)}, u32[]{:S(2)}, u32[]{:S(2)}) collective-permute-start(bf16[8,2,128,128]{3,2,1,0:T(8,128)(2,1)} %collective-permute-done.5.refs_3_), channel_id=1, source_target_pairs={{0,8},{8,0},{16,24},{24,16},{32,40},{40,32},{48,56},{56,48},{64,72... | collective-permute-start | bytes 1572872 | tf_op jit(solution)/shard_map/ppermute | solution.py:476
  86.2 25.0 %all-to-all-start.2 = ((bf16[8,128,512]{2,1,0:T(8,128)(2,1)}), bf16[8,128,512]{2,1,0:T(8,128)(2,1)S(1)}, u32[]{:S(2)}, u32[]{:S(2)}) async-start(bf16[8,128,512]{2,1,0:T(8,128)(2,1)} %copy-done.4), calls=%async_computation.2 | async-start | bytes 2097152 | tf_op jit(solution)/shard_map/all_to_all | solution.py:480
  89.9 0.8 copy-start.8
  90.0 1.0 copy-start.9
  96.2 2.0 %copy-start = (bf16[2,2,8,128,512]{4,3,2,1,0:T(8,128)(2,1)}, bf16[2,2,8,128,512]{4,3,2,1,0:T(8,128)(2,1)S(1)}, u32[]{:S(2)}) copy-start(bf16[2,2,8,128,512]{4,3,2,1,0:T(8,128)(2,1)S(1)} %get-tuple-element.39.refs_4_) | copy-start | bytes 12582916
  106.5 6.2 %collective-permute-start.12 = (bf16[1024,256]{1,0:T(8,128)(2,1)S(1)}, bf16[1024,256]{1,0:T(8,128)(2,1)S(1)}, u32[]{:S(2)}, u32[]{:S(2)}) collective-permute-start(bf16[1024,256]{1,0:T(8,128)(2,1)S(1)} %get-tuple-element.40), channel_id=1, source_target_pairs={{0,8},{8,0},{16,24},{24,16},{32,40},{40,32},{48,56},{56,48},{64,72... | collective-permute-start | bytes 1572872 | tf_op jit(solution)/shard_map/ppermute | solution.py:476

commit v5 on v4

--- a/solution.py
+++ b/solution.py
@@ -143,7 +143,7 @@
 
 
 def convolve(received, matrix, rows, flip):
-    chunk = 512
+    chunk = 256
     n_chunks = SEQ // chunk
 
     def kernel(r_ref, m_ref, w_ref, j_ref, b_ref, o_ref, c_ref, x_ref, y_ref):

time: 115 us -> 117 us (1.017)
  Pallas kernels: 35.4 us -> 37.4 us
    pallas_call x1, Pallas kernels: 5.42 us -> 7.42 us  [convolve(): call(kernel, in_specs=[vm, vm, vm, vm], out_specs=[vm, vm, vm], out_shape...]
where the time goes in v5:
time: 117 us; the launch traced here: 116 us
  Pallas kernels  37.4 us (32%)
  starting transfers between devices  30.3 us (26%)
  blocking collectives  28.1 us (24%)
  waiting for transfers between devices  15.5 us (13%)
  local copies, waits for them, and re-layouts  4.08 us (3%)
    all_to_all x1, blocking collectives, swap(): lax.all_to_all(pieces, axis, 0, 0, axis_index_groups=groups, tiled=True)  28.1 us
    ppermute x5, waiting for transfers between devices, hop(): return lax.ppermute(value, 'ctx', chip_hop(x_flip, z_step))  14.7 us
    ppermute x5, starting transfers between devices, hop(): return lax.ppermute(value, 'ctx', chip_hop(x_flip, z_step))  9.36 us
    pallas_call x1, Pallas kernels, project(): call(kernel, in_specs=[pl.BlockSpec(memory_space=pltpu.SMEM)] + [hbm] * 5...  7.68 us
    ppermute x5, starting transfers between devices, swap_cores(): return lax.ppermute(value, 'ctx', [(i, i ^ 1) for i in range(16)])  7.65 us
    all_to_all x2, starting transfers between devices, swap(): lax.all_to_all(pieces, axis, 0, 0, axis_index_groups=groups, tiled=True)  7.6 us
    pallas_call x1, Pallas kernels, convolve(): call(kernel, in_specs=[vm, vm, vm, vm], out_specs=[vm, vm, vm], out_shape...  7.42 us
    pallas_call x1, Pallas kernels, input_partial(): call(kernel, in_specs=[vm, pl.BlockSpec(memory_space=pl.ANY)], out_specs=...  6.91 us
  transfers between devices with their start and end apart: 15, of which 3 were waited for; matrix products, arithmetic and copies ran while one was open for 0% of the time, Pallas kernels for 18%

profile of v5, /device:TPU:1, one launch (start us, length us, event | category | flops | bytes accessed | tf_op | source)
XLA Modules:
  0.0 116.5 jit_solution(16019546928998875854)
XLA Ops:
  0.6 0.0 copy-start.5
  0.7 0.0 copy-start.6
  0.7 0.0 copy-start.7
  0.7 7.7 %project.1 = bf16[8,2,288,128]{3,2,1,0:T(8,128)(2,1)S(1)} custom-call(s32[1]{0:T(128)} %bitcast.y_ref, bf16[128,4096]{1,0:T(8,128)(2,1)} %t_hbm.1, bf16[128,4096]{1,0:T(8,128)(2,1)} %g_hbm.1, f32[128,512]{1,0:T(8,128)} %f_hbm.1, bf16[3,4096,512]{2,1,0:T(8,128)(2,1)} %bitcast.18, bf16[512,4096]{1,0:T(8,128)(2,1)} %ow_hbm.1), custom_call_target="tpu_custom_call" | custom-call | flops 2147483648 | bytes 19922944 | tf_op jit(solution)/shard_map/project/pallas_call | solution.py:111
  8.4 28.1 %all_to_all.15.r_ref = bf16[16,288,128]{2,1,0:T(8,128)(2,1)S(1)} all-to-all(bf16[16,288,128]{2,1,0:T(8,128)(2,1)S(1)} %bitcast.17), channel_id=1, replica_groups=mesh['ctx'=16,'mp'=8] {'ctx'}, dimensions={0} | all-to-all | bytes 2359296 | tf_op jit(solution)/shard_map/all_to_all | solution.py:480
  36.5 7.4 %convolve.1 = (bf16[128,2048]{1,0:T(8,128)(2,1)S(1)}, bf16[16,160,128]{2,1,0:T(8,128)(2,1)}, bf16[8,2,128,128]{3,2,1,0:T(8,128)(2,1)S(1)}) custom-call(bf16[16,288,128]{2,1,0:T(8,128)(2,1)S(1)} %all_to_all.15.r_ref, bf16[2048,2048]{1,0:T(8,128)(2,1)S(1)} %copy-done.5, f32[8,2048]{1,0:T(8,128)S(1)} %copy-done.7, bf16[256,256]{1,0:T(8,128)(2,1)S(1)} %copy-done.6), custom_call_target="tpu_custom_call" | custom-call | flops 3221225472 | bytes 12582912 | tf_op jit(solution)/shard_map/convolve/pallas_call | solution.py:208
  43.9 4.0 %all-to-all-start.1 = ((bf16[16,160,128]{2,1,0:T(8,128)(2,1)}), bf16[16,160,128]{2,1,0:T(8,128)(2,1)S(1)}, u32[]{:S(2)}, u32[]{:S(2)}) async-start(bf16[16,160,128]{2,1,0:T(8,128)(2,1)} %get-tuple-element.26), calls=%async_computation.1 | async-start | bytes 1310720 | tf_op jit(solution)/shard_map/all_to_all | solution.py:480
  47.9 2.9 %collective-permute-start.2 = (bf16[128,2048]{1,0:T(8,128)(2,1)S(1)}, bf16[128,2048]{1,0:T(8,128)(2,1)S(1)}, u32[]{:S(2)}, u32[]{:S(2)}) collective-permute-start(bf16[128,2048]{1,0:T(8,128)(2,1)S(1)} %get-tuple-element.25.c.refs_8_), channel_id=1, source_target_pairs={{0,64},{8,72},{16,80},{24,88},{32,96},{40,104},{48,112},{56,120},{... | collective-permute-start | bytes 1572872 | tf_op jit(solution)/shard_map/ppermute | solution.py:487
  50.9 2.4 %collective-permute-start.1 = (bf16[128,2048]{1,0:T(8,128)(2,1)S(1)}, bf16[128,2048]{1,0:T(8,128)(2,1)S(1)}, u32[]{:S(2)}, u32[]{:S(2)}) collective-permute-start(bf16[128,2048]{1,0:T(8,128)(2,1)S(1)} %get-tuple-element.25.c.refs_8_), channel_id=1, source_target_pairs={{0,48},{8,56},{16,0},{24,8},{32,16},{40,24},{48,32},{56,40},{64,11... | collective-permute-start | bytes 1572872 | tf_op jit(solution)/shard_map/ppermute | solution.py:487
  53.3 0.0 collective-permute-start
  53.3 2.9 %collective-permute-start.5 = (bf16[8,2,128,128]{3,2,1,0:T(8,128)(2,1)S(1)}, bf16[8,2,128,128]{3,2,1,0:T(8,128)(2,1)}, u32[]{:S(2)}, u32[]{:S(2)}) collective-permute-start(bf16[8,2,128,128]{3,2,1,0:T(8,128)(2,1)S(1)} %get-tuple-element.34.refs_0_), channel_id=1, source_target_pairs={{0,2},{1,3},{2,0},{3,1},{4,6},{5,7},{6,4},{7,5},{8,10},{9,11},{10,... | collective-permute-start | bytes 1572872 | tf_op jit(solution)/shard_map/ppermute | solution.py:495
  56.2 1.2 %collective-permute-start.6 = (bf16[8,2,128,128]{3,2,1,0:T(8,128)(2,1)S(1)}, bf16[8,2,128,128]{3,2,1,0:T(8,128)(2,1)}, u32[]{:S(2)}, u32[]{:S(2)}) collective-permute-start(bf16[8,2,128,128]{3,2,1,0:T(8,128)(2,1)S(1)} %get-tuple-element.34.refs_0_), channel_id=1, source_target_pairs={{0,8},{8,0},{16,24},{24,16},{32,40},{40,32},{48,56},{56,48},{64,72... | collective-permute-start | bytes 1572872 | tf_op jit(solution)/shard_map/ppermute | solution.py:476
  57.4 12.7 %collective-permute-done.2.d.refs_11_ = bf16[128,2048]{1,0:T(8,128)(2,1)S(1)} collective-permute-done((bf16[128,2048]{1,0:T(8,128)(2,1)S(1)}, bf16[128,2048]{1,0:T(8,128)(2,1)S(1)}, u32[]{:S(2)}, u32[]{:S(2)}) %collective-permute-start.2) | collective-permute-done | bytes 524320 | tf_op jit(solution)/shard_map/ppermute | solution.py:487
  70.1 1.3 %collective-permute-start.3 = (bf16[8,2,128,128]{3,2,1,0:T(8,128)(2,1)S(1)}, bf16[8,2,128,128]{3,2,1,0:T(8,128)(2,1)}, u32[]{:S(2)}, u32[]{:S(2)}) collective-permute-start(bf16[8,2,128,128]{3,2,1,0:T(8,128)(2,1)S(1)} %get-tuple-element.34.refs_0_), channel_id=1, source_target_pairs={{0,1},{1,2},{2,3},{3,0},{4,5},{5,6},{6,7},{7,4},{8,9},{9,10},{10,1... | collective-permute-start | bytes 1572872 | tf_op jit(solution)/shard_map/ppermute | solution.py:495
  71.4 0.0 collective-permute-done.1.b.refs_10_
  71.4 1.5 %collective-permute-start.4 = (bf16[8,2,128,128]{3,2,1,0:T(8,128)(2,1)S(1)}, bf16[8,2,128,128]{3,2,1,0:T(8,128)(2,1)}, u32[]{:S(2)}, u32[]{:S(2)}) collective-permute-start(bf16[8,2,128,128]{3,2,1,0:T(8,128)(2,1)S(1)} %get-tuple-element.34.refs_0_), channel_id=1, source_target_pairs={{0,3},{1,0},{2,1},{3,2},{4,7},{5,4},{6,5},{7,6},{8,11},{9,8},{10,9... | collective-permute-start | bytes 1572872 | tf_op jit(solution)/shard_map/ppermute | solution.py:495
  72.9 0.0 collective-permute-done.a.refs_9_
  72.9 0.0 all-to-all-done.1.r_ref
  72.9 1.5 %pair.1 = (bf16[256,2048]{1,0:T(8,128)(2,1)}, bf16[256,2048]{1,0:T(8,128)(2,1)}) custom-call(bf16[128,2048]{1,0:T(8,128)(2,1)S(1)} %collective-permute-done.a.refs_9_, bf16[128,2048]{1,0:T(8,128)(2,1)S(1)} %collective-permute-done.1.b.refs_10_, bf16[128,2048]{1,0:T(8,128)(2,1)S(1)} %get-tuple-element.25.c.refs_8_, ...), custom_call_target="tpu_custom_call" | custom-call | tf_op jit(solution)/shard_map/pair/pallas_call | solution.py:306
  74.5 2.8 %collective-permute-start.10 = (bf16[256,2048]{1,0:T(8,128)(2,1)}, bf16[256,2048]{1,0:T(8,128)(2,1)}, u32[]{:S(2)}, u32[]{:S(2)}) collective-permute-start(bf16[256,2048]{1,0:T(8,128)(2,1)} %get-tuple-element.38), channel_id=1, source_target_pairs={{0,32},{8,40},{16,48},{24,56},{32,0},{40,8},{48,16},{56,24},{64,96... | collective-permute-start | bytes 3145736 | tf_op jit(solution)/shard_map/ppermute | solution.py:487
  77.3 0.0 collective-permute-done.5.refs_3_
  77.3 1.2 %collective-permute-start.11 = (bf16[256,2048]{1,0:T(8,128)(2,1)}, bf16[256,2048]{1,0:T(8,128)(2,1)}, u32[]{:S(2)}, u32[]{:S(2)}) collective-permute-start(bf16[256,2048]{1,0:T(8,128)(2,1)} %get-tuple-element.31), channel_id=1, source_target_pairs={{0,64},{8,72},{16,80},{24,88},{32,96},{40,104},{48,112},{56,120},{... | collective-permute-start | bytes 3145736 | tf_op jit(solution)/shard_map/ppermute | solution.py:487
  78.5 6.9 %input_partial.1 = (bf16[8,128,512]{2,1,0:T(8,128)(2,1)S(1)}, f32[128,512]{1,0:T(8,128)}) custom-call(bf16[16,160,128]{2,1,0:T(8,128)(2,1)S(1)} %all-to-all-done.1.r_ref, bf16[3,4096,512]{2,1,0:T(8,128)(2,1)} %bitcast.19), custom_call_target="tpu_custom_call" | custom-call | flops 1610612736 | bytes 14680064 | tf_op jit(solution)/shard_map/input_partial/pallas_call | solution.py:257
  85.4 1.0 copy-done.4
  86.4 0.0 collective-permute-done.3.refs_1_
  86.4 1.3 %collective-permute-start.7 = (bf16[8,2,128,128]{3,2,1,0:T(8,128)(2,1)}, bf16[8,2,128,128]{3,2,1,0:T(8,128)(2,1)S(1)}, u32[]{:S(2)}, u32[]{:S(2)}) collective-permute-start(bf16[8,2,128,128]{3,2,1,0:T(8,128)(2,1)} %collective-permute-done.3.refs_1_), channel_id=1, source_target_pairs={{0,8},{8,0},{16,24},{24,16},{32,40},{40,32},{48,56},{56,48},{64,72... | collective-permute-start | bytes 1572872 | tf_op jit(solution)/shard_map/ppermute | solution.py:476
  87.7 0.0 collective-permute-done.4.refs_2_
  87.7 0.1 collective-permute-start.8
  87.8 0.0 collective-permute-done.6.refs_4_
  87.8 0.4 collective-permute-start.9
  88.2 3.6 %all-to-all-start.2 = ((bf16[8,128,512]{2,1,0:T(8,128)(2,1)}), bf16[8,128,512]{2,1,0:T(8,128)(2,1)S(1)}, u32[]{:S(2)}, u32[]{:S(2)}) async-start(bf16[8,128,512]{2,1,0:T(8,128)(2,1)} %copy-done.4), calls=%async_computation.2 | async-start | bytes 2097152 | tf_op jit(solution)/shard_map/all_to_all | solution.py:480
  91.8 0.1 stack.55.place_ref
  91.9 0.0 collective-permute-done.7.refs_5_
  91.9 0.0 copy-start.8
  91.9 0.0 collective-permute-done.8.refs_6_
  92.0 0.0 collective-permute-done.9.refs_7_
  92.0 0.8 copy-done.8
  92.7 0.2 copy-done.9
  93.0 5.2 %first_products.1 = (f32[4,128,512]{2,1,0:T(8,128)S(1)}, bf16[2,2,8,128,512]{4,3,2,1,0:T(8,128)(2,1)S(1)}) custom-call(s32[13]{0:T(128)S(1)} %stack.55.place_ref, bf16[8,2,128,128]{3,2,1,0:T(8,128)(2,1)S(1)} %get-tuple-element.34.refs_0_, bf16[8,2,128,128]{3,2,1,0:T(8,128)(2,1)} %collective-permute-done.3.refs_1_, ...), custom_call_target="tpu_custom_call" | custom-call | tf_op jit(solution)/shard_map/first_products/pallas_call | solution.py:365
  98.2 2.0 %copy-done = bf16[2,2,8,128,512]{4,3,2,1,0:T(8,128)(2,1)} copy-done((bf16[2,2,8,128,512]{4,3,2,1,0:T(8,128)(2,1)}, bf16[2,2,8,128,512]{4,3,2,1,0:T(8,128)(2,1)S(1)}, u32[]{:S(2)}) %copy-start) | copy-done | bytes 4194328
  100.1 0.0 collective-permute-done.10.refs_0_.refs_3_
  100.1 2.1 %collective-permute-done.11.refs_1_.refs_2_ = bf16[256,2048]{1,0:T(8,128)(2,1)} collective-permute-done((bf16[256,2048]{1,0:T(8,128)(2,1)}, bf16[256,2048]{1,0:T(8,128)(2,1)}, u32[]{:S(2)}, u32[]{:S(2)}) %collective-permute-start.11) | collective-permute-done | bytes 1048608 | tf_op jit(solution)/shard_map/ppermute | solution.py:487
  102.2 6.3 %weight_gradients.1 = (f32[3,256,512]{2,1,0:T(8,128)}, f32[512,256]{1,0:T(8,128)}, bf16[1024,256]{1,0:T(8,128)(2,1)S(1)}) custom-call(s32[13]{0:T(128)S(1)} %stack.55.place_ref, f32[4,128,512]{2,1,0:T(8,128)S(1)} %get-tuple-element.37.p_ref, bf16[256,2048]{1,0:T(8,128)(2,1)} %collective-permute-done.10.refs_0_.refs_3_, ...), custom_call_target="tpu_custom_call" | custom-call | tf_op jit(solution)/shard_map/weight_gradients/pallas_call | solution.py:421
  108.5 4.7 %collective-permute-start.12 = (bf16[1024,256]{1,0:T(8,128)(2,1)S(1)}, bf16[1024,256]{1,0:T(8,128)(2,1)S(1)}, u32[]{:S(2)}, u32[]{:S(2)}) collective-permute-start(bf16[1024,256]{1,0:T(8,128)(2,1)S(1)} %get-tuple-element.40), channel_id=1, source_target_pairs={{0,8},{8,0},{16,24},{24,16},{32,40},{40,32},{48,56},{56,48},{64,72... | collective-permute-start | bytes 1572872 | tf_op jit(solution)/shard_map/ppermute | solution.py:476
  113.2 0.0 all-to-all-done.2.p_ref
  113.2 0.8 sum_partials.1
  114.0 0.7 collective-permute-done.12.s_ref
  114.7 1.6 %fill_halves.1 = (f32[3,256,512]{2,1,0:T(8,128)}, f32[512,256]{1,0:T(8,128)}) custom-call(s32[13]{0:T(128)S(1)} %stack.55.place_ref, bf16[1024,256]{1,0:T(8,128)(2,1)S(1)} %collective-permute-done.12.s_ref, f32[3,256,512]{2,1,0:T(8,128)} %get-tuple-element.41.in_old, f32[512,256]{1,0:T(8,128)} %get-tuple-element.42.out_old), custom_call_target="tpu_custom_call", output_to_operand_aliasing={{0}: (2, {}), {1}: (3, {})} | custom-call | tf_op jit(solution)/shard_map/fill_halves/pallas_call | solution.py:455
  (12 shorter events, 0.0 us)
Async XLA Ops:
  0.6 35.8 %copy-start.5 = (bf16[2048,2048]{1,0:T(8,128)(2,1)S(1)}, bf16[2048,2048]{1,0:T(8,128)(2,1)}, u32[]{:S(2)}) copy-start(bf16[2048,2048]{1,0:T(8,128)(2,1)} %constant.31.clone.m_ref) | copy-start | bytes 25165828
  0.7 35.8 %copy-start.6 = (bf16[256,256]{1,0:T(8,128)(2,1)S(1)}, bf16[256,256]{1,0:T(8,128)(2,1)}, u32[]{:S(2)}) copy-start(bf16[256,256]{1,0:T(8,128)(2,1)} %constant.30.clone.j_ref) | copy-start | bytes 393220
  0.7 35.8 %copy-start.7 = (f32[8,2048]{1,0:T(8,128)S(1)}, f32[8,2048]{1,0:T(8,128)}, u32[]{:S(2)}) copy-start(f32[8,2048]{1,0:T(8,128)} %constant.32.clone.w_ref) | copy-start | bytes 196612
  43.9 29.0 %all-to-all-start.1 = ((bf16[16,160,128]{2,1,0:T(8,128)(2,1)}), bf16[16,160,128]{2,1,0:T(8,128)(2,1)S(1)}, u32[]{:S(2)}, u32[]{:S(2)}) async-start(bf16[16,160,128]{2,1,0:T(8,128)(2,1)} %get-tuple-element.26), calls=%async_computation.1 | async-start | bytes 1310720 | tf_op jit(solution)/shard_map/all_to_all | solution.py:480
  47.9 22.2 %collective-permute-start.2 = (bf16[128,2048]{1,0:T(8,128)(2,1)S(1)}, bf16[128,2048]{1,0:T(8,128)(2,1)S(1)}, u32[]{:S(2)}, u32[]{:S(2)}) collective-permute-start(bf16[128,2048]{1,0:T(8,128)(2,1)S(1)} %get-tuple-element.25.c.refs_8_), channel_id=1, source_target_pairs={{0,64},{8,72},{16,80},{24,88},{32,96},{40,104},{48,112},{56,120},{... | collective-permute-start | bytes 1572872 | tf_op jit(solution)/shard_map/ppermute | solution.py:487
  50.9 20.5 %collective-permute-start.1 = (bf16[128,2048]{1,0:T(8,128)(2,1)S(1)}, bf16[128,2048]{1,0:T(8,128)(2,1)S(1)}, u32[]{:S(2)}, u32[]{:S(2)}) collective-permute-start(bf16[128,2048]{1,0:T(8,128)(2,1)S(1)} %get-tuple-element.25.c.refs_8_), channel_id=1, source_target_pairs={{0,48},{8,56},{16,0},{24,8},{32,16},{40,24},{48,32},{56,40},{64,11... | collective-permute-start | bytes 1572872 | tf_op jit(solution)/shard_map/ppermute | solution.py:487
  53.3 19.6 %collective-permute-start = (bf16[128,2048]{1,0:T(8,128)(2,1)S(1)}, bf16[128,2048]{1,0:T(8,128)(2,1)S(1)}, u32[]{:S(2)}, u32[]{:S(2)}) collective-permute-start(bf16[128,2048]{1,0:T(8,128)(2,1)S(1)} %get-tuple-element.25.c.refs_8_), channel_id=1, source_target_pairs={{0,16},{8,24},{16,32},{24,40},{32,48},{40,56},{48,0},{56,8},{64,80... | collective-permute-start | bytes 1572872 | tf_op jit(solution)/shard_map/ppermute | solution.py:487
  53.3 24.0 %collective-permute-start.5 = (bf16[8,2,128,128]{3,2,1,0:T(8,128)(2,1)S(1)}, bf16[8,2,128,128]{3,2,1,0:T(8,128)(2,1)}, u32[]{:S(2)}, u32[]{:S(2)}) collective-permute-start(bf16[8,2,128,128]{3,2,1,0:T(8,128)(2,1)S(1)} %get-tuple-element.34.refs_0_), channel_id=1, source_target_pairs={{0,2},{1,3},{2,0},{3,1},{4,6},{5,7},{6,4},{7,5},{8,10},{9,11},{10,... | collective-permute-start | bytes 1572872 | tf_op jit(solution)/shard_map/ppermute | solution.py:495
  56.2 31.6 %collective-permute-start.6 = (bf16[8,2,128,128]{3,2,1,0:T(8,128)(2,1)S(1)}, bf16[8,2,128,128]{3,2,1,0:T(8,128)(2,1)}, u32[]{:S(2)}, u32[]{:S(2)}) collective-permute-start(bf16[8,2,128,128]{3,2,1,0:T(8,128)(2,1)S(1)} %get-tuple-element.34.refs_0_), channel_id=1, source_target_pairs={{0,8},{8,0},{16,24},{24,16},{32,40},{40,32},{48,56},{56,48},{64,72... | collective-permute-start | bytes 1572872 | tf_op jit(solution)/shard_map/ppermute | solution.py:476
  70.1 15.3 %copy-start.1 = (bf16[128,2048]{1,0:T(8,128)(2,1)}, bf16[128,2048]{1,0:T(8,128)(2,1)S(1)}, u32[]{:S(2)}) copy-start(bf16[128,2048]{1,0:T(8,128)(2,1)S(1)} %collective-permute-done.2.d.refs_11_) | copy-start | bytes 1572868
  70.1 16.3 %collective-permute-start.3 = (bf16[8,2,128,128]{3,2,1,0:T(8,128)(2,1)S(1)}, bf16[8,2,128,128]{3,2,1,0:T(8,128)(2,1)}, u32[]{:S(2)}, u32[]{:S(2)}) collective-permute-start(bf16[8,2,128,128]{3,2,1,0:T(8,128)(2,1)S(1)} %get-tuple-element.34.refs_0_), channel_id=1, source_target_pairs={{0,1},{1,2},{2,3},{3,0},{4,5},{5,6},{6,7},{7,4},{8,9},{9,10},{10,1... | collective-permute-start | bytes 1572872 | tf_op jit(solution)/shard_map/ppermute | solution.py:495
  71.4 14.0 %copy-start.2 = (bf16[128,2048]{1,0:T(8,128)(2,1)}, bf16[128,2048]{1,0:T(8,128)(2,1)S(1)}, u32[]{:S(2)}) copy-start(bf16[128,2048]{1,0:T(8,128)(2,1)S(1)} %collective-permute-done.1.b.refs_10_) | copy-start | bytes 1572868
  71.4 16.3 %collective-permute-start.4 = (bf16[8,2,128,128]{3,2,1,0:T(8,128)(2,1)S(1)}, bf16[8,2,128,128]{3,2,1,0:T(8,128)(2,1)}, u32[]{:S(2)}, u32[]{:S(2)}) collective-permute-start(bf16[8,2,128,128]{3,2,1,0:T(8,128)(2,1)S(1)} %get-tuple-element.34.refs_0_), channel_id=1, source_target_pairs={{0,3},{1,0},{2,1},{3,2},{4,7},{5,4},{6,5},{7,6},{8,11},{9,8},{10,9... | collective-permute-start | bytes 1572872 | tf_op jit(solution)/shard_map/ppermute | solution.py:495
  72.9 12.5 %copy-start.3 = (bf16[128,2048]{1,0:T(8,128)(2,1)}, bf16[128,2048]{1,0:T(8,128)(2,1)S(1)}, u32[]{:S(2)}) copy-start(bf16[128,2048]{1,0:T(8,128)(2,1)S(1)} %collective-permute-done.a.refs_9_) | copy-start | bytes 1572868
  74.5 25.6 %collective-permute-start.10 = (bf16[256,2048]{1,0:T(8,128)(2,1)}, bf16[256,2048]{1,0:T(8,128)(2,1)}, u32[]{:S(2)}, u32[]{:S(2)}) collective-permute-start(bf16[256,2048]{1,0:T(8,128)(2,1)} %get-tuple-element.38), channel_id=1, source_target_pairs={{0,32},{8,40},{16,48},{24,56},{32,0},{40,8},{48,16},{56,24},{64,96... | collective-permute-start | bytes 3145736 | tf_op jit(solution)/shard_map/ppermute | solution.py:487
  77.3 24.9 %collective-permute-start.11 = (bf16[256,2048]{1,0:T(8,128)(2,1)}, bf16[256,2048]{1,0:T(8,128)(2,1)}, u32[]{:S(2)}, u32[]{:S(2)}) collective-permute-start(bf16[256,2048]{1,0:T(8,128)(2,1)} %get-tuple-element.31), channel_id=1, source_target_pairs={{0,64},{8,72},{16,80},{24,88},{32,96},{40,104},{48,112},{56,120},{... | collective-permute-start | bytes 3145736 | tf_op jit(solution)/shard_map/ppermute | solution.py:487
  85.4 1.0 copy-start.4
  86.4 5.5 %collective-permute-start.7 = (bf16[8,2,128,128]{3,2,1,0:T(8,128)(2,1)}, bf16[8,2,128,128]{3,2,1,0:T(8,128)(2,1)S(1)}, u32[]{:S(2)}, u32[]{:S(2)}) collective-permute-start(bf16[8,2,128,128]{3,2,1,0:T(8,128)(2,1)} %collective-permute-done.3.refs_1_), channel_id=1, source_target_pairs={{0,8},{8,0},{16,24},{24,16},{32,40},{40,32},{48,56},{56,48},{64,72... | collective-permute-start | bytes 1572872 | tf_op jit(solution)/shard_map/ppermute | solution.py:476
  87.7 4.2 %collective-permute-start.8 = (bf16[8,2,128,128]{3,2,1,0:T(8,128)(2,1)}, bf16[8,2,128,128]{3,2,1,0:T(8,128)(2,1)S(1)}, u32[]{:S(2)}, u32[]{:S(2)}) collective-permute-start(bf16[8,2,128,128]{3,2,1,0:T(8,128)(2,1)} %collective-permute-done.4.refs_2_), channel_id=1, source_target_pairs={{0,8},{8,0},{16,24},{24,16},{32,40},{40,32},{48,56},{56,48},{64,72... | collective-permute-start | bytes 1572872 | tf_op jit(solution)/shard_map/ppermute | solution.py:476
  87.8 4.2 %collective-permute-start.9 = (bf16[8,2,128,128]{3,2,1,0:T(8,128)(2,1)}, bf16[8,2,128,128]{3,2,1,0:T(8,128)(2,1)}, u32[]{:S(2)}, u32[]{:S(2)}) collective-permute-start(bf16[8,2,128,128]{3,2,1,0:T(8,128)(2,1)} %collective-permute-done.5.refs_3_), channel_id=1, source_target_pairs={{0,8},{8,0},{16,24},{24,16},{32,40},{40,32},{48,56},{56,48},{64,72... | collective-permute-start | bytes 1572872 | tf_op jit(solution)/shard_map/ppermute | solution.py:476
  88.2 25.0 %all-to-all-start.2 = ((bf16[8,128,512]{2,1,0:T(8,128)(2,1)}), bf16[8,128,512]{2,1,0:T(8,128)(2,1)S(1)}, u32[]{:S(2)}, u32[]{:S(2)}) async-start(bf16[8,128,512]{2,1,0:T(8,128)(2,1)} %copy-done.4), calls=%async_computation.2 | async-start | bytes 2097152 | tf_op jit(solution)/shard_map/all_to_all | solution.py:480
  91.9 0.8 copy-start.8
  91.9 1.0 copy-start.9
  98.2 2.0 %copy-start = (bf16[2,2,8,128,512]{4,3,2,1,0:T(8,128)(2,1)}, bf16[2,2,8,128,512]{4,3,2,1,0:T(8,128)(2,1)S(1)}, u32[]{:S(2)}) copy-start(bf16[2,2,8,128,512]{4,3,2,1,0:T(8,128)(2,1)S(1)} %get-tuple-element.39.refs_4_) | copy-start | bytes 12582916
  108.5 6.2 %collective-permute-start.12 = (bf16[1024,256]{1,0:T(8,128)(2,1)S(1)}, bf16[1024,256]{1,0:T(8,128)(2,1)S(1)}, u32[]{:S(2)}, u32[]{:S(2)}) collective-permute-start(bf16[1024,256]{1,0:T(8,128)(2,1)S(1)} %get-tuple-element.40), channel_id=1, source_target_pairs={{0,8},{8,0},{16,24},{24,16},{32,40},{40,32},{48,56},{56,48},{64,72... | collective-permute-start | bytes 1572872 | tf_op jit(solution)/shard_map/ppermute | solution.py:476

commit v6 on v5

--- a/solution.py
+++ b/solution.py
@@ -143,7 +143,7 @@
 
 
 def convolve(received, matrix, rows, flip):
-    chunk = 256
+    chunk = 1024
     n_chunks = SEQ // chunk
 
     def kernel(r_ref, m_ref, w_ref, j_ref, b_ref, o_ref, c_ref, x_ref, y_ref):

time: 117 us -> 114 us (0.974)
  Pallas kernels: 37.4 us -> 35.1 us
    pallas_call x1, Pallas kernels: 7.42 us -> 5.11 us  [convolve(): call(kernel, in_specs=[vm, vm, vm, vm], out_specs=[vm, vm, vm], out_shape...]
where the time goes in v6:
time: 114 us
  Pallas kernels  35.1 us (31%)
  starting transfers between devices  30.3 us (27%)
  blocking collectives  28.1 us (25%)
  waiting for transfers between devices  15.5 us (14%)
  local copies, waits for them, and re-layouts  4.08 us (4%)
    all_to_all x1, blocking collectives, swap(): lax.all_to_all(pieces, axis, 0, 0, axis_index_groups=groups, tiled=True)  28.1 us
    ppermute x5, waiting for transfers between devices, hop(): return lax.ppermute(value, 'ctx', chip_hop(x_flip, z_step))  14.7 us
    ppermute x5, starting transfers between devices, hop(): return lax.ppermute(value, 'ctx', chip_hop(x_flip, z_step))  9.36 us
    pallas_call x1, Pallas kernels, project(): call(kernel, in_specs=[pl.BlockSpec(memory_space=pltpu.SMEM)] + [hbm] * 5...  7.68 us
    ppermute x5, starting transfers between devices, swap_cores(): return lax.ppermute(value, 'ctx', [(i, i ^ 1) for i in range(16)])  7.67 us
    all_to_all x2, starting transfers between devices, swap(): lax.all_to_all(pieces, axis, 0, 0, axis_index_groups=groups, tiled=True)  7.6 us
    pallas_call x1, Pallas kernels, input_partial(): call(kernel, in_specs=[vm, pl.BlockSpec(memory_space=pl.ANY)], out_specs=...  6.91 us
    pallas_call x1, Pallas kernels, weight_gradients(): call(kernel, in_specs=[pl.BlockSpec(memory_space=pltpu.SMEM), vm] + [hbm]...  6.34 us
  transfers between devices with their start and end apart: 15, of which 3 were waited for; matrix products, arithmetic and copies ran while one was open for 0% of the time, Pallas kernels for 18%

profile of v6, /device:TPU:1, one launch (start us, length us, event | category | flops | bytes accessed | tf_op | source)
XLA Modules:
  0.0 114.1 jit_solution(8979131087542497735)
XLA Ops:
  0.6 0.0 copy-start.5
  0.7 0.0 copy-start.6
  0.7 0.0 copy-start.7
  0.7 7.7 %project.1 = bf16[8,2,288,128]{3,2,1,0:T(8,128)(2,1)S(1)} custom-call(s32[1]{0:T(128)} %bitcast.y_ref, bf16[128,4096]{1,0:T(8,128)(2,1)} %t_hbm.1, bf16[128,4096]{1,0:T(8,128)(2,1)} %g_hbm.1, f32[128,512]{1,0:T(8,128)} %f_hbm.1, bf16[3,4096,512]{2,1,0:T(8,128)(2,1)} %bitcast.18, bf16[512,4096]{1,0:T(8,128)(2,1)} %ow_hbm.1), custom_call_target="tpu_custom_call" | custom-call | flops 2147483648 | bytes 19922944 | tf_op jit(solution)/shard_map/project/pallas_call | solution.py:111
  8.4 28.1 %all_to_all.15.r_ref = bf16[16,288,128]{2,1,0:T(8,128)(2,1)S(1)} all-to-all(bf16[16,288,128]{2,1,0:T(8,128)(2,1)S(1)} %bitcast.17), channel_id=1, replica_groups=mesh['ctx'=16,'mp'=8] {'ctx'}, dimensions={0} | all-to-all | bytes 2359296 | tf_op jit(solution)/shard_map/all_to_all | solution.py:480
  36.5 5.1 %convolve.1 = (bf16[128,2048]{1,0:T(8,128)(2,1)S(1)}, bf16[16,160,128]{2,1,0:T(8,128)(2,1)}, bf16[8,2,128,128]{3,2,1,0:T(8,128)(2,1)S(1)}) custom-call(bf16[16,288,128]{2,1,0:T(8,128)(2,1)S(1)} %all_to_all.15.r_ref, bf16[2048,2048]{1,0:T(8,128)(2,1)S(1)} %copy-done.5, f32[8,2048]{1,0:T(8,128)S(1)} %copy-done.7, bf16[256,256]{1,0:T(8,128)(2,1)S(1)} %copy-done.6), custom_call_target="tpu_custom_call" | custom-call | flops 3221225472 | bytes 12582912 | tf_op jit(solution)/shard_map/convolve/pallas_call | solution.py:208
  41.6 4.0 %all-to-all-start.1 = ((bf16[16,160,128]{2,1,0:T(8,128)(2,1)}), bf16[16,160,128]{2,1,0:T(8,128)(2,1)S(1)}, u32[]{:S(2)}, u32[]{:S(2)}) async-start(bf16[16,160,128]{2,1,0:T(8,128)(2,1)} %get-tuple-element.26), calls=%async_computation.1 | async-start | bytes 1310720 | tf_op jit(solution)/shard_map/all_to_all | solution.py:480
  45.6 2.9 %collective-permute-start.2 = (bf16[128,2048]{1,0:T(8,128)(2,1)S(1)}, bf16[128,2048]{1,0:T(8,128)(2,1)S(1)}, u32[]{:S(2)}, u32[]{:S(2)}) collective-permute-start(bf16[128,2048]{1,0:T(8,128)(2,1)S(1)} %get-tuple-element.25.c.refs_8_), channel_id=1, source_target_pairs={{0,64},{8,72},{16,80},{24,88},{32,96},{40,104},{48,112},{56,120},{... | collective-permute-start | bytes 1572872 | tf_op jit(solution)/shard_map/ppermute | solution.py:487
  48.6 2.4 %collective-permute-start.1 = (bf16[128,2048]{1,0:T(8,128)(2,1)S(1)}, bf16[128,2048]{1,0:T(8,128)(2,1)S(1)}, u32[]{:S(2)}, u32[]{:S(2)}) collective-permute-start(bf16[128,2048]{1,0:T(8,128)(2,1)S(1)} %get-tuple-element.25.c.refs_8_), channel_id=1, source_target_pairs={{0,48},{8,56},{16,0},{24,8},{32,16},{40,24},{48,32},{56,40},{64,11... | collective-permute-start | bytes 1572872 | tf_op jit(solution)/shard_map/ppermute | solution.py:487
  51.0 0.0 collective-permute-start
  51.0 2.9 %collective-permute-start.5 = (bf16[8,2,128,128]{3,2,1,0:T(8,128)(2,1)S(1)}, bf16[8,2,128,128]{3,2,1,0:T(8,128)(2,1)}, u32[]{:S(2)}, u32[]{:S(2)}) collective-permute-start(bf16[8,2,128,128]{3,2,1,0:T(8,128)(2,1)S(1)} %get-tuple-element.34.refs_0_), channel_id=1, source_target_pairs={{0,2},{1,3},{2,0},{3,1},{4,6},{5,7},{6,4},{7,5},{8,10},{9,11},{10,... | collective-permute-start | bytes 1572872 | tf_op jit(solution)/shard_map/ppermute | solution.py:495
  53.9 1.2 %collective-permute-start.6 = (bf16[8,2,128,128]{3,2,1,0:T(8,128)(2,1)S(1)}, bf16[8,2,128,128]{3,2,1,0:T(8,128)(2,1)}, u32[]{:S(2)}, u32[]{:S(2)}) collective-permute-start(bf16[8,2,128,128]{3,2,1,0:T(8,128)(2,1)S(1)} %get-tuple-element.34.refs_0_), channel_id=1, source_target_pairs={{0,8},{8,0},{16,24},{24,16},{32,40},{40,32},{48,56},{56,48},{64,72... | collective-permute-start | bytes 1572872 | tf_op jit(solution)/shard_map/ppermute | solution.py:476
  55.1 12.7 %collective-permute-done.2.d.refs_11_ = bf16[128,2048]{1,0:T(8,128)(2,1)S(1)} collective-permute-done((bf16[128,2048]{1,0:T(8,128)(2,1)S(1)}, bf16[128,2048]{1,0:T(8,128)(2,1)S(1)}, u32[]{:S(2)}, u32[]{:S(2)}) %collective-permute-start.2) | collective-permute-done | bytes 524320 | tf_op jit(solution)/shard_map/ppermute | solution.py:487
  67.8 1.3 %collective-permute-start.3 = (bf16[8,2,128,128]{3,2,1,0:T(8,128)(2,1)S(1)}, bf16[8,2,128,128]{3,2,1,0:T(8,128)(2,1)}, u32[]{:S(2)}, u32[]{:S(2)}) collective-permute-start(bf16[8,2,128,128]{3,2,1,0:T(8,128)(2,1)S(1)} %get-tuple-element.34.refs_0_), channel_id=1, source_target_pairs={{0,1},{1,2},{2,3},{3,0},{4,5},{5,6},{6,7},{7,4},{8,9},{9,10},{10,1... | collective-permute-start | bytes 1572872 | tf_op jit(solution)/shard_map/ppermute | solution.py:495
  69.1 0.0 collective-permute-done.1.b.refs_10_
  69.1 1.5 %collective-permute-start.4 = (bf16[8,2,128,128]{3,2,1,0:T(8,128)(2,1)S(1)}, bf16[8,2,128,128]{3,2,1,0:T(8,128)(2,1)}, u32[]{:S(2)}, u32[]{:S(2)}) collective-permute-start(bf16[8,2,128,128]{3,2,1,0:T(8,128)(2,1)S(1)} %get-tuple-element.34.refs_0_), channel_id=1, source_target_pairs={{0,3},{1,0},{2,1},{3,2},{4,7},{5,4},{6,5},{7,6},{8,11},{9,8},{10,9... | collective-permute-start | bytes 1572872 | tf_op jit(solution)/shard_map/ppermute | solution.py:495
  70.6 0.0 collective-permute-done.a.refs_9_
  70.6 0.0 all-to-all-done.1.r_ref
  70.6 1.5 %pair.1 = (bf16[256,2048]{1,0:T(8,128)(2,1)}, bf16[256,2048]{1,0:T(8,128)(2,1)}) custom-call(bf16[128,2048]{1,0:T(8,128)(2,1)S(1)} %collective-permute-done.a.refs_9_, bf16[128,2048]{1,0:T(8,128)(2,1)S(1)} %collective-permute-done.1.b.refs_10_, bf16[128,2048]{1,0:T(8,128)(2,1)S(1)} %get-tuple-element.25.c.refs_8_, ...), custom_call_target="tpu_custom_call" | custom-call | tf_op jit(solution)/shard_map/pair/pallas_call | solution.py:306
  72.2 2.8 %collective-permute-start.10 = (bf16[256,2048]{1,0:T(8,128)(2,1)}, bf16[256,2048]{1,0:T(8,128)(2,1)}, u32[]{:S(2)}, u32[]{:S(2)}) collective-permute-start(bf16[256,2048]{1,0:T(8,128)(2,1)} %get-tuple-element.38), channel_id=1, source_target_pairs={{0,32},{8,40},{16,48},{24,56},{32,0},{40,8},{48,16},{56,24},{64,96... | collective-permute-start | bytes 3145736 | tf_op jit(solution)/shard_map/ppermute | solution.py:487
  75.0 0.0 collective-permute-done.5.refs_3_
  75.0 1.2 %collective-permute-start.11 = (bf16[256,2048]{1,0:T(8,128)(2,1)}, bf16[256,2048]{1,0:T(8,128)(2,1)}, u32[]{:S(2)}, u32[]{:S(2)}) collective-permute-start(bf16[256,2048]{1,0:T(8,128)(2,1)} %get-tuple-element.31), channel_id=1, source_target_pairs={{0,64},{8,72},{16,80},{24,88},{32,96},{40,104},{48,112},{56,120},{... | collective-permute-start | bytes 3145736 | tf_op jit(solution)/shard_map/ppermute | solution.py:487
  76.2 6.9 %input_partial.1 = (bf16[8,128,512]{2,1,0:T(8,128)(2,1)S(1)}, f32[128,512]{1,0:T(8,128)}) custom-call(bf16[16,160,128]{2,1,0:T(8,128)(2,1)S(1)} %all-to-all-done.1.r_ref, bf16[3,4096,512]{2,1,0:T(8,128)(2,1)} %bitcast.19), custom_call_target="tpu_custom_call" | custom-call | flops 1610612736 | bytes 14680064 | tf_op jit(solution)/shard_map/input_partial/pallas_call | solution.py:257
  83.1 1.0 copy-done.4
  84.1 0.0 collective-permute-done.3.refs_1_
  84.1 1.3 %collective-permute-start.7 = (bf16[8,2,128,128]{3,2,1,0:T(8,128)(2,1)}, bf16[8,2,128,128]{3,2,1,0:T(8,128)(2,1)S(1)}, u32[]{:S(2)}, u32[]{:S(2)}) collective-permute-start(bf16[8,2,128,128]{3,2,1,0:T(8,128)(2,1)} %collective-permute-done.3.refs_1_), channel_id=1, source_target_pairs={{0,8},{8,0},{16,24},{24,16},{32,40},{40,32},{48,56},{56,48},{64,72... | collective-permute-start | bytes 1572872 | tf_op jit(solution)/shard_map/ppermute | solution.py:476
  85.4 0.0 collective-permute-done.4.refs_2_
  85.4 0.1 collective-permute-start.8
  85.5 0.0 collective-permute-done.6.refs_4_
  85.5 0.4 collective-permute-start.9
  85.9 3.6 %all-to-all-start.2 = ((bf16[8,128,512]{2,1,0:T(8,128)(2,1)}), bf16[8,128,512]{2,1,0:T(8,128)(2,1)S(1)}, u32[]{:S(2)}, u32[]{:S(2)}) async-start(bf16[8,128,512]{2,1,0:T(8,128)(2,1)} %copy-done.4), calls=%async_computation.2 | async-start | bytes 2097152 | tf_op jit(solution)/shard_map/all_to_all | solution.py:480
  89.5 0.1 stack.55.place_ref
  89.6 0.0 collective-permute-done.7.refs_5_
  89.6 0.0 copy-start.8
  89.6 0.0 collective-permute-done.8.refs_6_
  89.6 0.0 collective-permute-done.9.refs_7_
  89.7 0.8 copy-done.8
  90.4 0.2 copy-done.9
  90.7 5.2 %first_products.1 = (f32[4,128,512]{2,1,0:T(8,128)S(1)}, bf16[2,2,8,128,512]{4,3,2,1,0:T(8,128)(2,1)S(1)}) custom-call(s32[13]{0:T(128)S(1)} %stack.55.place_ref, bf16[8,2,128,128]{3,2,1,0:T(8,128)(2,1)S(1)} %get-tuple-element.34.refs_0_, bf16[8,2,128,128]{3,2,1,0:T(8,128)(2,1)} %collective-permute-done.3.refs_1_, ...), custom_call_target="tpu_custom_call" | custom-call | tf_op jit(solution)/shard_map/first_products/pallas_call | solution.py:365
  95.9 2.0 %copy-done = bf16[2,2,8,128,512]{4,3,2,1,0:T(8,128)(2,1)} copy-done((bf16[2,2,8,128,512]{4,3,2,1,0:T(8,128)(2,1)}, bf16[2,2,8,128,512]{4,3,2,1,0:T(8,128)(2,1)S(1)}, u32[]{:S(2)}) %copy-start) | copy-done | bytes 4194328
  97.8 0.0 collective-permute-done.10.refs_0_.refs_3_
  97.8 2.0 %collective-permute-done.11.refs_1_.refs_2_ = bf16[256,2048]{1,0:T(8,128)(2,1)} collective-permute-done((bf16[256,2048]{1,0:T(8,128)(2,1)}, bf16[256,2048]{1,0:T(8,128)(2,1)}, u32[]{:S(2)}, u32[]{:S(2)}) %collective-permute-start.11) | collective-permute-done | bytes 1048608 | tf_op jit(solution)/shard_map/ppermute | solution.py:487
  99.9 6.3 %weight_gradients.1 = (f32[3,256,512]{2,1,0:T(8,128)}, f32[512,256]{1,0:T(8,128)}, bf16[1024,256]{1,0:T(8,128)(2,1)S(1)}) custom-call(s32[13]{0:T(128)S(1)} %stack.55.place_ref, f32[4,128,512]{2,1,0:T(8,128)S(1)} %get-tuple-element.37.p_ref, bf16[256,2048]{1,0:T(8,128)(2,1)} %collective-permute-done.10.refs_0_.refs_3_, ...), custom_call_target="tpu_custom_call" | custom-call | tf_op jit(solution)/shard_map/weight_gradients/pallas_call | solution.py:421
  106.2 4.7 %collective-permute-start.12 = (bf16[1024,256]{1,0:T(8,128)(2,1)S(1)}, bf16[1024,256]{1,0:T(8,128)(2,1)S(1)}, u32[]{:S(2)}, u32[]{:S(2)}) collective-permute-start(bf16[1024,256]{1,0:T(8,128)(2,1)S(1)} %get-tuple-element.40), channel_id=1, source_target_pairs={{0,8},{8,0},{16,24},{24,16},{32,40},{40,32},{48,56},{56,48},{64,72... | collective-permute-start | bytes 1572872 | tf_op jit(solution)/shard_map/ppermute | solution.py:476
  110.9 0.0 all-to-all-done.2.p_ref
  110.9 0.8 sum_partials.1
  111.7 0.7 collective-permute-done.12.s_ref
  112.4 1.6 %fill_halves.1 = (f32[3,256,512]{2,1,0:T(8,128)}, f32[512,256]{1,0:T(8,128)}) custom-call(s32[13]{0:T(128)S(1)} %stack.55.place_ref, bf16[1024,256]{1,0:T(8,128)(2,1)S(1)} %collective-permute-done.12.s_ref, f32[3,256,512]{2,1,0:T(8,128)} %get-tuple-element.41.in_old, f32[512,256]{1,0:T(8,128)} %get-tuple-element.42.out_old), custom_call_target="tpu_custom_call", output_to_operand_aliasing={{0}: (2, {}), {1}: (3, {})} | custom-call | tf_op jit(solution)/shard_map/fill_halves/pallas_call | solution.py:455
  (12 shorter events, 0.0 us)
Async XLA Ops:
  0.6 35.8 %copy-start.5 = (bf16[2048,2048]{1,0:T(8,128)(2,1)S(1)}, bf16[2048,2048]{1,0:T(8,128)(2,1)}, u32[]{:S(2)}) copy-start(bf16[2048,2048]{1,0:T(8,128)(2,1)} %constant.31.clone.m_ref) | copy-start | bytes 25165828
  0.7 35.8 %copy-start.6 = (bf16[256,256]{1,0:T(8,128)(2,1)S(1)}, bf16[256,256]{1,0:T(8,128)(2,1)}, u32[]{:S(2)}) copy-start(bf16[256,256]{1,0:T(8,128)(2,1)} %constant.30.clone.j_ref) | copy-start | bytes 393220
  0.7 35.8 %copy-start.7 = (f32[8,2048]{1,0:T(8,128)S(1)}, f32[8,2048]{1,0:T(8,128)}, u32[]{:S(2)}) copy-start(f32[8,2048]{1,0:T(8,128)} %constant.32.clone.w_ref) | copy-start | bytes 196612
  41.6 29.0 %all-to-all-start.1 = ((bf16[16,160,128]{2,1,0:T(8,128)(2,1)}), bf16[16,160,128]{2,1,0:T(8,128)(2,1)S(1)}, u32[]{:S(2)}, u32[]{:S(2)}) async-start(bf16[16,160,128]{2,1,0:T(8,128)(2,1)} %get-tuple-element.26), calls=%async_computation.1 | async-start | bytes 1310720 | tf_op jit(solution)/shard_map/all_to_all | solution.py:480
  45.6 22.2 %collective-permute-start.2 = (bf16[128,2048]{1,0:T(8,128)(2,1)S(1)}, bf16[128,2048]{1,0:T(8,128)(2,1)S(1)}, u32[]{:S(2)}, u32[]{:S(2)}) collective-permute-start(bf16[128,2048]{1,0:T(8,128)(2,1)S(1)} %get-tuple-element.25.c.refs_8_), channel_id=1, source_target_pairs={{0,64},{8,72},{16,80},{24,88},{32,96},{40,104},{48,112},{56,120},{... | collective-permute-start | bytes 1572872 | tf_op jit(solution)/shard_map/ppermute | solution.py:487
  48.6 20.5 %collective-permute-start.1 = (bf16[128,2048]{1,0:T(8,128)(2,1)S(1)}, bf16[128,2048]{1,0:T(8,128)(2,1)S(1)}, u32[]{:S(2)}, u32[]{:S(2)}) collective-permute-start(bf16[128,2048]{1,0:T(8,128)(2,1)S(1)} %get-tuple-element.25.c.refs_8_), channel_id=1, source_target_pairs={{0,48},{8,56},{16,0},{24,8},{32,16},{40,24},{48,32},{56,40},{64,11... | collective-permute-start | bytes 1572872 | tf_op jit(solution)/shard_map/ppermute | solution.py:487
  51.0 19.6 %collective-permute-start = (bf16[128,2048]{1,0:T(8,128)(2,1)S(1)}, bf16[128,2048]{1,0:T(8,128)(2,1)S(1)}, u32[]{:S(2)}, u32[]{:S(2)}) collective-permute-start(bf16[128,2048]{1,0:T(8,128)(2,1)S(1)} %get-tuple-element.25.c.refs_8_), channel_id=1, source_target_pairs={{0,16},{8,24},{16,32},{24,40},{32,48},{40,56},{48,0},{56,8},{64,80... | collective-permute-start | bytes 1572872 | tf_op jit(solution)/shard_map/ppermute | solution.py:487
  51.0 24.0 %collective-permute-start.5 = (bf16[8,2,128,128]{3,2,1,0:T(8,128)(2,1)S(1)}, bf16[8,2,128,128]{3,2,1,0:T(8,128)(2,1)}, u32[]{:S(2)}, u32[]{:S(2)}) collective-permute-start(bf16[8,2,128,128]{3,2,1,0:T(8,128)(2,1)S(1)} %get-tuple-element.34.refs_0_), channel_id=1, source_target_pairs={{0,2},{1,3},{2,0},{3,1},{4,6},{5,7},{6,4},{7,5},{8,10},{9,11},{10,... | collective-permute-start | bytes 1572872 | tf_op jit(solution)/shard_map/ppermute | solution.py:495
  53.9 31.6 %collective-permute-start.6 = (bf16[8,2,128,128]{3,2,1,0:T(8,128)(2,1)S(1)}, bf16[8,2,128,128]{3,2,1,0:T(8,128)(2,1)}, u32[]{:S(2)}, u32[]{:S(2)}) collective-permute-start(bf16[8,2,128,128]{3,2,1,0:T(8,128)(2,1)S(1)} %get-tuple-element.34.refs_0_), channel_id=1, source_target_pairs={{0,8},{8,0},{16,24},{24,16},{32,40},{40,32},{48,56},{56,48},{64,72... | collective-permute-start | bytes 1572872 | tf_op jit(solution)/shard_map/ppermute | solution.py:476
  67.8 15.3 %copy-start.1 = (bf16[128,2048]{1,0:T(8,128)(2,1)}, bf16[128,2048]{1,0:T(8,128)(2,1)S(1)}, u32[]{:S(2)}) copy-start(bf16[128,2048]{1,0:T(8,128)(2,1)S(1)} %collective-permute-done.2.d.refs_11_) | copy-start | bytes 1572868
  67.8 16.3 %collective-permute-start.3 = (bf16[8,2,128,128]{3,2,1,0:T(8,128)(2,1)S(1)}, bf16[8,2,128,128]{3,2,1,0:T(8,128)(2,1)}, u32[]{:S(2)}, u32[]{:S(2)}) collective-permute-start(bf16[8,2,128,128]{3,2,1,0:T(8,128)(2,1)S(1)} %get-tuple-element.34.refs_0_), channel_id=1, source_target_pairs={{0,1},{1,2},{2,3},{3,0},{4,5},{5,6},{6,7},{7,4},{8,9},{9,10},{10,1... | collective-permute-start | bytes 1572872 | tf_op jit(solution)/shard_map/ppermute | solution.py:495
  69.1 14.0 %copy-start.2 = (bf16[128,2048]{1,0:T(8,128)(2,1)}, bf16[128,2048]{1,0:T(8,128)(2,1)S(1)}, u32[]{:S(2)}) copy-start(bf16[128,2048]{1,0:T(8,128)(2,1)S(1)} %collective-permute-done.1.b.refs_10_) | copy-start | bytes 1572868
  69.1 16.3 %collective-permute-start.4 = (bf16[8,2,128,128]{3,2,1,0:T(8,128)(2,1)S(1)}, bf16[8,2,128,128]{3,2,1,0:T(8,128)(2,1)}, u32[]{:S(2)}, u32[]{:S(2)}) collective-permute-start(bf16[8,2,128,128]{3,2,1,0:T(8,128)(2,1)S(1)} %get-tuple-element.34.refs_0_), channel_id=1, source_target_pairs={{0,3},{1,0},{2,1},{3,2},{4,7},{5,4},{6,5},{7,6},{8,11},{9,8},{10,9... | collective-permute-start | bytes 1572872 | tf_op jit(solution)/shard_map/ppermute | solution.py:495
  70.6 12.5 %copy-start.3 = (bf16[128,2048]{1,0:T(8,128)(2,1)}, bf16[128,2048]{1,0:T(8,128)(2,1)S(1)}, u32[]{:S(2)}) copy-start(bf16[128,2048]{1,0:T(8,128)(2,1)S(1)} %collective-permute-done.a.refs_9_) | copy-start | bytes 1572868
  72.2 25.6 %collective-permute-start.10 = (bf16[256,2048]{1,0:T(8,128)(2,1)}, bf16[256,2048]{1,0:T(8,128)(2,1)}, u32[]{:S(2)}, u32[]{:S(2)}) collective-permute-start(bf16[256,2048]{1,0:T(8,128)(2,1)} %get-tuple-element.38), channel_id=1, source_target_pairs={{0,32},{8,40},{16,48},{24,56},{32,0},{40,8},{48,16},{56,24},{64,96... | collective-permute-start | bytes 3145736 | tf_op jit(solution)/shard_map/ppermute | solution.py:487
  75.0 24.9 %collective-permute-start.11 = (bf16[256,2048]{1,0:T(8,128)(2,1)}, bf16[256,2048]{1,0:T(8,128)(2,1)}, u32[]{:S(2)}, u32[]{:S(2)}) collective-permute-start(bf16[256,2048]{1,0:T(8,128)(2,1)} %get-tuple-element.31), channel_id=1, source_target_pairs={{0,64},{8,72},{16,80},{24,88},{32,96},{40,104},{48,112},{56,120},{... | collective-permute-start | bytes 3145736 | tf_op jit(solution)/shard_map/ppermute | solution.py:487
  83.1 1.0 copy-start.4
  84.1 5.5 %collective-permute-start.7 = (bf16[8,2,128,128]{3,2,1,0:T(8,128)(2,1)}, bf16[8,2,128,128]{3,2,1,0:T(8,128)(2,1)S(1)}, u32[]{:S(2)}, u32[]{:S(2)}) collective-permute-start(bf16[8,2,128,128]{3,2,1,0:T(8,128)(2,1)} %collective-permute-done.3.refs_1_), channel_id=1, source_target_pairs={{0,8},{8,0},{16,24},{24,16},{32,40},{40,32},{48,56},{56,48},{64,72... | collective-permute-start | bytes 1572872 | tf_op jit(solution)/shard_map/ppermute | solution.py:476
  85.4 4.2 %collective-permute-start.8 = (bf16[8,2,128,128]{3,2,1,0:T(8,128)(2,1)}, bf16[8,2,128,128]{3,2,1,0:T(8,128)(2,1)S(1)}, u32[]{:S(2)}, u32[]{:S(2)}) collective-permute-start(bf16[8,2,128,128]{3,2,1,0:T(8,128)(2,1)} %collective-permute-done.4.refs_2_), channel_id=1, source_target_pairs={{0,8},{8,0},{16,24},{24,16},{32,40},{40,32},{48,56},{56,48},{64,72... | collective-permute-start | bytes 1572872 | tf_op jit(solution)/shard_map/ppermute | solution.py:476
  85.5 4.2 %collective-permute-start.9 = (bf16[8,2,128,128]{3,2,1,0:T(8,128)(2,1)}, bf16[8,2,128,128]{3,2,1,0:T(8,128)(2,1)}, u32[]{:S(2)}, u32[]{:S(2)}) collective-permute-start(bf16[8,2,128,128]{3,2,1,0:T(8,128)(2,1)} %collective-permute-done.5.refs_3_), channel_id=1, source_target_pairs={{0,8},{8,0},{16,24},{24,16},{32,40},{40,32},{48,56},{56,48},{64,72... | collective-permute-start | bytes 1572872 | tf_op jit(solution)/shard_map/ppermute | solution.py:476
  85.9 25.0 %all-to-all-start.2 = ((bf16[8,128,512]{2,1,0:T(8,128)(2,1)}), bf16[8,128,512]{2,1,0:T(8,128)(2,1)S(1)}, u32[]{:S(2)}, u32[]{:S(2)}) async-start(bf16[8,128,512]{2,1,0:T(8,128)(2,1)} %copy-done.4), calls=%async_computation.2 | async-start | bytes 2097152 | tf_op jit(solution)/shard_map/all_to_all | solution.py:480
  89.6 0.8 copy-start.8
  89.6 1.0 copy-start.9
  95.9 2.0 %copy-start = (bf16[2,2,8,128,512]{4,3,2,1,0:T(8,128)(2,1)}, bf16[2,2,8,128,512]{4,3,2,1,0:T(8,128)(2,1)S(1)}, u32[]{:S(2)}) copy-start(bf16[2,2,8,128,512]{4,3,2,1,0:T(8,128)(2,1)S(1)} %get-tuple-element.39.refs_4_) | copy-start | bytes 12582916
  106.2 6.2 %collective-permute-start.12 = (bf16[1024,256]{1,0:T(8,128)(2,1)S(1)}, bf16[1024,256]{1,0:T(8,128)(2,1)S(1)}, u32[]{:S(2)}, u32[]{:S(2)}) collective-permute-start(bf16[1024,256]{1,0:T(8,128)(2,1)S(1)} %get-tuple-element.40), channel_id=1, source_target_pairs={{0,8},{8,0},{16,24},{24,16},{32,40},{40,32},{48,56},{56,48},{64,72... | collective-permute-start | bytes 1572872 | tf_op jit(solution)/shard_map/ppermute | solution.py:476
